TPU v7x, 32 devices: a whole 2x2x4 slice. The times are simulated.
32 devices in a mesh: items: 2 (over x), rows: 16 (over z, y, core).
Axes of the slice: x: 2, y: 2, z: 4, core: 2. Of those that a mesh axis runs over, the one named last changes fastest.
Arguments:
- latents: float32 [2, 2048, 1536], P('items', 'rows'), may hold values from -6 to 6
- conditions: bfloat16 [2, 2, 1024], P('items'), may hold values from -6 to 6
- captions: bfloat16 [2, 2, 256, 4096], P('items'), may hold values from -6 to 6
- row_counts: int32 [2, 16, 2], P('items', 'rows'), may hold values from 16 to 112, as said below
- text_lengths: int32 [2, 2], P('items'), may hold values from 64 to 256, as said below
- qkv_weight: bfloat16 [1536, 4608], P(('items', 'rows')), may hold values from -0.15625 to 0.15625
- text_weight: bfloat16 [4096, 3072], P(('items', 'rows')), may hold values from -0.09375 to 0.09375
- out_weight: bfloat16 [1536, 1536], P(('items', 'rows')), may hold values from -0.15625 to 0.15625
- gate_up_weight: bfloat16 [1536, 8192], P(('items', 'rows')), may hold values from -0.15625 to 0.15625
- down_weight: bfloat16 [4096, 1536], P(('items', 'rows')), may hold values from -0.09375 to 0.09375
- ada_weight: bfloat16 [1024, 6144], P(('items', 'rows')), may hold values from -0.1875 to 0.1875
- ada_bias: bfloat16 [6144], P(('items', 'rows')), may hold values from -3 to 3
- norm_gains: bfloat16 [7, 1536], P(None, ('items', 'rows')), may hold values from 0.5 to 1.5
- head_gates: bfloat16 [24], replicated, may hold values from -3 to 3
- cotangent: float32 [2, 2048, 1536], P('items', 'rows'), may hold values from -6 to 6
Outputs:
- block_out: float32 [2, 2048, 1536], P('items', 'rows')
- latent_grad: float32 [2, 2048, 1536], P('items', 'rows')
- qkv_grad: float32 [1536, 4608], P(('items', 'rows'))
- text_grad: float32 [4096, 3072], P(('items', 'rows'))
- out_grad: float32 [1536, 1536], P(('items', 'rows'))
- gate_up_grad: float32 [1536, 8192], P(('items', 'rows'))
- down_grad: float32 [4096, 1536], P(('items', 'rows'))
- ada_grad: float32 [1024, 6144], P(('items', 'rows'))
- bias_grad: float32 [6144], P(('items', 'rows'))
- gains_grad: float32 [7, 1536], P(None, ('items', 'rows'))
- head_gates_grad: float32 [24], replicated
Inputs may be any that keep to these rules, and one draw needn't show every extreme that they name: `row_counts`: for each group and each device of rows, how many of that device's 128 rows belong to the group's clip (first) and to its image (second); the clip's rows come first; the two sum to 128. `text_lengths`: live caption tokens are the first ones of each caption.
All inputs are finite; a program needn't handle non-finite values.
Results may differ from a plain program's by a relative error of at most 0.013.
Values may be sent and summed in bfloat16 or wider, within the bound.
A program may use at most 768 MiB of HBM per device.

v0:
```python
import jax
import jax.numpy as jnp
from jax import lax
from jax.sharding import PartitionSpec as P

D = 1536
HEADS = 24
HEAD = 64
FF = 4096
TEXT_DIM = 4096
TEXT = 256
FRAMES = 2
TOK_DEV = 128


epsilon = 1e-05
theta_base = 10000.0
score_scale = 0.125
masked_value = -1e30
highest = lax.Precision.HIGHEST


def normed(value, gain_row):
    return value * lax.rsqrt(jnp.mean(value * value, axis=-1, keepdims=True) + epsilon) * gain_row


def rotate(value, position, head_size):
    width = value.shape[-1]
    pair_index = jnp.arange(width, dtype=jnp.int32) % head_size // 2
    frequency = theta_base ** (-2.0 * pair_index.astype(jnp.float32) / head_size)
    angle = position[:, None] * frequency[None, :]
    paired = value.reshape(value.shape[0], width // 2, 2)
    turned = jnp.stack([-paired[:, :, 1], paired[:, :, 0]], axis=-1).reshape(value.shape)
    return value * jnp.cos(angle) + turned * jnp.sin(angle)


def shards(
    latents,
    conditions,
    captions,
    row_counts,
    text_lengths,
    qkv_weight,
    text_weight,
    out_weight,
    gate_up_weight,
    down_weight,
    ada_weight,
    ada_bias,
    norm_gains,
    head_gates,
    cotangent,
):
    devices_rows = lax.axis_size("rows")
    own_index = lax.axis_index("rows")
    counts_all = lax.all_gather(row_counts[0], "rows", axis=0, tiled=True)
    shard_line = jnp.arange(devices_rows, dtype=jnp.int32)
    own_counts = jnp.sum(jnp.where((shard_line == own_index)[:, None], counts_all, 0), axis=0)
    before_own = jnp.sum(jnp.where((shard_line < own_index)[:, None], counts_all, 0), axis=0)
    own_bounds = jnp.cumsum(own_counts)
    all_bounds = jnp.cumsum(counts_all, axis=1)
    local_line = jnp.arange(TOK_DEV, dtype=jnp.int32)
    frame_rows = jnp.sum((local_line[:, None] >= own_bounds[None, :-1]).astype(jnp.int32), axis=1)
    frame_onehot = frame_rows[:, None] == jnp.arange(FRAMES, dtype=jnp.int32)[None, :]
    offsets = jnp.sum(
        jnp.where(frame_onehot, (before_own - own_bounds + own_counts)[None, :], 0), axis=1
    )
    positions = (offsets + local_line).astype(jnp.float32)
    onehot_float = frame_onehot.astype(jnp.float32)
    full_qkv, full_text, full_out, full_ada, full_gains, full_bias = (
        lax.all_gather(qkv_weight, ("items", "rows"), axis=0, tiled=True),
        lax.all_gather(text_weight, ("items", "rows"), axis=0, tiled=True),
        lax.all_gather(out_weight, ("items", "rows"), axis=0, tiled=True),
        lax.all_gather(ada_weight, ("items", "rows"), axis=0, tiled=True),
        lax.all_gather(norm_gains, ("items", "rows"), axis=1, tiled=True),
        lax.all_gather(ada_bias, ("items", "rows"), axis=0, tiled=True),
    )
    gains_float = full_gains.astype(jnp.float32)
    gain_one, gain_two, gain_three, gain_four = (
        gains_float[0],
        gains_float[1],
        gains_float[2],
        gains_float[3],
    )
    gain_query, gain_key, gain_caption = (gains_float[4], gains_float[5], gains_float[6])
    silu_cond = jax.nn.silu(conditions[0].astype(jnp.float32)).astype(jnp.bfloat16)
    modulation = jnp.dot(
        silu_cond, full_ada, preferred_element_type=jnp.float32
    ) + full_bias.astype(jnp.float32)
    mod_rows = jnp.dot(onehot_float, modulation, precision=highest)
    scale_attn, gate_attn = (mod_rows[:, :D], mod_rows[:, D : 2 * D])
    scale_ffn, gate_ffn = (mod_rows[:, 2 * D : 3 * D], mod_rows[:, 3 * D :])
    caption_rows = captions[0].reshape(FRAMES * TEXT, TEXT_DIM)
    text_share = FRAMES * TEXT // devices_rows
    own_captions = lax.dynamic_slice_in_dim(caption_rows, own_index * text_share, text_share, 0)
    text_full = jnp.dot(caption_rows, full_text, preferred_element_type=jnp.float32)
    own_text = lax.dynamic_slice_in_dim(text_full, own_index * text_share, text_share, 0)
    text_keys = normed(text_full[:, :D], gain_caption).astype(jnp.bfloat16)
    text_values = text_full[:, D:].astype(jnp.bfloat16)
    text_key_float = text_keys.reshape(FRAMES * TEXT, HEADS, HEAD).astype(jnp.float32)
    text_value_float = text_values.reshape(FRAMES * TEXT, HEADS, HEAD).astype(jnp.float32)
    inputs = latents[0]

    def attn_head(input_rows, scale_rows, gain_row):
        return normed(input_rows, gain_row) * (1.0 + scale_rows)

    attn_in_float, attn_head_back = jax.vjp(attn_head, inputs, scale_attn, gain_one)
    attn_in = attn_in_float.astype(jnp.bfloat16)
    qkv_raw = jnp.dot(attn_in, full_qkv, preferred_element_type=jnp.float32)

    def project_heads(qkv_rows, gain_q, gain_k):
        query_rows = rotate(normed(qkv_rows[:, :D], gain_q), positions, HEAD)
        key_rows = rotate(normed(qkv_rows[:, D : 2 * D], gain_k), positions, HEAD)
        return (query_rows, key_rows, qkv_rows[:, 2 * D :])

    (query_rows, key_rows, value_rows), heads_back = jax.vjp(
        project_heads, qkv_raw, gain_query, gain_key
    )
    query_b = query_rows.astype(jnp.bfloat16)
    key_b = key_rows.astype(jnp.bfloat16)
    value_b = value_rows.astype(jnp.bfloat16)
    query_heads = query_b.reshape(TOK_DEV, HEADS, HEAD)
    query_float = query_heads.astype(jnp.float32)

    def key_frames(amount):
        global_line = jnp.arange(amount, dtype=jnp.int32)
        shard_of = global_line // TOK_DEV
        within = global_line % TOK_DEV
        picked = jnp.where(
            (shard_of[:, None] == shard_line[None, :])[:, :, None], all_bounds[None, :, :], 0
        )
        bounds_of = jnp.sum(picked, axis=1)
        return jnp.sum((within[:, None] >= bounds_of[:, :-1]).astype(jnp.int32), axis=1)

    run_max = jnp.full((HEADS, TOK_DEV), masked_value, jnp.float32)
    run_acc = jnp.zeros((TOK_DEV, HEADS, HEAD), jnp.float32)
    piece_keys = lax.all_gather(key_b, "rows", axis=0, tiled=True)
    piece_values = lax.all_gather(value_b, "rows", axis=0, tiled=True)
    amount = piece_keys.shape[0]
    key_heads = piece_keys.reshape(amount, HEADS, HEAD)
    value_heads = piece_values.reshape(amount, HEADS, HEAD).astype(jnp.float32)
    allowed = frame_rows[:, None] == key_frames(amount)[None, :]
    scores = (
        jnp.einsum("qhe,khe->hqk", query_heads, key_heads, preferred_element_type=jnp.float32)
        * score_scale
    )
    scores = jnp.where(allowed[None], scores, masked_value)
    new_max = jnp.maximum(run_max, jnp.max(scores, axis=-1))
    shrink = jnp.exp(run_max - new_max)
    weights = jnp.exp(scores - new_max[:, :, None])
    new_sum = jnp.sum(weights, axis=-1)
    added = jnp.einsum("hqk,khe->qhe", weights, value_heads, precision=highest)
    run_max, run_sum, run_acc = (new_max, new_sum, run_acc * shrink.T[:, :, None] + added)
    log_total = run_max + jnp.log(run_sum)
    self_out = run_acc / run_sum.T[:, :, None]
    text_line = jnp.arange(FRAMES * TEXT, dtype=jnp.int32)
    text_live = text_line % TEXT < jnp.repeat(text_lengths[0], TEXT)
    text_allowed = (frame_rows[:, None] == (text_line // TEXT)[None, :]) & text_live[None, :]
    cross_scores = (
        jnp.einsum("qhe,khe->hqk", query_float, text_key_float, precision=highest) * score_scale
    )
    cross_probs = jax.nn.softmax(jnp.where(text_allowed[None], cross_scores, masked_value), axis=-1)
    cross_out = jnp.einsum("hqk,khe->qhe", cross_probs, text_value_float, precision=highest)
    gate_heads = jnp.tanh(head_gates.astype(jnp.float32))
    mixed_heads = self_out + gate_heads[None, :, None] * cross_out
    mixed_b = mixed_heads.reshape(TOK_DEV, D).astype(jnp.bfloat16)
    attn_proj = jnp.dot(mixed_b, full_out, preferred_element_type=jnp.float32)

    def attn_tail(input_rows, proj_rows, gate_rows, gain_row):
        return input_rows + jnp.tanh(gate_rows) * normed(proj_rows, gain_row)

    state_rows, attn_tail_back = jax.vjp(attn_tail, inputs, attn_proj, gate_attn, gain_two)
    full_gate_up, full_down = (
        lax.all_gather(gate_up_weight, ("items", "rows"), axis=0, tiled=True),
        lax.all_gather(down_weight, ("items", "rows"), axis=0, tiled=True),
    )
    ffn_in_float, ffn_head_back = jax.vjp(attn_head, state_rows, scale_ffn, gain_three)
    ffn_in = ffn_in_float.astype(jnp.bfloat16)
    gate_up = jnp.dot(ffn_in, full_gate_up, preferred_element_type=jnp.float32)

    def swiglu(gate_up_rows):
        return jax.nn.silu(gate_up_rows[:, :FF]) * gate_up_rows[:, FF:]

    activated, swiglu_back = jax.vjp(swiglu, gate_up)
    activated_b = activated.astype(jnp.bfloat16)
    down_out = jnp.dot(activated_b, full_down, preferred_element_type=jnp.float32)
    result_rows, ffn_tail_back = jax.vjp(attn_tail, state_rows, down_out, gate_ffn, gain_four)
    back_gate_up, back_down = (
        lax.all_gather(gate_up_weight, ("items", "rows"), axis=0, tiled=True),
        lax.all_gather(down_weight, ("items", "rows"), axis=0, tiled=True),
    )
    d_state_tail, d_down, d_gate_ffn, d_gain_four = ffn_tail_back(cotangent[0])
    d_down_b = d_down.astype(jnp.bfloat16)
    grad_down = jnp.einsum("tf,td->fd", activated_b, d_down_b, preferred_element_type=jnp.float32)
    d_activated = jnp.einsum("td,fd->tf", d_down_b, back_down, preferred_element_type=jnp.float32)
    (d_gate_up,) = swiglu_back(d_activated)
    d_gate_up_b = d_gate_up.astype(jnp.bfloat16)
    grad_gate_up = jnp.einsum("td,tf->df", ffn_in, d_gate_up_b, preferred_element_type=jnp.float32)
    d_ffn_in = jnp.einsum(
        "tf,df->td", d_gate_up_b, back_gate_up, preferred_element_type=jnp.float32
    )
    d_state_head, d_scale_ffn, d_gain_three = ffn_head_back(d_ffn_in)
    d_state = d_state_tail + d_state_head
    ffn_grads = (
        lax.psum_scatter(grad_gate_up, ("items", "rows"), scatter_dimension=0, tiled=True),
        lax.psum_scatter(grad_down, ("items", "rows"), scatter_dimension=0, tiled=True),
    )
    back_qkv, back_out = (
        lax.all_gather(qkv_weight, ("items", "rows"), axis=0, tiled=True),
        lax.all_gather(out_weight, ("items", "rows"), axis=0, tiled=True),
    )
    d_inputs_tail, d_proj, d_gate_attn, d_gain_two = attn_tail_back(d_state)
    d_proj_b = d_proj.astype(jnp.bfloat16)
    grad_out_weight = jnp.einsum("td,te->de", mixed_b, d_proj_b, preferred_element_type=jnp.float32)
    d_mixed_b = jnp.einsum(
        "te,de->td", d_proj_b, back_out, preferred_element_type=jnp.float32
    ).astype(jnp.bfloat16)
    d_self = d_mixed_b.astype(jnp.float32).reshape(TOK_DEV, HEADS, HEAD)
    d_cross = d_self * gate_heads[None, :, None]
    grad_head_gates = jnp.sum(d_self * cross_out, axis=(0, 2)) * (1.0 - gate_heads * gate_heads)
    d_cross_probs = jnp.einsum("qhe,khe->hqk", d_cross, text_value_float, precision=highest)
    d_cross_scores = (
        cross_probs
        * (d_cross_probs - jnp.sum(cross_probs * d_cross_probs, axis=-1, keepdims=True))
        * score_scale
    )
    d_query_cross = jnp.einsum("hqk,khe->qhe", d_cross_scores, text_key_float, precision=highest)
    d_text_keys = jnp.einsum(
        "hqk,qhe->khe", d_cross_scores, query_float, precision=highest
    ).reshape(FRAMES * TEXT, D)
    d_text_values = jnp.einsum("hqk,qhe->khe", cross_probs, d_cross, precision=highest).reshape(
        FRAMES * TEXT, D
    )
    own_d_keys, own_d_values = (
        lax.psum_scatter(d_text_keys, "rows", scatter_dimension=0, tiled=True),
        lax.psum_scatter(d_text_values, "rows", scatter_dimension=0, tiled=True),
    )

    def text_head(text_rows, gain_row):
        return (normed(text_rows[:, :D], gain_row), text_rows[:, D:])

    text_pair, text_back = jax.vjp(text_head, own_text, gain_caption)
    d_own_text, d_gain_caption = text_back((own_d_keys, own_d_values))
    grad_text = jnp.einsum(
        "rc,rd->cd",
        own_captions,
        d_own_text.astype(jnp.bfloat16),
        preferred_element_type=jnp.float32,
    )
    delta_rows = jnp.sum(d_self * self_out, axis=-1).T
    piece_keys = lax.all_gather(key_b, "rows", axis=0, tiled=True)
    piece_values = lax.all_gather(value_b, "rows", axis=0, tiled=True)
    amount = piece_keys.shape[0]
    key_heads = piece_keys.reshape(amount, HEADS, HEAD)
    key_float = key_heads.astype(jnp.float32)
    value_float = piece_values.reshape(amount, HEADS, HEAD).astype(jnp.float32)
    allowed = frame_rows[:, None] == key_frames(amount)[None, :]
    scores = (
        jnp.einsum("qhe,khe->hqk", query_heads, key_heads, preferred_element_type=jnp.float32)
        * score_scale
    )
    scores = jnp.where(allowed[None], scores, masked_value)
    probs = jnp.exp(scores - log_total[:, :, None])
    d_probs = jnp.einsum("qhe,khe->hqk", d_self, value_float, precision=highest)
    d_scores = probs * (d_probs - delta_rows[:, :, None]) * score_scale
    grad_query = jnp.einsum("hqk,khe->qhe", d_scores, key_float, precision=highest)
    d_key_piece = jnp.einsum("hqk,qhe->khe", d_scores, query_float, precision=highest).reshape(
        amount, D
    )
    d_value_piece = jnp.einsum("hqk,qhe->khe", probs, d_self, precision=highest).reshape(amount, D)
    joined = jnp.concatenate([d_key_piece, d_value_piece], axis=1)
    grad_keys = joined
    grad_query, grad_keys = (grad_query, grad_keys)
    own_grad_kv = lax.psum_scatter(grad_keys, "rows", scatter_dimension=0, tiled=True)
    total_query = (grad_query + d_query_cross).reshape(TOK_DEV, D)
    d_qkv, d_gain_query, d_gain_key = heads_back(
        (total_query, own_grad_kv[:, :D], own_grad_kv[:, D:])
    )
    d_qkv_b = d_qkv.astype(jnp.bfloat16)
    grad_qkv = jnp.einsum("td,te->de", attn_in, d_qkv_b, preferred_element_type=jnp.float32)
    d_attn_in = jnp.einsum("te,de->td", d_qkv_b, back_qkv, preferred_element_type=jnp.float32)
    d_inputs_head, d_scale_attn, d_gain_one = attn_head_back(d_attn_in)
    grad_latent = d_inputs_tail + d_inputs_head
    d_mod_rows = jnp.concatenate([d_scale_attn, d_gate_attn, d_scale_ffn, d_gate_ffn], axis=1)
    d_modulation = jnp.einsum("tf,td->fd", onehot_float, d_mod_rows, precision=highest)
    grad_ada = jnp.einsum(
        "fc,fd->cd", silu_cond.astype(jnp.float32), d_modulation, precision=highest
    )
    grad_bias = jnp.sum(d_modulation, axis=0)
    grad_gains = jnp.stack(
        [
            d_gain_one,
            d_gain_two,
            d_gain_three,
            d_gain_four,
            d_gain_query,
            d_gain_key,
            d_gain_caption,
        ]
    )
    attn_grads = (
        lax.psum_scatter(grad_qkv, ("items", "rows"), scatter_dimension=0, tiled=True),
        lax.psum_scatter(grad_text, ("items", "rows"), scatter_dimension=0, tiled=True),
        lax.psum_scatter(grad_out_weight, ("items", "rows"), scatter_dimension=0, tiled=True),
        lax.psum_scatter(grad_ada, ("items", "rows"), scatter_dimension=0, tiled=True),
        lax.psum_scatter(grad_gains, ("items", "rows"), scatter_dimension=1, tiled=True),
        lax.psum_scatter(grad_bias, ("items", "rows"), scatter_dimension=0, tiled=True),
    )
    gates_total = lax.psum(grad_head_gates, ("items", "rows"))
    return (
        result_rows[None],
        grad_latent[None],
        attn_grads[0],
        attn_grads[1],
        attn_grads[2],
        ffn_grads[0],
        ffn_grads[1],
        attn_grads[3],
        attn_grads[5],
        attn_grads[4],
        gates_total,
    )


def solution(mesh):
    placed = (
        P("items", "rows", None),
        P("items", None, None),
        P("items", None, None, None),
        P("items", "rows", None),
        P("items", None),
        P(("items", "rows"), None),
        P(("items", "rows"), None),
        P(("items", "rows"), None),
        P(("items", "rows"), None),
        P(("items", "rows"), None),
        P(("items", "rows"), None),
        P(("items", "rows")),
        P(None, ("items", "rows")),
        P(),
        P("items", "rows", None),
    )
    return jax.shard_map(
        shards,
        mesh=mesh,
        in_specs=placed,
        out_specs=(
            P("items", "rows", None),
            P("items", "rows", None),
            P(("items", "rows"), None),
            P(("items", "rows"), None),
            P(("items", "rows"), None),
            P(("items", "rows"), None),
            P(("items", "rows"), None),
            P(("items", "rows"), None),
            P(("items", "rows")),
            P(None, ("items", "rows")),
            P(),
        ),
        check_vma=False,
    )
```

profile of v0, /device:TPU:0, one launch (start us, length us, event | category | flops | bytes accessed | tf_op | source)
XLA Modules:
  0.0 3230.2 jit_solution(13717199927711080514)
XLA Ops:
  9.6 42.9 %all-reduce.11 = bf16[6144]{0:T(1024)(128)(2,1)S(1)} all-reduce(bf16[6144]{0:T(1024)(128)(2,1)S(1)} %dynamic-update-slice), channel_id=1, replica_groups=mesh['items'=2,'rows'=16] {'items','rows'}, use_global_device_ids=true, to_apply=%add.11 | all-reduce | flops 6144 | bytes 24576
  52.5 21.5 all-gather
  74.0 37.5 %all-gather.1 = bf16[32,48,7]{1,2,0:T(8,128)(2,1)S(1)} all-gather(bf16[1,48,7]{1,2,0:T(8,128)(2,1)} %bitcast.196), channel_id=1, replica_groups=mesh['items'=2,'rows'=16] {'items','rows'}, dimensions={0}, use_global_device_ids=true | all-gather | bytes 22176 | tf_op jit(solution)/shard_map/all_gather | solution.py:75
  124.0 91.6 %all-gather.13.cloned.1.call-done = bf16[1536,4608]{1,0:T(8,128)(2,1)} async-done(((bf16[48,4608]{1,0:T(8,128)(2,1)}), bf16[1536,4608]{1,0:T(8,128)(2,1)}) %all-gather.13.cloned.1.call-update) | async-done | bytes 14155792 | tf_op jit(solution)/shard_map/all_gather | solution.py:71
  255.4 52.6 %all-gather.15.cloned.1.call-done = bf16[2048,1536]{1,0:T(8,128)(2,1)} async-done(((bf16[128,1536]{1,0:T(8,128)(2,1)}), bf16[2048,1536]{1,0:T(8,128)(2,1)}) %all-gather.15.cloned.1.call-update) | async-done | bytes 6291472 | tf_op jit(solution)/shard_map/all_gather | solution.py:137
  316.7 54.5 %all-gather.17.cloned.1.call-done = bf16[2048,1536]{1,0:T(8,128)(2,1)} async-done(((bf16[128,1536]{1,0:T(8,128)(2,1)}), bf16[2048,1536]{1,0:T(8,128)(2,1)}) %all-gather.17.cloned.1.call-update) | async-done | bytes 6291472 | tf_op jit(solution)/shard_map/all_gather | solution.py:138
  408.2 119.0 %all-gather.19.cloned.1.call-done = bf16[4096,3072]{1,0:T(8,128)(2,1)} async-done(((bf16[128,3072]{1,0:T(8,128)(2,1)}), bf16[4096,3072]{1,0:T(8,128)(2,1)}) %all-gather.19.cloned.1.call-update) | async-done | bytes 25165840 | tf_op jit(solution)/shard_map/all_gather | solution.py:72
  527.2 18.0 fusion.130
  571.1 24.3 add_convert_fusion.2
  601.6 146.5 %all-gather.23.cloned.1.call-done = bf16[1536,8192]{1,0:T(8,128)(2,1)} async-done(((bf16[48,8192]{1,0:T(8,128)(2,1)}), bf16[1536,8192]{1,0:T(8,128)(2,1)}) %all-gather.23.cloned.1.call-update) | async-done | bytes 25165840 | tf_op jit(solution)/shard_map/all_gather | solution.py:174
  762.2 83.0 %all-gather.25.cloned.1.call-done = bf16[4096,1536]{1,0:T(8,128)(2,1)} async-done(((bf16[128,1536]{1,0:T(8,128)(2,1)}), bf16[4096,1536]{1,0:T(8,128)(2,1)}) %all-gather.25.cloned.1.call-update) | async-done | bytes 12582928 | tf_op jit(solution)/shard_map/all_gather | solution.py:175
  903.4 19.4 fusion.2
  950.3 20.4 multiply_multiply_fusion
  1045.5 20.4 convolution_add_fusion.1
  1092.7 169.0 %reduce-scatter.13.cloned.1.call-done = f32[128,3072]{1,0:T(8,128)} async-done(((f32[2048,3072]{1,0:T(8,128)}), f32[128,3072]{1,0:T(8,128)}) %reduce-scatter.13.cloned.1.call-update) | async-done | bytes 1572880 | tf_op jit(solution)/shard_map/reduce_scatter | solution.py:274
  1321.2 21.7 fusion.63
  1362.8 20.6 fusion.65
  1398.2 40.0 %all-reduce.13 = (f32[6144]{0:T(1024)S(1)}, f32[24]{0:T(128)}) all-reduce(f32[6144]{0:T(1024)S(1)} %copy-done.47, f32[24]{0:T(128)S(1)} %subtract_multiply_fusion.1), channel_id=12, replica_groups=mesh['items'=2,'rows'=16] {'items','rows'}, use_global_device_ids=true, to_apply=%region_37.38.clone | all-reduce | flops 6168 | bytes 49344
  1443.1 128.4 %reduce-scatter.23.cloned.1.call-done = f32[48,1536]{1,0:T(8,128)} async-done(((f32[1536,1536]{1,0:T(8,128)}), f32[48,1536]{1,0:T(8,128)}) %reduce-scatter.23.cloned.1.call-update) | async-done | bytes 294928 | tf_op jit(solution)/shard_map/reduce_scatter | solution.py:304
  1571.4 252.6 %reduce-scatter.27.cloned.1.call-done = f32[128,1536]{1,0:T(8,128)} async-done(((f32[4096,1536]{1,0:T(8,128)}), f32[128,1536]{1,0:T(8,128)}) %reduce-scatter.27.cloned.1.call-update) | async-done | bytes 786448 | tf_op jit(solution)/shard_map/reduce_scatter | solution.py:206
  1824.0 438.0 %reduce-scatter.25.cloned.1.call-done = f32[48,8192]{1,0:T(8,128)} async-done(((f32[1536,8192]{1,0:T(8,128)}), f32[48,8192]{1,0:T(8,128)}) %reduce-scatter.25.cloned.1.call-update) | async-done | bytes 1572880 | tf_op jit(solution)/shard_map/reduce_scatter | solution.py:205
  2262.0 251.3 %reduce-scatter.29.cloned.1.call-done = f32[32,6144]{1,0:T(8,128)} async-done(((f32[1024,6144]{1,0:T(8,128)}), f32[32,6144]{1,0:T(8,128)}) %reduce-scatter.29.cloned.1.call-update) | async-done | bytes 786448 | tf_op jit(solution)/shard_map/reduce_scatter | solution.py:305
  2513.3 439.1 %reduce-scatter.21.cloned.1.call-done = f32[128,3072]{1,0:T(8,128)} async-done(((f32[4096,3072]{1,0:T(8,128)}), f32[128,3072]{1,0:T(8,128)}) %reduce-scatter.21.cloned.1.call-update) | async-done | bytes 1572880 | tf_op jit(solution)/shard_map/reduce_scatter | solution.py:303
  2952.4 270.7 %reduce-scatter.15.cloned.1.call-done = f32[48,4608]{1,0:T(8,128)} async-done(((f32[1536,4608]{1,0:T(8,128)}), f32[48,4608]{1,0:T(8,128)}) %reduce-scatter.15.cloned.1.call-update) | async-done | bytes 884752 | tf_op jit(solution)/shard_map/reduce_scatter | solution.py:302
  (346 shorter events, 431.9 us)
Async XLA Ops:
  7.2 245.5 %copy-start = (s32[1,2]{1,0:T(1,128)S(1)}, s32[1,2]{1,0:T(1,128)}, u32[]{:S(2)}) copy-start(s32[1,2]{1,0:T(1,128)} %param.19) | copy-start | bytes 28
  7.2 108.6 %all-gather.11.cloned.1.call-start = ((), (), s32[]{:S(2)}) async-start(), calls=%async_computation.10 | async-start | bytes 12976128 | tf_op jit(solution)/shard_map/all_gather | solution.py:74
  7.9 207.7 %all-gather.13.cloned.1.call-start = ((), (), s32[]{:S(2)}) async-start(), calls=%async_computation.11 | async-start | bytes 14598144 | tf_op jit(solution)/shard_map/all_gather | solution.py:71
  8.7 299.3 %all-gather.15.cloned.1.call-start = ((), (), s32[]{:S(2)}) async-start(), calls=%async_computation.12 | async-start | bytes 6684672 | tf_op jit(solution)/shard_map/all_gather | solution.py:137
  247.8 123.3 %all-gather.17.cloned.1.call-start = ((), (), s32[]{:S(2)}) async-start(), calls=%async_computation.13 | async-start | bytes 6684672 | tf_op jit(solution)/shard_map/all_gather | solution.py:138
  249.8 277.3 %all-gather.19.cloned.1.call-start = ((), (), s32[]{:S(2)}) async-start(), calls=%async_computation.14 | async-start | bytes 25952256 | tf_op jit(solution)/shard_map/all_gather | solution.py:72
  250.4 345.0 %all-gather.21.cloned.1.call-start = ((), (), s32[]{:S(2)}) async-start(), calls=%async_computation.15 | async-start | bytes 4866048 | tf_op jit(solution)/shard_map/all_gather | solution.py:73
  251.0 497.1 %all-gather.23.cloned.1.call-start = ((), (), s32[]{:S(2)}) async-start(), calls=%async_computation.16 | async-start | bytes 25952256 | tf_op jit(solution)/shard_map/all_gather | solution.py:174
  251.8 593.4 %all-gather.25.cloned.1.call-start = ((), (), s32[]{:S(2)}) async-start(), calls=%async_computation.17 | async-start | bytes 12976128 | tf_op jit(solution)/shard_map/all_gather | solution.py:175
  252.5 837.8 %reduce-scatter.19.cloned.1.call-start = ((), (), s32[]{:S(2)}) async-start(), calls=%async_computation.21 | async-start | bytes 3342336 | tf_op jit(solution)/shard_map/reduce_scatter | solution.py:235
  253.0 318.0 %copy-start.77 = (f32[24]{0:T(128)}, f32[24]{0:T(128)S(1)}, u32[]{:S(2)}) copy-start(f32[24]{0:T(128)S(1)} %convert_tanh_fusion) | copy-start | bytes 292
  253.2 684.5 %copy-start.30 = (pred[128,512]{1,0:T(8,128)(4,1)}, pred[128,512]{1,0:T(8,128)(4,1)S(1)}, u32[]{:S(2)}) copy-start(pred[128,512]{1,0:T(8,128)(4,1)S(1)} %compare_and_fusion) | copy-start | bytes 196612
  562.8 374.8 %copy-start.44 = (f32[24,128]{1,0:T(8,128)}, f32[24,128]{1,0:T(8,128)S(1)}, u32[]{:S(2)}) copy-start(f32[24,128]{1,0:T(8,128)S(1)} %get-tuple-element.75) | copy-start | bytes 36868
  950.3 311.4 %reduce-scatter.13.cloned.1.call-start = ((), (), s32[]{:S(2)}) async-start(), calls=%async_computation.18 | async-start | bytes 26738688 | tf_op jit(solution)/shard_map/reduce_scatter | solution.py:274
  1017.9 344.9 %reduce-scatter.17.cloned.1.call-start = ((), (), s32[]{:S(2)}) async-start(), calls=%async_computation.20 | async-start | bytes 3342336 | tf_op jit(solution)/shard_map/reduce_scatter | solution.py:236
  1045.5 396.2 %reduce-scatter.31.cloned.1.call-start = ((), (), s32[]{:S(2)}) async-start(), calls=%async_computation.27 | async-start | bytes 811008
  1066.0 195.7 %copy-start.40 = (f32[1536]{0:T(1024)S(1)}, f32[1536]{0:T(1024)}, u32[]{:S(2)}) copy-start(f32[1536]{0:T(1024)} %fusion.74) | copy-start | bytes 18436
  1301.5 269.9 %reduce-scatter.23.cloned.1.call-start = ((), (), s32[]{:S(2)}) async-start(), calls=%async_computation.23 | async-start | bytes 9732096 | tf_op jit(solution)/shard_map/reduce_scatter | solution.py:304
  1307.6 516.4 %reduce-scatter.27.cloned.1.call-start = ((), (), s32[]{:S(2)}) async-start(), calls=%async_computation.25 | async-start | bytes 25952256 | tf_op jit(solution)/shard_map/reduce_scatter | solution.py:206
  1320.2 941.8 %reduce-scatter.25.cloned.1.call-start = ((), (), s32[]{:S(2)}) async-start(), calls=%async_computation.24 | async-start | bytes 51904512 | tf_op jit(solution)/shard_map/reduce_scatter | solution.py:205
  1343.0 1170.4 %reduce-scatter.29.cloned.1.call-start = ((), (), s32[]{:S(2)}) async-start(), calls=%async_computation.26 | async-start | bytes 25952256 | tf_op jit(solution)/shard_map/reduce_scatter | solution.py:305
  1360.9 1591.6 %reduce-scatter.21.cloned.1.call-start = ((), (), s32[]{:S(2)}) async-start(), calls=%async_computation.22 | async-start | bytes 51904512 | tf_op jit(solution)/shard_map/reduce_scatter | solution.py:303
  1383.5 1839.7 %reduce-scatter.15.cloned.1.call-start = ((), (), s32[]{:S(2)}) async-start(), calls=%async_computation.19 | async-start | bytes 29196288 | tf_op jit(solution)/shard_map/reduce_scatter | solution.py:302
  1397.5 1825.7 %copy-start.1 = (s32[1,2]{1,0:T(1,128)S(1)}, s32[1,2]{1,0:T(1,128)}, u32[]{:S(2)}) copy-start(s32[1,2]{1,0:T(1,128)} %param.19) | copy-start | bytes 28
  (78 other events, 1870.0 us)
Sparse Core Ops, SparseCore 0:
  10.9 100.2 all-gather.10
  114.1 101.4 all-gather.12
  248.0 59.9 all-gather.14
  310.7 60.4 all-gather.16
  373.9 153.2 all-gather.18
  529.9 61.7 all-gather.20
  594.6 153.4 all-gather.22
  751.0 94.1 all-gather.24
  950.4 64.4 reduce-scatter.18
  1018.9 242.7 reduce-scatter.12
  1265.5 65.3 reduce-scatter.16
  1335.9 94.4 reduce-scatter.30
  1436.8 134.5 reduce-scatter.22
  1579.4 244.5 reduce-scatter.26
  1830.9 431.1 reduce-scatter.24
  2268.9 244.3 reduce-scatter.28
  2521.3 431.0 reduce-scatter.20
  2960.4 262.6 reduce-scatter.14
where the time goes:
time: 3240 us; the launch traced here: 3230 us
  waiting for transfers between devices  2500 us (77%)
  matrix products  353 us (11%)
  blocking collectives  142 us (4%)
  local copies, waits for them, and re-layouts  112 us (3%)
  other arithmetic  106 us (3%)
    reduce_scatter x1, waiting for transfers between devices, shards(): lax.psum_scatter(grad_text, ('items', 'rows'), scatter_dimension=0, tiled...  439 us
    reduce_scatter x1, waiting for transfers between devices, shards(): lax.psum_scatter(grad_gate_up, ('items', 'rows'), scatter_dimension=0, ti...  438 us
    reduce_scatter x1, waiting for transfers between devices, shards(): lax.psum_scatter(grad_qkv, ('items', 'rows'), scatter_dimension=0, tiled=...  271 us
    reduce_scatter x1, waiting for transfers between devices, shards(): lax.psum_scatter(grad_down, ('items', 'rows'), scatter_dimension=0, tiled...  253 us
    reduce_scatter x1, waiting for transfers between devices, shards(): lax.psum_scatter(grad_ada, ('items', 'rows'), scatter_dimension=0, tiled=...  251 us
    reduce_scatter x1, waiting for transfers between devices, shards(): lax.psum_scatter(grad_keys, 'rows', scatter_dimension=0, tiled=True)  169 us
    all_gather x1, waiting for transfers between devices, shards(): lax.all_gather(gate_up_weight, ('items', 'rows'), axis=0, tiled=True)  147 us
    reduce_scatter x1, waiting for transfers between devices, shards(): lax.psum_scatter(grad_out_weight, ('items', 'rows'), scatter_dimension=0,...  128 us
  transfers between devices with their start and end apart: 18, of which 13 were waited for; matrix products, arithmetic and copies ran while one was open for 13% of the time, Pallas kernels for 0%

commit v1 on v0

v1 whole, which is shorter than its diff:
```python
import jax
import jax.numpy as jnp
import numpy as np
from jax import lax
from jax.experimental import pallas as pl
from jax.experimental.pallas import tpu as pltpu
from jax.sharding import Mesh
from jax.sharding import PartitionSpec as P

D = 1536
HEADS = 24
HEAD = 64
FF = 4096
TEXT_DIM = 4096
COND = 1024
TEXT = 256
FRAMES = 2
TOK = 128
GROUPS = 2
M = 8
LOCAL = HEADS // M * HEAD
ROWS = M * TOK
WIDE = 256
APART = 8192.0

epsilon = 1e-05
theta_base = 10000.0
highest = lax.Precision.HIGHEST
MESH = pl.DeviceIdType.MESH
f32 = jnp.float32
bf16 = jnp.bfloat16
ANY = pl.BlockSpec(memory_space=pl.ANY)
VMEM = pl.BlockSpec(memory_space=pltpu.VMEM)


def flip(where, mask):
    return tuple(a if b == 0 else a ^ b for a, b in zip(where, mask))


class Job:
    def __init__(self, x, shape, masks, src, dst, pass_on=(), by=None, source=None):
        self.x, self.shape, self.masks, self.src, self.dst = x, shape, masks, src, dst
        self.pass_on, self.by, self.source = tuple(pass_on), by, source
        if source is not None:
            self.x = None
        self.dtype = x.dtype

    def count(self):
        return len(self.masks) + len(self.pass_on)

    def block(self):
        return self.shape[len(self.dst((0, 0, 0))) :]

    def peers(self):
        return set(self.masks) | ({self.by} if self.pass_on else set())


class Transfers:
    def __init__(self, jobs):
        self.jobs = jobs
        self.sent = [j for j in jobs if j.source is None]
        self.total = sum(j.count() for j in jobs)

    def operands(self):
        return [j.x for j in self.sent]

    def out_shapes(self):
        return [jax.ShapeDtypeStruct(j.shape, j.dtype) for j in self.jobs]

    def scratch(self):
        if not self.jobs:
            return []
        return [
            pltpu.SemaphoreType.DMA((self.total,)),
            pltpu.SemaphoreType.DMA((self.total,)),
            pltpu.SemaphoreType.DMA((2, len(self.jobs))),
        ] + [pltpu.VMEM(j.block(), j.dtype) for j in self.jobs]

    def peers(self):
        found = set()
        for j in self.jobs:
            found |= j.peers()
        return found

    def bind(self, me, ins, outs, sems):
        self.me, self.outs, self.sems = me, outs, sems
        left = list(ins)
        self.ins = []
        for j in self.jobs:
            self.ins.append(left.pop(0) if j.source is None else outs[self.jobs.index(j.source)])
        self.base, at = [], 0
        for j in self.jobs:
            self.base.append(at)
            at += j.count()
        self.arrived, self.kept, self.settled, self.chained, self.forwarded = set(), set(), set(), set(), set()

    def remote(self, src, dst, slot, dest):
        return pltpu.make_async_remote_copy(
            src_ref=src,
            dst_ref=dst,
            send_sem=self.sems[0].at[slot],
            recv_sem=self.sems[1].at[slot],
            device_id=dest,
            device_id_type=MESH,
        )

    def send(self, k, i):
        j = self.jobs[k]
        if i < len(j.masks):
            dest = flip(self.me, j.masks[i])
            at = j.src(dest)
            src = self.ins[k] if at is None else self.ins[k].at[at]
            return self.remote(src, self.outs[k].at[j.dst(self.me)], self.base[k] + i, dest)
        mask = j.pass_on[i - len(j.masks)]
        block = self.outs[k].at[j.dst(flip(self.me, mask))]
        return self.remote(block, block, self.base[k] + i, flip(self.me, j.by))

    def own(self, k, leg):
        j = self.jobs[k]
        room = self.sems[3 + k]
        if leg == 0:
            at = j.src(self.me)
            src = self.ins[k] if at is None else self.ins[k].at[at]
            return pltpu.make_async_copy(src, room, self.sems[2].at[0, k])
        return pltpu.make_async_copy(room, self.outs[k].at[j.dst(self.me)], self.sems[2].at[1, k])

    def start_job(self, k):
        j = self.jobs[k]
        for i in range(len(j.masks)):
            self.send(k, i).start()
        self.own(k, 0).start()

    def start(self):
        for k, j in enumerate(self.jobs):
            if j.source is None:
                self.start_job(k)

    def receive(self, k, i):
        if (k, i) not in self.arrived:
            self.arrived.add((k, i))
            self.send(k, i).wait_recv()

    def take(self, k):
        self.keep(k)
        for i in range(self.jobs[k].count()):
            self.receive(k, i)
        if k not in self.settled:
            self.settled.add(k)
            self.own(k, 1).wait()

    def keep(self, k):
        if k not in self.kept:
            self.kept.add(k)
            self.own(k, 0).wait()
            self.own(k, 1).start()

    def chain(self):
        for k, j in enumerate(self.jobs):
            if j.source is not None and k not in self.chained:
                self.chained.add(k)
                self.take(self.jobs.index(j.source))
                self.start_job(k)

    def forward(self):
        self.chain()
        for k in range(len(self.jobs)):
            self.keep(k)
        for k, j in enumerate(self.jobs):
            if k not in self.forwarded:
                self.forwarded.add(k)
                for n, mask in enumerate(j.pass_on):
                    self.receive(k, j.masks.index(mask))
                    self.send(k, len(j.masks) + n).start()

    def finish(self):
        self.forward()
        for k, j in enumerate(self.jobs):
            self.take(k)
            for i in range(j.count()):
                self.send(k, i).wait_send()


class Plan:
    def __init__(self, times):
        self.times = times
        self.sets = GROUPS * times
        self.rows = times * M
        self.next_id = 0
        ones = [(i, t, m) for i in range(GROUPS) for t in range(times) for m in range(M)]
        self.all = ones[1:]
        self.ring = [(0, 0, m) for m in range(1, M)]
        self.chips = [(0, 0, m) for m in range(2, M, 2)]
        self.mate = (0, 0, 1)
        self.time = [(0, t, 0) for t in range(1, times)]
        self.item = (1, 0, 0)
        self.span = [(i, t, 0) for i in range(GROUPS) for t in range(times)][1:]
        self.group = [(0, t, m) for t in range(times) for m in range(M)][1:]

    def identity(self):
        self.next_id += 1
        return self.next_id

    def set_of(self, where):
        return where[0] * self.times + where[1]

    def gather_ring(self, x):
        return Job(
            x,
            (M,) + x.shape,
            [self.mate] + self.chips,
            lambda dest: None,
            lambda sender: (sender[2],),
            self.chips,
            self.mate,
        )

    def direct_ring(self, x):
        return Job(x, (M,) + x.shape, self.ring, lambda dest: None, lambda sender: (sender[2],))

    def scatter_ring(self, x):
        return Job(x, x.shape, self.ring, lambda dest: (dest[2],), lambda sender: (sender[2],))

    def gather_span(self, x, shape=None, source=None):
        return Job(
            x,
            (self.sets,) + (x.shape if shape is None else shape),
            [self.item] + self.time,
            lambda dest: None,
            lambda sender: (self.set_of(sender),),
            self.time,
            self.item,
            source,
        )

    def scatter_span(self, x):
        return Job(x, x.shape, self.span, lambda dest: (self.set_of(dest),), lambda sender: (self.set_of(sender),))

    def gather_time(self, x):
        return Job(x, (self.times,) + x.shape, self.time, lambda dest: None, lambda sender: (sender[1],))

    def gather_time_part(self, x, start, count):
        return Job(
            x,
            (self.times, count) + x.shape[1:],
            self.time,
            lambda dest: (pl.ds(start, count),),
            lambda sender: (sender[1],),
        )

    def swap_item_part(self, x, start, count):
        return Job(
            x,
            (GROUPS, count) + x.shape[1:],
            [self.item],
            lambda dest: (pl.ds(start, count),),
            lambda sender: (sender[0],),
        )

    def scatter_time(self, x):
        return Job(x, x.shape, self.time, lambda dest: (dest[1],), lambda sender: (sender[1],))

    def scatter_item(self, x):
        return Job(x, x.shape, [self.item], lambda dest: (dest[0],), lambda sender: (sender[0],))

    def gather_all(self, x):
        return Job(
            x,
            (self.sets, M) + x.shape,
            self.all,
            lambda dest: None,
            lambda sender: (self.set_of(sender), sender[2]),
        )

    def scatter_all(self, x):
        return Job(
            x,
            x.shape,
            self.all,
            lambda dest: (self.set_of(dest), dest[2]),
            lambda sender: (self.set_of(sender), sender[2]),
        )

    def swap_item(self, x):
        return Job(x, (GROUPS,) + x.shape, [self.item], lambda dest: None, lambda sender: (sender[0],))

    def gather_group(self, x):
        return Job(
            x,
            (self.times, M) + x.shape,
            self.group,
            lambda dest: None,
            lambda sender: (sender[1], sender[2]),
        )

    def scatter_group(self, x):
        return Job(
            x,
            x.shape,
            self.group,
            lambda dest: (dest[1], dest[2]),
            lambda sender: (sender[1], sender[2]),
        )


def here():
    return (lax.axis_index("items"), lax.axis_index("times"), lax.axis_index("ring"))


def greet(me, peers):
    barrier = pltpu.get_barrier_semaphore()
    for mask in sorted(peers):
        pl.semaphore_signal(barrier, inc=1, device_id=flip(me, mask), device_id_type=MESH)
    pl.semaphore_wait(barrier, len(peers))


def exchange(plan, name, jobs):
    moves = Transfers(jobs)
    n_in, n_out = len(moves.sent), len(jobs)

    def kernel(*refs):
        me = here()
        greet(me, moves.peers())
        moves.bind(me, refs[:n_in], refs[n_in : n_in + n_out], refs[n_in + n_out :])
        moves.start()
        moves.finish()

    return pl.pallas_call(
        kernel,
        out_shape=moves.out_shapes(),
        in_specs=[ANY] * n_in,
        out_specs=[ANY] * n_out,
        scratch_shapes=moves.scratch(),
        name=name,
        compiler_params=pltpu.CompilerParams(
            collective_id=plan.identity(), has_side_effects=True, vmem_limit_bytes=32 * 2**20
        ),
    )(*moves.operands())


def product_scatter(plan, name, factors, turned, jobs=()):
    moves = Transfers(list(jobs))
    n_factors = len(factors)
    n_in, n_out = len(moves.sent), len(moves.jobs)
    contract = (((1,), (1,)), ((), ())) if turned else (((1,), (0,)), ((), ()))

    def kernel(*refs):
        factor_refs, refs = refs[: 2 * n_factors], refs[2 * n_factors :]
        ins = refs[:n_in]
        out_ref = refs[n_in]
        outs = refs[1 + n_in : 1 + n_in + n_out]
        to_mate, from_mate, part, to_chip, from_chip, send_sem, recv_sem = refs[1 + n_in + n_out : 8 + n_in + n_out]
        me = here()
        ring = me[2]
        core, chip = ring % 2, ring // 2
        greet(me, moves.peers() | {plan.mate} | set(plan.chips))
        if moves.jobs:
            moves.bind(me, ins, outs, refs[8 + n_in + n_out :])
            moves.start()

        def mate_copy(d):
            return pltpu.make_async_remote_copy(
                src_ref=to_mate.at[d],
                dst_ref=from_mate.at[d],
                send_sem=send_sem.at[d],
                recv_sem=recv_sem.at[d],
                device_id=flip(me, plan.mate),
                device_id_type=MESH,
            )

        def chip_copy(d):
            return pltpu.make_async_remote_copy(
                src_ref=to_chip.at[d - 1],
                dst_ref=from_chip.at[d - 1],
                send_sem=send_sem.at[3 + d],
                recv_sem=recv_sem.at[3 + d],
                device_id=flip(me, (0, 0, 2 * d)),
                device_id_type=MESH,
            )

        def block(d, which):
            start = pl.multiple_of((chip ^ d) * (2 * TOK) + which * TOK, TOK)
            products = [
                lax.dot_general(
                    factor_refs[2 * i][pl.ds(start, TOK), :],
                    factor_refs[2 * i + 1][...],
                    contract,
                    preferred_element_type=f32,
                )
                for i in range(n_factors)
            ]
            return sum(products[1:], products[0])

        for d in (3, 2, 1, 0):
            to_mate[d] = block(d, 1 - core).astype(bf16)
            mate_copy(d).start()
        for d in (3, 2, 1):
            part[...] = block(d, core)
            mate_copy(d).wait_recv()
            to_chip[d - 1] = (part[...] + from_mate[d].astype(f32)).astype(bf16)
            chip_copy(d).start()
        part[...] = block(0, core)
        mate_copy(0).wait_recv()
        part[...] = part[...] + from_mate[0].astype(f32)
        for d in (3, 2, 1):
            chip_copy(d).wait_recv()
        out_ref[...] = part[...] + (
            from_chip[0].astype(f32) + from_chip[1].astype(f32) + from_chip[2].astype(f32)
        )
        for d in range(4):
            mate_copy(d).wait_send()
        for d in (1, 2, 3):
            chip_copy(d).wait_send()
        if moves.jobs:
            moves.finish()

    result = pl.pallas_call(
        kernel,
        out_shape=[jax.ShapeDtypeStruct((TOK, D), f32)] + moves.out_shapes(),
        in_specs=[VMEM] * (2 * n_factors) + [ANY] * n_in,
        out_specs=[VMEM] + [ANY] * n_out,
        scratch_shapes=[
            pltpu.VMEM((4, TOK, D), bf16),
            pltpu.VMEM((4, TOK, D), bf16),
            pltpu.VMEM((TOK, D), f32),
            pltpu.VMEM((3, TOK, D), bf16),
            pltpu.VMEM((3, TOK, D), bf16),
            pltpu.SemaphoreType.DMA((7,)),
            pltpu.SemaphoreType.DMA((7,)),
        ]
        + moves.scratch(),
        name=name,
        compiler_params=pltpu.CompilerParams(
            collective_id=plan.identity(), has_side_effects=True, vmem_limit_bytes=48 * 2**20
        ),
    )(*[x for pair in factors for x in pair], *moves.operands())
    return result[0], result[1:]


def normed(value, gain_row):
    return value * lax.rsqrt(jnp.mean(value * value, axis=-1, keepdims=True) + epsilon) * gain_row


def attn_head(input_rows, scale_rows, gain_row):
    return normed(input_rows, gain_row) * (1.0 + scale_rows)


def attn_tail(input_rows, proj_rows, gate_rows, gain_row):
    return input_rows + jnp.tanh(gate_rows) * normed(proj_rows, gain_row)


def dot(a, b, dims=(1, 0)):
    return lax.dot_general(a, b, (((dims[0],), (dims[1],)), ((), ())), preferred_element_type=f32)


def halves_order():
    col = np.arange(LOCAL)
    head, pair, odd = col // HEAD, col % HEAD // 2, col % 2
    place = odd * (LOCAL // 2) + head * (HEAD // 2) + pair
    order = np.zeros(LOCAL, np.int64)
    order[place] = col
    full = np.concatenate([order, LOCAL + order, 2 * LOCAL + col])
    return order, full


def shuffle(order):
    n = order.shape[0]
    line = jnp.arange(n, dtype=jnp.int32)
    return (line[:, None] == jnp.asarray(order, jnp.int32)[None, :]).astype(bf16)


def turn(rows, cos, sin):
    half = LOCAL // 2
    first, second = rows[:, :half], rows[:, half:]
    return jnp.concatenate([first * cos - second * sin, second * cos + first * sin], axis=1)


def lane_masks():
    lane = np.arange(WIDE)
    query, value = np.zeros((8, WIDE), np.float32), np.zeros((8, WIDE), np.float32)
    back = np.zeros((8, WIDE), np.float32)
    half = HEAD // 2
    for h in range(LOCAL // HEAD):
        query[h] = ((lane < LOCAL) & (lane % (LOCAL // 2) // half == h)) | (lane == LOCAL) | (lane == LOCAL + 1)
        query[h] += (lane >= LOCAL + 2 + 3 * h) & (lane < LOCAL + 5 + 3 * h)
        value[h] = ((lane >= HEAD) & (lane // HEAD - 1 == h)) | (lane // 16 == h)
        back[h] = ((lane >= HEAD) & (lane // HEAD - 1 == h)) | (lane == 2 * h) | (lane == 2 * h + 1)
    return query, value, back


def widen(packed_ref, feature, key_ref, value_ref, rows):
    lane = lax.broadcasted_iota(jnp.int32, (rows, 128), 1)
    middle = packed_ref[:, 128:256].astype(f32)
    key_ref[:rows, :128] = packed_ref[:, :128]
    key_ref[:rows, 128:] = jnp.where(lane < HEAD, middle, feature.astype(f32)).astype(bf16)
    value_ref[:rows, :128] = jnp.where(lane < HEAD, 1.0, middle).astype(bf16)
    value_ref[:rows, 128:] = packed_ref[:, 256:]


def flash_forward(plan, query, packed, features, text_packed, text_features, gates, jobs):
    heads = LOCAL // HEAD
    text_rows = text_packed.shape[0]
    keys_job = plan.gather_time(packed)
    moves = Transfers([keys_job] + list(jobs))
    n_in, n_out = len(moves.sent) - 1, len(moves.jobs)
    block = 256

    def kernel(*refs):
        query_ref, packed_ref, feature_ref, text_ref, text_feature_ref, gate_ref, qmask_ref, vmask_ref = refs[:8]
        ins = refs[8 : 9 + n_in]
        mixed_ref, self_ref, cross_ref = refs[9 + n_in : 12 + n_in]
        outs = refs[12 + n_in : 12 + n_in + n_out]
        key_ref, value_ref, far_ref, max_ref, sem = refs[12 + n_in + n_out : 17 + n_in + n_out]
        me = here()
        greet(me, moves.peers())
        moves.bind(me, ins, outs, refs[17 + n_in + n_out :])
        moves.start()

        def segment(rows, first, out_ref):
            def body(at, carry):
                where = pl.ds(pl.multiple_of(at * block, block), block)
                query_rows = query_ref[where, :]
                total = jnp.zeros((block, WIDE), f32)
                tops = jnp.zeros((block, WIDE), f32)
                for h in range(heads):
                    own_query = query_rows * qmask_ref[h : h + 1, :]
                    scores = lax.dot_general(
                        own_query, key_ref[:rows, :], (((1,), (1,)), ((), ())), preferred_element_type=f32
                    )
                    top = jnp.max(scores, axis=1, keepdims=True)
                    weights = jnp.exp(scores - top).astype(bf16)
                    product = jnp.dot(weights, value_ref[:rows, :], preferred_element_type=f32)
                    total += product * vmask_ref[h : h + 1, :]
                    tops += top * vmask_ref[h : h + 1, :]
                if first:
                    out_ref[where, :] = total
                    max_ref[where, :] = tops
                else:
                    before = max_ref[where, :]
                    after = jnp.maximum(before, tops)
                    out_ref[where, :] = out_ref[where, :] * jnp.exp(before - after) + total * jnp.exp(tops - after)
                    max_ref[where, :] = after
                return carry

            lax.fori_loop(0, ROWS // block, body, 0)

        def close(out_ref):
            def body(at, carry):
                where = pl.ds(pl.multiple_of(at * block, block), block)
                lane = lax.broadcasted_iota(jnp.int32, (block, WIDE), 1)
                values = out_ref[where, :]
                share = jnp.ones((block, WIDE), f32)
                for h in range(heads):
                    share = jnp.where(
                        (lane >= HEAD * (h + 1)) & (lane < HEAD * (h + 2)), values[:, 16 * h : 16 * h + 1], share
                    )
                logs = max_ref[where, :] + jnp.log(jnp.maximum(values, 1e-30))
                out_ref[where, :] = jnp.where(
                    lane < HEAD, jnp.where(lane < 16 * heads, logs, 0.0), values / share
                )
                return carry

            lax.fori_loop(0, ROWS // block, body, 0)

        widen(text_ref, text_feature_ref[...], key_ref, value_ref, text_rows)
        segment(text_rows, True, cross_ref)
        close(cross_ref)
        moves.chain()
        own_rows = pl.ds(pl.multiple_of(me[1] * ROWS, ROWS), ROWS)
        widen(packed_ref, feature_ref[own_rows, :], key_ref, value_ref, ROWS)
        segment(ROWS, True, self_ref)
        for i, mask in enumerate(plan.time):
            moves.receive(0, i)
            far = me[1] ^ mask[1]
            bring = pltpu.make_async_copy(outs[0].at[far], far_ref, sem)
            bring.start()
            bring.wait()
            far_rows = pl.ds(pl.multiple_of(far * ROWS, ROWS), ROWS)
            widen(far_ref, feature_ref[far_rows, :], key_ref, value_ref, ROWS)
            segment(ROWS, False, self_ref)
        moves.forward()
        close(self_ref)
        lane = lax.broadcasted_iota(jnp.int32, (ROWS, WIDE), 1)
        both = self_ref[...] + gate_ref[...] * cross_ref[...]
        mixed_ref[...] = jnp.where(lane < HEAD, 0.0, both).astype(bf16)
        moves.finish()

    qmask, vmask, _ = lane_masks()
    result = pl.pallas_call(
        kernel,
        out_shape=[
            jax.ShapeDtypeStruct((ROWS, WIDE), bf16),
            jax.ShapeDtypeStruct((ROWS, WIDE), f32),
            jax.ShapeDtypeStruct((ROWS, WIDE), f32),
        ]
        + moves.out_shapes(),
        in_specs=[VMEM] * 8 + [ANY] * (n_in + 1),
        out_specs=[VMEM] * 3 + [ANY] * n_out,
        scratch_shapes=[
            pltpu.VMEM((ROWS, WIDE), bf16),
            pltpu.VMEM((ROWS, WIDE), bf16),
            pltpu.VMEM((ROWS, 2 * LOCAL), bf16),
            pltpu.VMEM((ROWS, WIDE), f32),
            pltpu.SemaphoreType.DMA(()),
        ]
        + moves.scratch(),
        name="flash_forward",
        compiler_params=pltpu.CompilerParams(
            collective_id=plan.identity(), has_side_effects=True, vmem_limit_bytes=56 * 2**20
        ),
    )(
        query,
        packed,
        features,
        text_packed,
        text_features,
        gates,
        jnp.asarray(qmask, bf16),
        jnp.asarray(vmask, f32),
        *moves.operands(),
    )
    return result[0], result[1], result[2], result[3], result[4:]


def flash_backward(
    plan, query, packed_all, features, text_packed, text_features, self_out, cross_out, d_mixed, gates_q, gates_v, jobs
):
    heads = LOCAL // HEAD
    text_rows = text_packed.shape[0]
    moves = Transfers(list(jobs))
    n_in, n_out = len(moves.sent), len(moves.jobs)
    block = 256
    others = len(plan.time)
    turned = (((1,), (1,)), ((), ()))
    sunk = (((0,), (0,)), ((), ()))

    def kernel(*refs):
        (query_ref, packed_ref, feature_ref, text_ref, text_feature_ref, self_ref, cross_ref, d_ref) = refs[:8]
        gateq_ref, gatev_ref, qmask_ref, bmask_ref = refs[8:12]
        ins = refs[12 : 12 + n_in]
        dq_ref, dk_ref, dv_ref, tdk_ref, tdv_ref, sums_ref = refs[12 + n_in : 18 + n_in]
        outs = refs[18 + n_in : 18 + n_in + n_out]
        (key_ref, value_ref, near_ref, qs_ref, ds_ref, to_ref, from_ref, tto_ref, tfrom_ref, sem, send_sem, recv_sem) = refs[
            18 + n_in + n_out : 30 + n_in + n_out
        ]
        me = here()
        greet(me, moves.peers() | set(plan.time))
        if moves.jobs:
            moves.bind(me, ins, outs, refs[30 + n_in + n_out :])
            moves.start()

        def prepare(out_ref):
            def body(at, carry):
                where = pl.ds(pl.multiple_of(at * block, block), block)
                lane = lax.broadcasted_iota(jnp.int32, (block, 128), 1)
                tail = query_ref[where, 128:].astype(f32)
                out_rows = out_ref[where, :]
                d_rows = d_ref[where, :].astype(f32)
                product = d_rows * out_rows
                head_tile = jnp.where(lane < HEAD, 0.0, d_rows[:, :128])
                for h in range(heads):
                    log = -out_rows[:, 16 * h : 16 * h + 1]
                    for j in range(3):
                        piece = log.astype(bf16).astype(f32)
                        log = log - piece
                        tail = jnp.where(lane == HEAD + 2 + 3 * h + j, piece, tail)
                    delta = -jnp.sum(product * bmask_ref[h : h + 1, :].astype(f32), axis=1, keepdims=True)
                    for j in range(2):
                        piece = delta.astype(bf16).astype(f32)
                        delta = delta - piece
                        head_tile = jnp.where(lane == 2 * h + j, piece, head_tile)
                qs_ref[where, :128] = query_ref[where, :128]
                qs_ref[where, 128:] = tail.astype(bf16)
                ds_ref[where, :128] = head_tile.astype(bf16)
                ds_ref[where, 128:] = d_ref[where, 128:]
                return carry

            lax.fori_loop(0, ROWS // block, body, 0)

        def segment(rows, first, k_ref, v_ref, scale):
            k_ref[...] = jnp.zeros_like(k_ref)
            v_ref[...] = jnp.zeros_like(v_ref)

            def body(at, carry):
                where = pl.ds(pl.multiple_of(at * block, block), block)
                query_rows, d_rows = qs_ref[where, :], ds_ref[where, :]
                total = jnp.zeros((block, WIDE), f32)
                for h in range(heads):
                    own_query = query_rows * qmask_ref[h : h + 1, :]
                    own_d = d_rows * bmask_ref[h : h + 1, :]
                    keys = key_ref[:rows, :]
                    weights = jnp.exp(lax.dot_general(keys, own_query, turned, preferred_element_type=f32))
                    d_weights = lax.dot_general(value_ref[:rows, :], own_d, turned, preferred_element_type=f32)
                    d_scores = (weights * d_weights).astype(bf16)
                    v_ref[...] += jnp.dot(weights.astype(bf16), own_d, preferred_element_type=f32)
                    k_ref[...] += jnp.dot(d_scores, own_query, preferred_element_type=f32)
                    d_query = lax.dot_general(d_scores, keys, sunk, preferred_element_type=f32)
                    total += d_query * qmask_ref[h : h + 1, :].astype(f32)
                total = total * scale
                if first:
                    dq_ref[where, :] = total
                else:
                    dq_ref[where, :] += total
                return carry

            lax.fori_loop(0, ROWS // block, body, 0)

        def pack(k_ref, v_ref, rows):
            lane = lax.broadcasted_iota(jnp.int32, (rows, 128), 1)
            middle = jnp.where(lane < HEAD, k_ref[:, 128:], v_ref[:, :128])
            return k_ref[:, :128].astype(bf16), middle.astype(bf16), v_ref[:, 128:].astype(bf16)

        def bring(which):
            copy = pltpu.make_async_copy(packed_ref.at[which], near_ref, sem)
            copy.start()
            copy.wait()
            rows = pl.ds(pl.multiple_of(which * ROWS, ROWS), ROWS)
            widen(near_ref, feature_ref[rows, :], key_ref, value_ref, ROWS)

        def send(src, dst, slot, mask):
            return pltpu.make_async_remote_copy(
                src_ref=src,
                dst_ref=dst,
                send_sem=send_sem.at[slot],
                recv_sem=recv_sem.at[slot],
                device_id=flip(me, mask),
                device_id_type=MESH,
            )

        far_copies = [send(to_ref.at[i], from_ref.at[i], i, mask) for i, mask in enumerate(plan.time)]
        text_copies = [send(tto_ref, tfrom_ref.at[i], others + i, mask) for i, mask in enumerate(plan.time)]

        prepare(self_ref)
        for i, mask in enumerate(plan.time):
            bring(me[1] ^ mask[1])
            segment(ROWS, i == 0, dk_ref, dv_ref, 0.125)
            to_ref[i, :, :128], to_ref[i, :, 128:256], to_ref[i, :, 256:] = pack(dk_ref, dv_ref, ROWS)
            far_copies[i].start()
        bring(me[1])
        segment(ROWS, others == 0, dk_ref, dv_ref, 0.125)
        prepare(cross_ref)
        widen(text_ref, text_feature_ref[...], key_ref, value_ref, text_rows)
        segment(text_rows, False, tdk_ref, tdv_ref, 0.125 * gateq_ref[...])
        tdk_ref[...] = tdk_ref[...] * gateq_ref[...]
        tdv_ref[...] = tdv_ref[...] * gatev_ref[...]
        if others:
            tto_ref[:, :128], tto_ref[:, 128:256], tto_ref[:, 256:] = pack(tdk_ref, tdv_ref, text_rows)
            for copy in text_copies:
                copy.start()
        sums_ref[...] = jnp.sum(d_ref[...].astype(f32) * cross_ref[...], axis=0, keepdims=True)
        if moves.jobs:
            moves.forward()
        lane = lax.broadcasted_iota(jnp.int32, (ROWS, 128), 1)
        for i in range(others):
            far_copies[i].wait_recv()
            middle = from_ref[i, :, 128:256].astype(f32)
            dk_ref[:, :128] += from_ref[i, :, :128].astype(f32)
            dk_ref[:, 128:] += middle
            dv_ref[:, :128] += middle
            dv_ref[:, 128:] += from_ref[i, :, 256:].astype(f32)
        for i in range(others):
            text_copies[i].wait_recv()
            middle = tfrom_ref[i, :, 128:256].astype(f32)
            tdk_ref[:, :128] += tfrom_ref[i, :, :128].astype(f32)
            tdk_ref[:, 128:] += middle
            tdv_ref[:, :128] += middle
            tdv_ref[:, 128:] += tfrom_ref[i, :, 256:].astype(f32)
        for copy in far_copies + text_copies:
            copy.wait_send()
        if moves.jobs:
            moves.finish()

    qmask, _, bmask = lane_masks()
    result = pl.pallas_call(
        kernel,
        out_shape=[
            jax.ShapeDtypeStruct((ROWS, WIDE), f32),
            jax.ShapeDtypeStruct((ROWS, WIDE), f32),
            jax.ShapeDtypeStruct((ROWS, WIDE), f32),
            jax.ShapeDtypeStruct((text_rows, WIDE), f32),
            jax.ShapeDtypeStruct((text_rows, WIDE), f32),
            jax.ShapeDtypeStruct((1, WIDE), f32),
        ]
        + moves.out_shapes(),
        in_specs=[VMEM, ANY] + [VMEM] * 10 + [ANY] * n_in,
        out_specs=[VMEM] * 6 + [ANY] * n_out,
        scratch_shapes=[
            pltpu.VMEM((ROWS, WIDE), bf16),
            pltpu.VMEM((ROWS, WIDE), bf16),
            pltpu.VMEM((ROWS, 2 * LOCAL), bf16),
            pltpu.VMEM((ROWS, WIDE), bf16),
            pltpu.VMEM((ROWS, WIDE), bf16),
            pltpu.VMEM((max(others, 1), ROWS, 2 * LOCAL), bf16),
            pltpu.VMEM((max(others, 1), ROWS, 2 * LOCAL), bf16),
            pltpu.VMEM((text_rows, 2 * LOCAL), bf16),
            pltpu.VMEM((max(others, 1), text_rows, 2 * LOCAL), bf16),
            pltpu.SemaphoreType.DMA(()),
            pltpu.SemaphoreType.DMA((max(2 * others, 1),)),
            pltpu.SemaphoreType.DMA((max(2 * others, 1),)),
        ]
        + moves.scratch(),
        name="flash_backward",
        compiler_params=pltpu.CompilerParams(
            collective_id=plan.identity(), has_side_effects=True, vmem_limit_bytes=56 * 2**20
        ),
    )(
        query,
        packed_all,
        features,
        text_packed,
        text_features,
        self_out,
        cross_out,
        d_mixed,
        gates_q,
        gates_v,
        jnp.asarray(qmask, bf16),
        jnp.asarray(bmask, bf16),
        *moves.operands(),
    )
    return result[:6], result[6:]


def shards(
    latents,
    conditions,
    captions,
    row_counts,
    text_lengths,
    qkv_weight,
    text_weight,
    out_weight,
    gate_up_weight,
    down_weight,
    ada_weight,
    ada_bias,
    norm_gains,
    head_gates,
    cotangent,
):
    times = lax.axis_size("times")
    plan = Plan(times)
    sets, rows_axis = plan.sets, plan.rows
    devices = sets * M
    item, time, ring = here()
    place = (item * times + time) * M + ring
    group_place = time * M + ring
    heads = LOCAL // HEAD

    k_rows = qkv_weight.shape[0]
    t_rows = text_weight.shape[0]
    o_rows = out_weight.shape[0]
    d_rows = down_weight.shape[0]
    a_rows = ada_weight.shape[0]
    bias_n = ada_bias.shape[0]
    gain_n = norm_gains.shape[1]
    part_n = 4 * D // rows_axis

    package = jnp.concatenate(
        [norm_gains.astype(f32).reshape(-1), ada_bias.astype(f32), row_counts[0, 0].astype(f32)]
    )
    package_n = package.shape[0]
    lines = -(-package_n // 1024) * 8
    package = jnp.pad(package, (0, lines * 128 - package_n)).reshape(lines, 128)
    silu_own = jax.nn.silu(conditions[0].astype(f32)).astype(bf16)
    order, order_full = halves_order()
    mix = shuffle(order_full)
    qkv_send = qkv_weight.reshape(k_rows, 3, M, LOCAL).transpose(2, 0, 1, 3).reshape(M, k_rows, 3 * LOCAL)
    text_send = text_weight.reshape(t_rows, 2, M, LOCAL).transpose(2, 0, 1, 3).reshape(M, t_rows, 2 * LOCAL)
    gate_up_send = gate_up_weight.reshape(k_rows, 2, sets, M, d_rows).transpose(1, 3, 0, 2, 4)
    gate_up_send = gate_up_send.reshape(2, M, k_rows, sets * d_rows)
    out_forth = [(o, (o % sets) * M + o // sets) for o in range(devices)]
    out_back = [(b, a) for a, b in out_forth]
    axes = ("items", "times", "ring")
    out_shard = lax.ppermute(out_weight, axes, out_forth)
    half = M // 2

    packages, silu_both, qkv_shard, text_shard, down_time = exchange(
        plan,
        "gather_small",
        [
            plan.gather_all(package),
            plan.swap_item(silu_own),
            plan.scatter_ring(qkv_send),
            plan.scatter_ring(text_send),
            plan.gather_time(down_weight),
        ],
    )
    packages = packages.reshape(devices, lines * 128)
    gains = packages[:, : 7 * gain_n].reshape(devices, 7, gain_n).transpose(1, 0, 2).reshape(7, D)
    bias = packages[:, 7 * gain_n : 7 * gain_n + bias_n].reshape(4 * D)
    counts_all = packages[:, 7 * gain_n + bias_n : package_n].astype(jnp.int32).reshape(GROUPS, rows_axis, FRAMES)
    counts = lax.dynamic_index_in_dim(counts_all, item, 0, keepdims=False)
    silu_slice = lax.dynamic_slice_in_dim(silu_both.reshape(GROUPS * FRAMES, COND), place * a_rows, a_rows, 1)

    partial = dot(silu_slice, ada_weight).reshape(GROUPS, FRAMES, rows_axis, part_n)
    partial = partial.transpose(0, 2, 1, 3).reshape(sets, M, FRAMES, part_n)
    parts, qkv_time_a, text_a, gate_shard, out_time = exchange(
        plan,
        "scatter_modulation",
        [
            plan.scatter_all(partial),
            plan.gather_time_part(qkv_shard, 0, half),
            plan.swap_item_part(text_shard, 0, half),
            plan.scatter_ring(gate_up_send[0]),
            plan.gather_time(out_shard),
        ],
    )
    own_part = jnp.sum(parts, axis=(0, 1))
    modulation, qkv_time_b, text_b, up_shard = exchange(
        plan,
        "gather_modulation",
        [
            plan.gather_group(own_part),
            plan.gather_time_part(qkv_shard, half, half),
            plan.swap_item_part(text_shard, half, half),
            plan.scatter_ring(gate_up_send[1]),
        ],
    )
    modulation = modulation.reshape(rows_axis, FRAMES, part_n).transpose(1, 0, 2).reshape(FRAMES, 4 * D) + bias

    line = jnp.arange(TOK, dtype=jnp.int32)[None, :]
    clip = counts[:, :1]
    before = jnp.cumsum(counts, axis=0) - counts
    frame_all = (line >= clip).astype(jnp.int32)
    position_all = jnp.where(frame_all == 0, before[:, :1] + line, before[:, 1:] + line - clip)
    frame_k = frame_all.reshape(-1)
    frame_q = lax.dynamic_slice_in_dim(frame_k, time * ROWS, ROWS)
    position_q = lax.dynamic_slice_in_dim(position_all.reshape(-1), time * ROWS, ROWS).astype(f32)
    frame_own = lax.dynamic_index_in_dim(frame_all, group_place, 0, keepdims=False)
    mod_rows = jnp.where(frame_own[:, None] == 0, modulation[0][None], modulation[1][None])
    scale_attn, gate_attn = mod_rows[:, :D], mod_rows[:, D : 2 * D]
    scale_ffn, gate_ffn = mod_rows[:, 2 * D : 3 * D], mod_rows[:, 3 * D :]
    onehot = (frame_own[:, None] == jnp.arange(FRAMES, dtype=jnp.int32)[None, :]).astype(f32)
    text_line = jnp.arange(FRAMES * TEXT, dtype=jnp.int32)
    text_frame = text_line // TEXT
    text_live = text_line % TEXT < jnp.repeat(text_lengths[0], TEXT)

    inputs = latents[0]
    attn_in_float, attn_head_back = jax.vjp(attn_head, inputs, scale_attn, gains[0])
    attn_in = attn_in_float.astype(bf16)

    caption_rows = captions[0].reshape(FRAMES * TEXT, TEXT_DIM)
    width = half * t_rows
    own_captions = jnp.concatenate(
        [
            lax.dynamic_slice_in_dim(caption_rows, ((i * times + time) * 2 + h) * width, width, 1)
            for h in range(2)
            for i in range(GROUPS)
        ],
        axis=1,
    )
    text_full = jnp.concatenate(
        [text_a.reshape(GROUPS * width, 2 * LOCAL), text_b.reshape(GROUPS * width, 2 * LOCAL)], axis=0
    )
    text_partial = dot(own_captions, text_full).astype(bf16)
    attn_in_all, qkv_a, qkv_b, out_full, text_parts = exchange(
        plan,
        "gather_attn_in",
        [
            plan.gather_ring(attn_in),
            plan.swap_item(qkv_time_a),
            plan.swap_item(qkv_time_b),
            plan.swap_item(out_time),
            plan.gather_time(text_partial),
        ],
    )
    attn_in_all = attn_in_all.reshape(ROWS, D)
    qkv_full = jnp.concatenate([qkv_a, qkv_b], axis=2).reshape(D, 3 * LOCAL)
    qkv_full = dot(qkv_full, mix).astype(bf16)
    qkv_raw = dot(attn_in_all, qkv_full)
    text_raw = jnp.sum(text_parts.astype(f32), axis=0)
    q_raw, k_raw, v_raw = qkv_raw[:, :LOCAL], qkv_raw[:, LOCAL : 2 * LOCAL], qkv_raw[:, 2 * LOCAL :]
    tk_raw, tv_raw = text_raw[:, :LOCAL], text_raw[:, LOCAL:]

    squares = jnp.concatenate(
        [jnp.sum(q_raw * q_raw, axis=1), jnp.sum(k_raw * k_raw, axis=1), jnp.sum(tk_raw * tk_raw, axis=1)]
    ).reshape(-1, 128)
    (squares_all,) = exchange(plan, "gather_squares", [plan.direct_ring(squares)])
    out_full = jnp.pad(out_full.reshape(LOCAL, D), ((HEAD, 0), (0, 0)))
    inverse = lax.rsqrt(jnp.sum(squares_all, axis=0).reshape(-1) / D + epsilon)
    q_inv, k_inv, t_inv = inverse[:ROWS, None], inverse[ROWS : 2 * ROWS, None], inverse[2 * ROWS :, None]

    def own_gain(row):
        return lax.dynamic_slice_in_dim(gains[row], ring * LOCAL, LOCAL)

    def halves(vector):
        return vector.reshape(heads, HEAD // 2, 2).transpose(2, 0, 1).reshape(LOCAL)

    gain_q, gain_k, gain_t = own_gain(4), own_gain(5), own_gain(6)
    gain_q, gain_k = halves(gain_q), halves(gain_k)
    pair = jnp.arange(LOCAL // 2, dtype=jnp.int32) % (HEAD // 2)
    frequency = theta_base ** (-2.0 * pair.astype(f32) / HEAD)
    angle = position_q[:, None] * frequency[None, :]
    cos, sin = jnp.cos(angle), jnp.sin(angle)
    query = turn(q_raw * q_inv * gain_q, cos, sin).astype(bf16) * jnp.asarray(0.125, bf16)
    key = turn(k_raw * k_inv * gain_k, cos, sin).astype(bf16)
    text_key = ((tk_raw * t_inv) * gain_t).astype(bf16)
    text_key = dot(text_key, shuffle(order)).astype(bf16)
    text_value = tv_raw.astype(bf16)

    feature = jnp.arange(128, dtype=jnp.int32)[None, :]

    def key_features(apart_first, apart_second):
        ones = (feature >= HEAD + 2) & (feature < HEAD + 2 + 3 * heads)
        pick = jnp.where(feature == HEAD, apart_first[:, None], (feature == HEAD + 1) & apart_second[:, None])
        return jnp.where(pick | ones, 1.0, 0.0).astype(bf16)

    features = key_features(frame_k == 1, frame_k == 0)
    text_features = key_features(~((text_frame == 0) & text_live), ~((text_frame == 1) & text_live))
    lanes = jnp.arange(WIDE - LOCAL, dtype=jnp.int32)[None, :]
    query = jnp.concatenate(
        [query, jnp.where(lanes == frame_q[:, None], -APART, 0.0).astype(bf16)], axis=1
    )
    packed = jnp.concatenate([key, v_raw.astype(bf16)], axis=1)
    text_packed = jnp.concatenate([text_key, text_value], axis=1)
    own_gates = jnp.tanh(lax.dynamic_slice_in_dim(head_gates.astype(f32), ring * heads, heads))
    gates_v = jnp.concatenate([jnp.zeros((HEAD,), f32), jnp.repeat(own_gates, HEAD)]).reshape(1, WIDE)
    gates_q = jnp.concatenate(
        [jnp.tile(jnp.repeat(own_gates, HEAD // 2), 2), jnp.zeros((WIDE - LOCAL,), f32)]
    ).reshape(1, WIDE)

    mixed, self_out, cross_out, kv_all, (gate_time, down_full) = flash_forward(
        plan,
        query,
        packed,
        features,
        text_packed,
        text_features,
        gates_v,
        [plan.gather_time(gate_shard), plan.swap_item(down_time)],
    )
    down_full = down_full.reshape(sets * d_rows, D)
    attn_proj, (up_time, gate_full) = product_scatter(
        plan, "out_proj", [(mixed, out_full)], False, [plan.gather_time(up_shard), plan.swap_item(gate_time)]
    )
    gate_full = gate_full.reshape(D, sets * d_rows)

    state_rows, attn_tail_back = jax.vjp(attn_tail, inputs, attn_proj, gate_attn, gains[1])
    ffn_in_float, ffn_head_back = jax.vjp(attn_head, state_rows, scale_ffn, gains[2])
    ffn_in_all, up_full = exchange(
        plan, "gather_ffn_in", [plan.gather_ring(ffn_in_float.astype(bf16)), plan.swap_item(up_time)]
    )
    ffn_in_all = ffn_in_all.reshape(ROWS, D)
    up_full = up_full.reshape(D, sets * d_rows)
    gate, up = dot(ffn_in_all, gate_full), dot(ffn_in_all, up_full)

    def swiglu(gate_rows, up_rows):
        return jax.nn.silu(gate_rows) * up_rows

    activated, swiglu_back = jax.vjp(swiglu, gate, up)
    activated = activated.astype(bf16)
    down_out, _ = product_scatter(plan, "down", [(activated, down_full)], False)
    result_rows, ffn_tail_back = jax.vjp(attn_tail, state_rows, down_out, gate_ffn, gains[3])

    d_state_tail, d_down, d_gate_ffn, d_gain_four = ffn_tail_back(cotangent[0])
    (d_down_all,) = exchange(plan, "gather_d_down", [plan.gather_ring(d_down.astype(bf16))])
    d_down_all = d_down_all.reshape(ROWS, D)
    grad_down = dot(activated, d_down_all, (0, 0)).astype(bf16)
    d_activated = dot(d_down_all, down_full, (1, 1))
    d_gate, d_up = swiglu_back(d_activated)
    d_gate, d_up = d_gate.astype(bf16), d_up.astype(bf16)
    span_block = (GROUPS, times, M * k_rows, sets * d_rows)

    def add(parts):
        return jnp.sum(parts.astype(f32), axis=0)

    d_ffn_in, (down_parts,) = product_scatter(
        plan,
        "d_ffn_in",
        [(d_gate, gate_full), (d_up, up_full)],
        True,
        [plan.scatter_item(grad_down.reshape(GROUPS, times, d_rows, D))],
    )
    down_sum = add(down_parts).astype(bf16)
    grad_gate = dot(ffn_in_all, d_gate, (0, 0)).astype(bf16).reshape(span_block)
    grad_up = dot(ffn_in_all, d_up, (0, 0)).astype(bf16).reshape(span_block)
    d_state_head, d_scale_ffn, d_gain_three = ffn_head_back(d_ffn_in)
    d_state = d_state_tail + d_state_head
    d_inputs_tail, d_proj, d_gate_attn, d_gain_two = attn_tail_back(d_state)
    d_proj_all, gate_parts, down_parts = exchange(
        plan,
        "gather_d_proj",
        [plan.gather_ring(d_proj.astype(bf16)), plan.scatter_item(grad_gate), plan.scatter_time(down_sum)],
    )
    d_proj_all = d_proj_all.reshape(ROWS, D)
    down_grad = add(down_parts)
    gate_sum = add(gate_parts).astype(bf16)
    grad_out = dot(mixed, d_proj_all, (0, 0))[HEAD:].astype(bf16)
    d_mixed = dot(d_proj_all, out_full, (1, 1)).astype(bf16)
    (dq, dk, dv, tdk, tdv, gate_sums), (gate_parts, up_parts, out_parts) = flash_backward(
        plan,
        query,
        kv_all,
        features,
        text_packed,
        text_features,
        self_out,
        cross_out,
        d_mixed,
        gates_q,
        gates_v,
        [
            plan.scatter_time(gate_sum),
            plan.scatter_item(grad_up),
            plan.scatter_item(grad_out.reshape(GROUPS, times, o_rows, D)),
        ],
    )
    gate_sum = add(gate_parts).astype(bf16).reshape(M, k_rows, sets * d_rows)
    up_sum = add(up_parts).astype(bf16)
    out_sum = add(out_parts).astype(bf16)
    gate_sums = jnp.sum(gate_sums[0, HEAD:].reshape(heads, HEAD), axis=1)
    dq, dk, dv, tdk, tdv = dq[:, :LOCAL], dk[:, :LOCAL], dv[:, HEAD:], tdk[:, :LOCAL], tdv[:, HEAD:]

    d_query = turn(dq, cos, -sin)
    d_key = turn(dk, cos, -sin)
    d_tk = dot(tdk.astype(bf16), shuffle(order), (1, 1))
    qn, kn, tn = q_raw * q_inv, k_raw * k_inv, tk_raw * t_inv
    d_gain_q, d_gain_k, d_gain_t = jnp.sum(d_query * qn, axis=0), jnp.sum(d_key * kn, axis=0), jnp.sum(d_tk * tn, axis=0)
    d_qn, d_kn, d_tn = d_query * gain_q, d_key * gain_k, d_tk * gain_t
    sums = jnp.concatenate(
        [jnp.sum(d_qn * qn, axis=1), jnp.sum(d_kn * kn, axis=1), jnp.sum(d_tn * tn, axis=1)]
    ).reshape(-1, 128)
    sums_all, out_parts = exchange(plan, "gather_sums", [plan.direct_ring(sums), plan.scatter_time(out_sum)])
    out_grad = lax.ppermute(add(out_parts), axes, out_back)
    means = jnp.sum(sums_all, axis=0).reshape(-1) / D
    q_mean, k_mean, t_mean = means[:ROWS, None], means[ROWS : 2 * ROWS, None], means[2 * ROWS :, None]
    d_qkv = jnp.concatenate(
        [(d_qn - qn * q_mean) * q_inv, (d_kn - kn * k_mean) * k_inv, dv], axis=1
    ).astype(bf16)
    d_text = jnp.concatenate([(d_tn - tn * t_mean) * t_inv, tdv], axis=1).astype(bf16)
    grad_qkv = dot(dot(attn_in_all, d_qkv, (0, 0)).astype(bf16), mix, (1, 1)).astype(bf16)
    grad_text = dot(own_captions, d_text, (0, 0)).astype(bf16)
    grad_text = grad_text.reshape(2, GROUPS, width, 2 * LOCAL).transpose(1, 0, 2, 3)
    grad_qkv = grad_qkv.reshape(GROUPS, times, 2, half * k_rows, 3 * LOCAL)
    d_attn_in, (qkv_parts_a, qkv_parts_b, text_parts, up_parts) = product_scatter(
        plan,
        "d_attn_in",
        [(d_qkv, qkv_full)],
        True,
        [
            plan.scatter_item(grad_qkv[:, :, 0]),
            plan.scatter_time(grad_qkv[:, :, 1].transpose(1, 0, 2, 3)),
            plan.scatter_item(grad_text),
            plan.scatter_time(up_sum),
        ],
    )
    qkv_sum_a = add(qkv_parts_a).astype(bf16)
    qkv_sum_b = add(qkv_parts_b).astype(bf16)
    text_sum = add(text_parts).astype(bf16).reshape(M, t_rows, 2 * LOCAL)
    up_sum = add(up_parts).astype(bf16).reshape(M, k_rows, sets * d_rows)
    d_inputs_head, d_scale_attn, d_gain_one = attn_head_back(d_attn_in)
    grad_latent = d_inputs_tail + d_inputs_head

    d_mod_rows = jnp.concatenate([d_scale_attn, d_gate_attn, d_scale_ffn, d_gate_ffn], axis=1)
    d_mod = jnp.einsum("tf,td->fd", onehot, d_mod_rows, precision=highest)
    d_mod = d_mod.reshape(FRAMES, rows_axis, part_n).transpose(1, 0, 2).reshape(times, M, FRAMES, part_n)

    def spread(vector):
        return lax.dynamic_update_slice_in_dim(jnp.zeros((D,), f32), vector, ring * LOCAL, 0)

    def unhalve(vector):
        return vector.reshape(2, heads, HEAD // 2).transpose(1, 2, 0).reshape(LOCAL)

    first = (time == 0).astype(f32)
    d_gains = jnp.stack(
        [
            d_gain_one,
            d_gain_two,
            d_gain_three,
            d_gain_four,
            spread(unhalve(d_gain_q)),
            spread(unhalve(d_gain_k)),
            spread(d_gain_t * first),
            jnp.zeros((D,), f32),
        ]
    )
    d_gains = d_gains.reshape(8, devices, gain_n).transpose(1, 0, 2).reshape(sets, M, 8, gain_n)
    gate_row = lax.dynamic_update_slice_in_dim(
        jnp.zeros((HEADS,), f32), gate_sums * (1.0 - own_gates * own_gates), ring * heads, 0
    )
    gate_row = jnp.pad(gate_row, (0, 128 - HEADS)).reshape(1, 128)
    d_mod_parts, d_gain_parts, gate_rows, qkv_parts_a, qkv_parts_b, text_pieces, gate_pieces, up_pieces = exchange(
        plan,
        "scatter_grads",
        [
            plan.scatter_group(d_mod),
            plan.scatter_all(d_gains),
            plan.gather_all(gate_row),
            plan.scatter_time(qkv_sum_a),
            plan.scatter_item(qkv_sum_b),
            plan.scatter_ring(text_sum),
            plan.scatter_ring(gate_sum),
            plan.scatter_ring(up_sum),
        ],
    )
    gains_grad = jnp.sum(d_gain_parts, axis=(0, 1))[:7]
    gates_grad = jnp.sum(gate_rows, axis=(0, 1, 2))[:HEADS]
    text_grad = text_pieces.reshape(M, t_rows, 2, LOCAL).transpose(1, 2, 0, 3).reshape(t_rows, 2 * D).astype(f32)
    gate_up_grad = jnp.stack([gate_pieces, up_pieces]).reshape(2, M, k_rows, sets, d_rows)
    gate_up_grad = gate_up_grad.transpose(2, 0, 3, 1, 4).reshape(k_rows, 2 * FF).astype(f32)
    qkv_sum = jnp.concatenate([add(qkv_parts_a), add(qkv_parts_b)], axis=0).astype(bf16)
    d_mod_all, qkv_pieces = exchange(
        plan,
        "gather_d_mod",
        [
            plan.gather_all(jnp.sum(d_mod_parts, axis=(0, 1))),
            plan.scatter_ring(qkv_sum.reshape(M, k_rows, 3 * LOCAL)),
        ],
    )
    qkv_grad = qkv_pieces.reshape(M, k_rows, 3, LOCAL).transpose(1, 2, 0, 3).reshape(k_rows, 3 * D).astype(f32)
    d_mod_all = (
        d_mod_all.reshape(GROUPS, rows_axis, FRAMES, part_n).transpose(0, 2, 1, 3).reshape(GROUPS * FRAMES, 4 * D)
    )
    ada_grad = jnp.einsum("fc,fd->cd", silu_slice.astype(f32), d_mod_all, precision=highest)
    bias_grad = lax.dynamic_slice_in_dim(jnp.sum(d_mod_all, axis=0), place * bias_n, bias_n)
    return (
        result_rows[None],
        grad_latent[None],
        qkv_grad,
        text_grad,
        out_grad,
        gate_up_grad,
        down_grad,
        ada_grad,
        bias_grad,
        gains_grad,
        gates_grad,
    )


def solution(mesh):
    items, rows = mesh.shape["items"], mesh.shape["rows"]
    fine = Mesh(mesh.devices.reshape(items, rows // M, M), ("items", "times", "ring"))
    whole = ("items", "times", "ring")
    rows_of = ("times", "ring")
    return jax.shard_map(
        shards,
        mesh=fine,
        in_specs=(
            P("items", rows_of, None),
            P("items", None, None),
            P("items", None, None, None),
            P("items", rows_of, None),
            P("items", None),
            P(whole, None),
            P(whole, None),
            P(whole, None),
            P(whole, None),
            P(whole, None),
            P(whole, None),
            P(whole),
            P(None, whole),
            P(),
            P("items", rows_of, None),
        ),
        out_specs=(
            P("items", rows_of, None),
            P("items", rows_of, None),
            P(whole, None),
            P(whole, None),
            P(whole, None),
            P(whole, None),
            P(whole, None),
            P(whole, None),
            P(whole),
            P(None, whole),
            P(),
        ),
        check_vma=False,
    )
```

time: 3240 us -> 727 us (0.22)
  waiting for transfers between devices: 2500 us -> 0.01 us
  Pallas kernels: 0 us -> 509 us
  matrix products: 353 us -> 42.2 us
  blocking collectives: 142 us -> 0 us
    reduce_scatter x9 -> x0, waiting for transfers between devices: 1950 us -> none  [the longest x1 439 us: shards(): lax.psum_scatter(grad_text, ('items', 'rows'), scatter_dimension=0, tiled...]
    all_gather x8 -> x0, waiting for transfers between devices: 547 us -> none  [the longest x1 147 us: shards(): lax.all_gather(gate_up_weight, ('items', 'rows'), axis=0, tiled=True)]
    pallas_call x0 -> x17, Pallas kernels: none -> 509 us  [the longest x11 245 us: exchange(): pl.pallas_call(kernel, out_shape=moves.out_shapes(), in_specs=[ANY] * n_i...]
    dot_general x30 -> x18, matrix products: 353 us -> 42.2 us  [the longest x16 37 us: dot(): lax.dot_general(a, b, (((dims[0],), (dims[1],)), ((), ())), preferred_ele...]
    unnamed x2 -> x0, blocking collectives: 82.9 us -> none
    all_gather x2 -> x0, blocking collectives: 59 us -> none  [the longest x1 37.5 us: shards(): lax.all_gather(norm_gains, ('items', 'rows'), axis=1, tiled=True)]
    reshape x16 -> x18, local copies, waits for them, and re-layouts: 52.3 us -> 6.5 us  [the longest x3 2.39 us: shards(): qkv_weight.reshape(k_rows, 3, M, LOCAL).transpose(2, 0, 1, 3)]
  transfers between devices with their start and end apart: 18 -> 2, of which waited for: 13 -> 0; matrix products, arithmetic and copies ran while one was open for 13% -> 8% of each run, Pallas kernels for 0% -> 7%
where the time goes in v1:
time: 727 us; the launch traced here: 718 us
  Pallas kernels  509 us (70%)
  local copies, waits for them, and re-layouts  81.4 us (11%)
  other arithmetic  75.9 us (10%)
  matrix products  42.2 us (6%)
    pallas_call x11, Pallas kernels, exchange(): pl.pallas_call(kernel, out_shape=moves.out_shapes(), in_specs=[ANY] * n_i...  245 us
    pallas_call x4, Pallas kernels, product_scatter(): pl.pallas_call(kernel, out_shape=[jax.ShapeDtypeStruct((TOK, D), f32)] +...  130 us
    pallas_call x1, Pallas kernels, flash_backward(): pl.pallas_call(kernel, out_shape=[jax.ShapeDtypeStruct((ROWS, WIDE), f32)...  75.8 us
    pallas_call x1, Pallas kernels, flash_forward(): pl.pallas_call(kernel, out_shape=[jax.ShapeDtypeStruct((ROWS, WIDE), bf16...  58.3 us
    dot_general x16, matrix products, dot(): lax.dot_general(a, b, (((dims[0],), (dims[1],)), ((), ())), preferred_ele...  37 us
    unnamed x252, local copies, waits for them, and re-layouts  30.5 us
    reduce_sum x13, other arithmetic, add(): return jnp.sum(parts.astype(f32), axis=0)  15.3 us
  transfers between devices with their start and end apart: 2, of which 0 were waited for; matrix products, arithmetic and copies ran while one was open for 8% of the time, Pallas kernels for 7%

profile of v1, /device:TPU:0, one launch (start us, length us, event | category | flops | bytes accessed | tf_op | source)
XLA Modules:
  0.0 717.7 jit_solution(7682197871000275529)
XLA Ops:
  9.6 34.8 %gather_small.1 = (f32[4,8,8,128]{3,2,1,0:T(8,128)S(1)}, bf16[2,2,1024]{2,1,0:T(2,128)(2,1)S(1)}, bf16[8,48,576]{2,1,0:T(8,128)(2,1)S(1)}, bf16[8,128,384]{2,1,0:T(8,128)(2,1)S(1)}, bf16[2,128,1536]{2,1,0:T(8,128)(2,1)S(1)}) custom-call(f32[8,128]{1,0:T(8,128)S(1)} %fusion.78.refs_0_, bf16[2,1024]{1,0:T(2,128)(2,1)S(1)} %fusion.74.refs_1_, ...), custom_call_target="tpu_custom_call" | custom-call | tf_op jit(solution)/shard_map/gather_small/pallas_call | solution.py:327
  71.9 25.3 %scatter_modulation.1 = (f32[4,8,2,384]{3,2,1,0:T(2,128)S(1)}, bf16[2,4,48,576]{3,2,1,0:T(8,128)(2,1)S(1)}, bf16[2,4,128,384]{3,2,1,0:T(8,128)(2,1)S(1)}, bf16[8...) custom-call(f32[4,8,2,384]{3,2,1,0:T(2,128)S(1)} %bitcast.238, bf16[8,48,576]{2,1,0:T(8,128)(2,1)S(1)} %get-tuple-element.74.refs_1_, ...), custom_call_target="tpu_custom_call" | custom-call | tf_op jit(solution)/shard_map/scatter_modulation/pallas_call | solution.py:327
  98.9 17.1 %gather_modulation.1 = (f32[2,8,2,384]{3,2,1,0:T(2,128)S(1)}, bf16[2,4,48,576]{3,2,1,0:T(8,128)(2,1)S(1)}, bf16[2,4,128,384]{3,2,1,0:T(8,128)(2,1)S(1)}, bf16[8,48,512]{2,1,0:T(8,128)(2,1)S(1)}) custom-call(f32[2,384]{1,0:T(2,128)S(1)} %reduce_sum.448.refs_0_, bf16[8,48,576]{2,1,0:T(8,128)(2,1)S(1)} %get-tuple-element.74.refs_1_, ...), custom_call_target="tpu_custom_call" | custom-call | tf_op jit(solution)/shard_map/gather_modulation/pallas_call | solution.py:327
  120.8 30.8 %gather_attn_in.1 = (bf16[8,128,1536]{2,1,0:T(8,128)(2,1)S(1)}, bf16[2,2,4,48,576]{4,3,2,1,0:T(8,128)(2,1)S(1)}, bf16[2,2,4,48,576]{4,3,2,1,0:T(8,128)(2,1)S(1)}...) custom-call(bf16[128,1536]{1,0:T(8,128)(2,1)S(1)} %multiply_convert_fusion.5.refs_0_, ...), custom_call_target="tpu_custom_call" | custom-call | tf_op jit(solution)/shard_map/gather_attn_in/pallas_call | solution.py:327
  163.5 5.0 gather_squares.1
  180.5 58.3 %flash_forward.1 = (bf16[1024,256]{1,0:T(8,128)(2,1)}, f32[1024,256]{1,0:T(8,128)}, f32[1024,256]{1,0:T(8,128)}, bf16[2,1024,384]{2,1,0:T(8,128)(2,1)}, bf16[2,8...) custom-call(bf16[1024,256]{1,0:T(8,128)(2,1)} %pad_maximum_fusion.6.refs_0_, ...), custom_call_target="tpu_custom_call" | custom-call | tf_op jit(solution)/shard_map/flash_forward/pallas_call | solution.py:588
  241.0 31.2 %out_proj.1 = (f32[128,1536]{1,0:T(8,128)S(1)}, bf16[2,8,48,512]{3,2,1,0:T(8,128)(2,1)S(1)}, bf16[2,2,8,48,512]{4,3,2,1,0:T(8,128)(2,1)S(1)}) custom-call(bf16[1024,256]{1,0:T(8,128)(2,1)S(1)} %copy-done.12, bf16[256,1536]{1,0:T(8,128)(2,1)S(1)} %pad.15.refs_1_, bf16[8,48,512]{2,1,0:T(8,128)(2,1)S(1)} %get-tuple-element.91.refs_2_, ...), custom_call_target="tpu_custom_call" | custom-call | tf_op jit(solution)/shard_map/out_proj/pallas_call | solution.py:416
  275.2 22.0 %gather_ffn_in.1 = (bf16[8,128,1536]{2,1,0:T(8,128)(2,1)S(1)}, bf16[2,2,8,48,512]{4,3,2,1,0:T(8,128)(2,1)S(1)}) custom-call(bf16[128,1536]{1,0:T(8,128)(2,1)S(1)} %multiply_convert_fusion.4.refs_0_, bf16[2,8,48,512]{3,2,1,0:T(8,128)(2,1)S(1)} %get-tuple-element.94.refs_1_), custom_call_target="tpu_custom_call" | custom-call | tf_op jit(solution)/shard_map/gather_ffn_in/pallas_call | solution.py:327
  299.4 3.2 multiply_convert_fusion.1
  302.6 23.2 %down.1 = f32[128,1536]{1,0:T(8,128)S(1)} custom-call(bf16[1024,512]{1,0:T(8,128)(2,1)S(1)} %get-tuple-element.233.refs_0_, bf16[512,1536]{1,0:T(8,128)(2,1)S(1)} %bitcast.224), custom_call_target="tpu_custom_call" | custom-call | tf_op jit(solution)/shard_map/down/pallas_call | solution.py:416
  326.0 3.1 multiply_reduce_fusion.6
  331.4 21.9 %gather_d_down.1 = bf16[8,128,1536]{2,1,0:T(8,128)(2,1)S(1)} custom-call(bf16[128,1536]{1,0:T(8,128)(2,1)S(1)} %get-tuple-element.202.refs_0_), custom_call_target="tpu_custom_call" | custom-call | tf_op jit(solution)/shard_map/gather_d_down/pallas_call | solution.py:327
  364.9 28.7 %d_ffn_in.1 = (f32[128,1536]{1,0:T(8,128)S(1)}, bf16[2,2,128,1536]{3,2,1,0:T(8,128)(2,1)S(1)}) custom-call(bf16[1024,512]{1,0:T(8,128)(2,1)S(1)} %get-tuple-element.197.refs_0_, bf16[1536,512]{1,0:T(8,128)(2,1)S(1)} %bitcast.230, bf16[1024,512]{1,0:T(8,128)(2,1)S(1)} %get-tuple-element.196.refs_2_, bf16[1536,512]{1,0:T(8,128)(2,1)} %bitcast.232, ...), custom_call_target="tpu_custom_call" | custom-call | tf_op jit(solution)/shard_map/d_ffn_in/pallas_call | solution.py:416
  404.7 30.4 %gather_d_proj.1 = (bf16[8,128,1536]{2,1,0:T(8,128)(2,1)S(1)}, bf16[2,2,384,512]{3,2,1,0:T(8,128)(2,1)S(1)}, bf16[2,128,1536]{2,1,0:T(8,128)(2,1)S(1)}) custom-call(bf16[128,1536]{1,0:T(8,128)(2,1)S(1)} %fusion.21.refs_0_, bf16[2,2,384,512]{3,2,1,0:T(8,128)(2,1)S(1)} %bitcast.226, bf16[2,128,1536]{2,1,0:T(8,128)(2,1)S(1)} %reduce_sum.461.refs_2_), custom_call_target="tpu_custom_call" | custom-call | tf_op jit(solution)/shard_map/gather_d_proj/pallas_call | solution.py:327
  440.2 75.8 %flash_backward.1 = (f32[1024,256]{1,0:T(8,128)}, f32[1024,256]{1,0:T(8,128)}, f32[1024,256]{1,0:T(8,128)}, f32[512,256]{1,0:T(8,128)}, f32[512,256]{1,0:T(8,128...) custom-call(bf16[1024,256]{1,0:T(8,128)(2,1)} %pad_maximum_fusion.6., ...), custom_call_target="tpu_custom_call" | custom-call | tf_op jit(solution)/shard_map/flash_backward/pallas_call | solution.py:773
  520.1 3.9 fusion.51
  526.8 10.5 %gather_sums.1 = (f32[8,20,128]{2,1,0:T(8,128)S(1)}, bf16[2,48,1536]{2,1,0:T(8,128)(2,1)S(1)}) custom-call(f32[20,128]{1,0:T(8,128)S(1)} %maximum_bitcast_fusion.1.refs_0_, bf16[2,48,1536]{2,1,0:T(8,128)(2,1)S(1)} %reduce_sum.466.refs_1_), custom_call_target="tpu_custom_call" | custom-call | tf_op jit(solution)/shard_map/gather_sums/pallas_call | solution.py:327
  543.3 6.0 convolution_convert_fusion.2
  549.3 3.9 copy.130
  561.8 46.9 %d_attn_in.1 = (f32[128,1536]{1,0:T(8,128)S(1)}, bf16[2,2,192,576]{3,2,1,0:T(8,128)(2,1)S(1)}, bf16[2,2,192,576]{3,2,1,0:T(8,128)(2,1)S(1)}, bf16[2,2,512,384]{3,2,1,0:T(8,128)(2,1)}, bf16[2,384,512]{2,1,0:T(8,128)(2,1)S(1)}) custom-call(bf16[1024,576]{1,0:T(8,128)(2,1)} %pad_maximum_fusion.2.refs_0_, bf16[1536,576]{1,0:T(8,128)(2,1)} %copy-done.54, ...), custom_call_target="tpu_custom_call" | custom-call | tf_op jit(solution)/shard_map/d_attn_in/pallas_call | solution.py:416
  629.4 32.0 %scatter_grads.1 = (f32[2,8,2,384]{3,2,1,0:T(2,128)S(1)}, f32[4,8,8,48]{3,2,1,0:T(8,128)S(1)}, f32[4,8,1,128]{3,2,1,0:T(1,128)S(1)}, bf16[2,192,576]{2,1,0:T(8,1...) custom-call(f32[2,8,2,384]{3,2,1,0:T(2,128)S(1)} %bitcast.240, ...), custom_call_target="tpu_custom_call" | custom-call | tf_op jit(solution)/shard_map/scatter_grads/pallas_call | solution.py:327
  669.9 4.0 collective-permute-start.1
  676.6 15.6 %gather_d_mod.1 = (f32[4,8,2,384]{3,2,1,0:T(2,128)S(1)}, bf16[8,48,576]{2,1,0:T(8,128)(2,1)S(1)}) custom-call(f32[2,384]{1,0:T(2,128)S(1)} %reduce_sum.483.refs_0_, bf16[8,48,576]{2,1,0:T(8,128)(2,1)S(1)} %bitcast.223), custom_call_target="tpu_custom_call" | custom-call | tf_op jit(solution)/shard_map/gather_d_mod/pallas_call | solution.py:327
  695.8 3.1 copy.138
  (465 shorter events, 178.0 us)
Async XLA Ops:
  0.6 51.1 %copy-start = (bf16[32,6144]{1,0:T(8,128)(2,1)S(1)}, bf16[32,6144]{1,0:T(8,128)(2,1)}, u32[]{:S(2)}) copy-start(bf16[32,6144]{1,0:T(8,128)(2,1)} %param.32) | copy-start | bytes 1179652
  0.7 71.2 %collective-permute-start = (bf16[48,1536]{1,0:T(8,128)(2,1)}, bf16[48,1536]{1,0:T(8,128)(2,1)S(1)}, u32[]{:S(2)}, u32[]{:S(2)}) collective-permute-start(bf16[48,1536]{1,0:T(8,128)(2,1)} %param.29), channel_id=1, source_target_pairs={{0,0},{1,8},{2,16},{3,24},{4,1},{5,9},{6,17},{7,25},{8,2},{9,10},{... | collective-permute-start | bytes 442376 | tf_op jit(solution)/shard_map/ppermute | solution.py:874
  55.0 9.0 %copy-start.90 = (pred[2048]{0:T(1024)(128)(4,1)S(1)}, pred[2048]{0:T(1024)(128)(4,1)}, u32[]{:S(2)}) copy-start(pred[2048]{0:T(1024)(128)(4,1)} %get-tuple-element.231) | copy-start | bytes 6148
  55.0 9.0 %copy-start.92 = (pred[2048]{0:T(1024)(128)(4,1)S(1)}, pred[2048]{0:T(1024)(128)(4,1)}, u32[]{:S(2)}) copy-start(pred[2048]{0:T(1024)(128)(4,1)} %get-tuple-element.230) | copy-start | bytes 6148
  55.0 9.0 %copy-start.100 = (pred[128]{0:T(512)(128)(4,1)S(1)}, pred[128]{0:T(512)(128)(4,1)}, u32[]{:S(2)}) copy-start(pred[128]{0:T(512)(128)(4,1)} %get-tuple-element.242) | copy-start | bytes 388
  55.0 9.0 %copy-start.101 = (pred[128]{0:T(512)(128)(4,1)S(1)}, pred[128]{0:T(512)(128)(4,1)}, u32[]{:S(2)}) copy-start(pred[128]{0:T(512)(128)(4,1)} %get-tuple-element.243) | copy-start | bytes 388
  55.1 13.3 %copy-start.82 = (s32[2048]{0:T(1024)S(1)}, s32[2048]{0:T(1024)}, u32[]{:S(2)}) copy-start(s32[2048]{0:T(1024)} %get-tuple-element.241) | copy-start | bytes 24580
  71.9 44.2 %copy-start.111 = (pred[128]{0:T(512)(128)(4,1)S(1)}, pred[128]{0:T(512)(128)(4,1)}, u32[]{:S(2)}) copy-start(pred[128]{0:T(512)(128)(4,1)} %broadcast_compare_fusion.2) | copy-start | bytes 388
  161.2 12.5 %copy-start.36 = (f32[1024,192]{1,0:T(8,128)}, f32[1024,192]{1,0:T(8,128)S(1)}, u32[]{:S(2)}) copy-start(f32[1024,192]{1,0:T(8,128)S(1)} %copy.148) | copy-start | bytes 2359300
  163.1 10.9 %copy-start.34 = (f32[1024,192]{1,0:T(8,128)}, f32[1024,192]{1,0:T(8,128)S(1)}, u32[]{:S(2)}) copy-start(f32[1024,192]{1,0:T(8,128)S(1)} %copy.147) | copy-start | bytes 2359300
  163.1 10.6 %copy-start.83 = (f32[192]{0:T(256)S(1)}, f32[192]{0:T(256)}, u32[]{:S(2)}) copy-start(f32[192]{0:T(256)} %mul.631) | copy-start | bytes 2308
  180.5 91.8 %copy-start.40 = (f32[1,128,1536]{2,1,0:T(8,128)S(1)}, f32[1,128,1536]{2,1,0:T(8,128)}, u32[]{:S(2)}) copy-start(f32[1,128,1536]{2,1,0:T(8,128)} %param.22) | copy-start | bytes 2359300
  302.6 23.4 %copy-start.47 = (f32[1,128,1536]{2,1,0:T(8,128)S(1)}, f32[1,128,1536]{2,1,0:T(8,128)}, u32[]{:S(2)}) copy-start(f32[1,128,1536]{2,1,0:T(8,128)} %param.36) | copy-start | bytes 2359300
  440.2 75.9 %copy-start.43 = (f32[512,384]{1,0:T(8,128)S(1)}, f32[512,384]{1,0:T(8,128)}, u32[]{:S(2)}) copy-start(f32[512,384]{1,0:T(8,128)} %copy-done.42) | copy-start | bytes 2359300
  440.2 75.9 %copy-start.77 = (f32[512]{0:T(512)S(1)}, f32[512]{0:T(512)}, u32[]{:S(2)}) copy-start(f32[512]{0:T(512)} %copy-done.76) | copy-start | bytes 6148
  440.2 75.9 %copy-start.88 = (f32[192]{0:T(256)S(1)}, f32[192]{0:T(256)}, u32[]{:S(2)}) copy-start(f32[192]{0:T(256)} %dynamic_slice.55) | copy-start | bytes 2308
  440.2 75.9 %copy-start.98 = (s32[192]{0:T(256)S(1)}, s32[192]{0:T(256)}, u32[]{:S(2)}) copy-start(s32[192]{0:T(256)} %constant.181.clone) | copy-start | bytes 2308
  524.1 14.0 %copy-start.66 = (f32[1024,256]{1,0:T(8,128)S(1)}, f32[1024,256]{1,0:T(8,128)}, u32[]{:S(2)}) copy-start(f32[1024,256]{1,0:T(8,128)} %get-tuple-element.111) | copy-start | bytes 3145732
  561.8 46.9 %copy-start.41 = (f32[1,128,1536]{2,1,0:T(8,128)S(1)}, f32[1,128,1536]{2,1,0:T(8,128)}, u32[]{:S(2)}) copy-start(f32[1,128,1536]{2,1,0:T(8,128)} %param.22) | copy-start | bytes 2359300
  561.8 46.9 %copy-start.94 = (f32[128]{0:T(128)S(1)}, f32[128]{0:T(128)}, u32[]{:S(2)}) copy-start(f32[128]{0:T(128)} %fusion.99) | copy-start | bytes 1540
  665.7 9.8 %copy-start.8 = (bf16[2,128,1536]{2,1,0:T(8,128)(2,1)S(1)}, bf16[2,128,1536]{2,1,0:T(8,128)(2,1)}, u32[]{:S(2)}) copy-start(bf16[2,128,1536]{2,1,0:T(8,128)(2,1)} %copy-done.7) | copy-start | bytes 2359300
  665.7 9.0 %copy-start.17 = (bf16[8,48,512]{2,1,0:T(8,128)(2,1)S(1)}, bf16[8,48,512]{2,1,0:T(8,128)(2,1)}, u32[]{:S(2)}) copy-start(bf16[8,48,512]{2,1,0:T(8,128)(2,1)} %copy-done.16) | copy-start | bytes 1179652
  667.0 9.6 %copy-start.26 = (f32[2,8,2,384]{3,2,1,0:T(2,128)S(1)}, f32[2,8,2,384]{3,2,1,0:T(2,128)}, u32[]{:S(2)}) copy-start(f32[2,8,2,384]{3,2,1,0:T(2,128)} %copy-done.25) | copy-start | bytes 147460
  669.9 45.7 %collective-permute-start.1 = (f32[48,1536]{1,0:T(8,128)}, f32[48,1536]{1,0:T(8,128)}, u32[]{:S(2)}, u32[]{:S(2)}) collective-permute-start(f32[48,1536]{1,0:T(8,128)} %convert_reduce_fusion.2), channel_id=1, source_target_pairs={{0,0},{8,1},{16,2},{24,3},{1,4},{9,5},{17,6},{25,7},{2,8},{10,9},{... | collective-permute-start | bytes 884744 | tf_op jit(solution)/shard_map/ppermute | solution.py:1124
  (97 other events, 302.4 us)

commit v2 on v1

--- a/solution.py
+++ b/solution.py
@@ -38,8 +38,9 @@
 
 
 class Job:
-    def __init__(self, x, shape, masks, src, dst, pass_on=(), by=None, source=None):
+    def __init__(self, x, shape, masks, src, dst, pass_on=(), by=None, source=None, piece=None):
         self.x, self.shape, self.masks, self.src, self.dst = x, shape, masks, src, dst
+        self.piece = piece
         self.pass_on, self.by, self.source = tuple(pass_on), by, source
         if source is not None:
             self.x = None
@@ -49,7 +50,7 @@
         return len(self.masks) + len(self.pass_on)
 
     def block(self):
-        return self.shape[len(self.dst((0, 0, 0))) :]
+        return self.piece or self.shape[len(self.dst((0, 0, 0))) :]
 
     def peers(self):
         return set(self.masks) | ({self.by} if self.pass_on else set())
@@ -237,6 +238,40 @@
 
     def gather_time(self, x):
         return Job(x, (self.times,) + x.shape, self.time, lambda dest: None, lambda sender: (sender[1],))
+
+    def stack_time(self, x):
+        n = x.shape[0]
+        return Job(
+            x,
+            (self.times * n,) + x.shape[1:],
+            self.time,
+            lambda dest: None,
+            lambda sender: (pl.ds(pl.multiple_of(sender[1] * n, n), n),),
+            piece=x.shape,
+        )
+
+    def stack_item(self, x, source=None):
+        shape = x.shape if source is None else source.shape
+        n = shape[0]
+        return Job(
+            x,
+            (GROUPS * n,) + shape[1:],
+            [self.item],
+            lambda dest: None,
+            lambda sender: (pl.ds(pl.multiple_of(sender[0] * n, n), n),),
+            source=source,
+            piece=shape,
+        )
+
+    def split_time(self, x):
+        n = x.shape[0] // self.times
+        return Job(
+            x,
+            (self.times, n) + x.shape[1:],
+            self.time,
+            lambda dest: (pl.ds(pl.multiple_of(dest[1] * n, n), n),),
+            lambda sender: (sender[1],),
+        )
 
     def gather_time_part(self, x, start, count):
         return Job(
@@ -436,16 +471,317 @@
     return result[0], result[1:]
 
 
+def feed_forward(
+    plan, mixed, out_full, latents, cotangent, modulation, gains, first_rows, gate_time, up_shard, down_full, d_rows
+):
+    width = down_full.shape[0]
+    deep = out_full.shape[0]
+    up_job = plan.stack_time(up_shard)
+    moves = Transfers([plan.stack_item(gate_time), up_job, plan.stack_item(up_shard, up_job)])
+    n_in, n_out = len(moves.sent), len(moves.jobs)
+    turned = (((1,), (1,)), ((), ()))
+    sunk = (((0,), (0,)), ((), ()))
+    plain = (((1,), (0,)), ((), ()))
+    chip_rows = 2 * TOK
+    part_rows = D // GROUPS
+    others = len(plan.time)
+    slab = plan.times * d_rows
+
+    def kernel(*refs):
+        (mixed_ref, out_w, latent_ref, cot_ref, mod_ref, gain_ref, first_ref, down_w) = refs[:8]
+        ins = refs[8 : 8 + n_in]
+        refs = refs[8 + n_in :]
+        (result_ref, d_state_ref, d_mixed_ref, grad_out_ref, gate_sum_ref, up_sum_ref, down_grad_ref, sums_ref) = refs[:8]
+        outs = refs[8 : 8 + n_out]
+        refs = refs[8 + n_out :]
+        (gate_w, up_w, ffn_all, down_all, proj_all, gate_ref, up_ref, act_ref, d_gate_ref, d_up_ref) = refs[:10]
+        (grad_gate, grad_up, grad_down, from_gate, from_up, from_down, down_sum, from_time) = refs[10:18]
+        (to_mate, from_mate, to_chip, from_chip, part, proj_ref, state_ref, own_ref, send_sem, recv_sem, local_sem) = refs[
+            18:29
+        ]
+        me = here()
+        item, time, ring = me
+        core, chip = ring % 2, ring // 2
+        greet(me, moves.peers() | {plan.mate, plan.item} | set(plan.chips) | set(plan.time))
+        moves.bind(me, ins, outs, refs[29:])
+        moves.start()
+        used = [0]
+
+        def link(src, dst, mask):
+            slot = used[0]
+            used[0] += 1
+            return pltpu.make_async_remote_copy(
+                src_ref=src,
+                dst_ref=dst,
+                send_sem=send_sem.at[slot],
+                recv_sem=recv_sem.at[slot],
+                device_id=flip(me, mask),
+                device_id_type=MESH,
+            )
+
+        def rows_at(index, count):
+            return pl.ds(pl.multiple_of(index * count, count), count)
+
+        def scatter(product, meanwhile=lambda: None):
+            mates = [link(to_mate.at[d], from_mate.at[d], plan.mate) for d in range(4)]
+            chips = [link(to_chip.at[d - 1], from_chip.at[d - 1], (0, 0, 2 * d)) for d in (1, 2, 3)]
+            for d in (3, 2, 1, 0):
+                to_mate[d] = product((chip ^ d) * 2 + 1 - core).astype(bf16)
+                mates[d].start()
+            for d in (3, 2, 1):
+                part[...] = product((chip ^ d) * 2 + core)
+                mates[d].wait_recv()
+                to_chip[d - 1] = (part[...] + from_mate[d].astype(f32)).astype(bf16)
+                chips[d - 1].start()
+            part[...] = product(chip * 2 + core)
+            mates[0].wait_recv()
+            part[...] = part[...] + from_mate[0].astype(f32)
+            meanwhile()
+            for copy in chips:
+                copy.wait_recv()
+            part[...] = part[...] + (
+                from_chip[0].astype(f32) + from_chip[1].astype(f32) + from_chip[2].astype(f32)
+            )
+            for copy in mates + chips:
+                copy.wait_send()
+
+        def gather(all_ref, each, meanwhile=lambda: None):
+            own = all_ref.at[rows_at(ring, TOK)]
+            first = [link(own, own, plan.mate)] + [link(own, own, (0, 0, 2 * d)) for d in (1, 2, 3)]
+            for copy in first[1:] + first[:1]:
+                copy.start()
+            meanwhile()
+            first[0].wait_recv()
+            each(chip)
+            later = []
+            for d in (1, 2, 3):
+                first[d].wait_recv()
+                block = all_ref.at[rows_at(ring ^ (2 * d), TOK)]
+                copy = link(block, block, plan.mate)
+                copy.start()
+                later.append(copy)
+            for d in (1, 2, 3):
+                later[d - 1].wait_recv()
+                each(chip ^ d)
+            for copy in first + later:
+                copy.wait_send()
+
+        is_first = first_ref[...] > 0.5
+
+        def modulated(index):
+            cols = pl.ds(index * D, D)
+            return jnp.where(is_first, mod_ref[0:1, cols], mod_ref[1:2, cols])
+
+        def column_sums(at, values):
+            total = jnp.sum(values, axis=0, keepdims=True)
+            start = jnp.sum(jnp.where(is_first, values, 0.0), axis=0, keepdims=True)
+            sums_ref[at : at + 1, :] = start
+            sums_ref[at + 1 : at + 2, :] = total - start
+
+        def scale_of(values):
+            return lax.rsqrt(jnp.mean(values * values, axis=1, keepdims=True) + epsilon)
+
+        def norm_back(d_hat, hat, inverse):
+            return inverse * (d_hat - hat * jnp.mean(d_hat * hat, axis=1, keepdims=True))
+
+        def load(job, target):
+            moves.take(job)
+            copy = pltpu.make_async_copy(outs[job], target, local_sem.at[0])
+            copy.start()
+            copy.wait()
+
+        def out_product(block):
+            return jnp.dot(mixed_ref[rows_at(block, TOK), :], out_w[...], preferred_element_type=f32)
+
+        scatter(out_product)
+        moves.chain()
+        proj_ref[...] = part[...]
+        proj = proj_ref[...]
+        gate_attn = jnp.tanh(modulated(1))
+        state_ref[...] = latent_ref[...] + gate_attn * (proj * scale_of(proj) * gain_ref[1:2, :])
+        state = state_ref[...]
+        ffn_in = state * scale_of(state) * gain_ref[2:3, :] * (1.0 + modulated(2))
+        ffn_all[rows_at(ring, TOK), :] = ffn_in.astype(bf16)
+
+        def forward_chip(which):
+            rows = rows_at(which, chip_rows)
+            block = ffn_all[rows, :]
+            gate = jnp.dot(block, gate_w[...], preferred_element_type=f32)
+            up = jnp.dot(block, up_w[...], preferred_element_type=f32)
+            gate_ref[rows, :] = gate
+            up_ref[rows, :] = up
+            act_ref[rows, :] = (gate * (1.0 / (1.0 + jnp.exp(-gate))) * up).astype(bf16)
+
+        def weights_here():
+            load(0, gate_w)
+            load(2, up_w)
+
+        gather(ffn_all, forward_chip, weights_here)
+
+        def down_product(block):
+            return jnp.dot(act_ref[rows_at(block, TOK), :], down_w[...], preferred_element_type=f32)
+
+        scatter(down_product)
+
+        down = part[...]
+        inverse = scale_of(down)
+        hat = down * inverse
+        gate_ffn = jnp.tanh(modulated(3))
+        gain = gain_ref[3:4, :]
+        cot = cot_ref[...]
+        result_ref[...] = state_ref[...] + gate_ffn * (hat * gain)
+        column_sums(7, cot * (hat * gain) * (1.0 - gate_ffn * gate_ffn))
+        d_norm = cot * gate_ffn
+        sums_ref[2:3, :] = jnp.sum(d_norm * hat, axis=0, keepdims=True)
+        down_all[rows_at(ring, TOK), :] = norm_back(d_norm * gain, hat, inverse).astype(bf16)
+
+        def backward_chip(which):
+            rows = rows_at(which, chip_rows)
+            d_act = lax.dot_general(down_all[rows, :], down_w[...], turned, preferred_element_type=f32)
+            gate, up = gate_ref[rows, :], up_ref[rows, :]
+            sigmoid = 1.0 / (1.0 + jnp.exp(-gate))
+            d_up_ref[rows, :] = (d_act * (gate * sigmoid)).astype(bf16)
+            d_gate_ref[rows, :] = (d_act * up * (sigmoid * (1.0 + gate * (1.0 - sigmoid)))).astype(bf16)
+
+        gather(down_all, backward_chip)
+
+        away = 1 - item
+        down_link = link(grad_down.at[rows_at(away, slab)], from_down, plan.item)
+        gate_link = link(grad_gate.at[rows_at(away, part_rows)], from_gate, plan.item)
+        up_link = link(grad_up.at[rows_at(away, part_rows)], from_up, plan.item)
+        time_links = [link(down_sum.at[rows_at(time ^ mask[1], d_rows)], from_time.at[i], mask) for i, mask in enumerate(plan.time)]
+
+        def down_gradient():
+            grad_down[...] = lax.dot_general(act_ref[...], down_all[...], sunk, preferred_element_type=f32).astype(bf16)
+            down_link.start()
+
+        def gate_gradients():
+            down_gradient()
+            grad_gate[...] = lax.dot_general(ffn_all[...], d_gate_ref[...], sunk, preferred_element_type=f32).astype(bf16)
+            gate_link.start()
+            grad_up[...] = lax.dot_general(ffn_all[...], d_up_ref[...], sunk, preferred_element_type=f32).astype(bf16)
+            up_link.start()
+
+        def back_product(block):
+            rows = rows_at(block, TOK)
+            return lax.dot_general(d_gate_ref[rows, :], gate_w[...], turned, preferred_element_type=f32) + lax.dot_general(
+                d_up_ref[rows, :], up_w[...], turned, preferred_element_type=f32
+            )
+
+        scatter(back_product, gate_gradients)
+
+        d_ffn = part[...]
+        state = state_ref[...]
+        inverse = scale_of(state)
+        hat = state * inverse
+        gain = gain_ref[2:3, :]
+        column_sums(5, d_ffn * (hat * gain))
+        d_norm = d_ffn * (1.0 + modulated(2))
+        sums_ref[1:2, :] = jnp.sum(d_norm * hat, axis=0, keepdims=True)
+        d_state_ref[...] = cot_ref[...] + norm_back(d_norm * gain, hat, inverse)
+        d_state = d_state_ref[...]
+        proj = proj_ref[...]
+        inverse = scale_of(proj)
+        hat = proj * inverse
+        gate_attn = jnp.tanh(modulated(1))
+        gain = gain_ref[1:2, :]
+        column_sums(3, d_state * (hat * gain) * (1.0 - gate_attn * gate_attn))
+        d_norm = d_state * gate_attn
+        sums_ref[0:1, :] = jnp.sum(d_norm * hat, axis=0, keepdims=True)
+        proj_all[rows_at(ring, TOK), :] = norm_back(d_norm * gain, hat, inverse).astype(bf16)
+
+        def down_time():
+            down_link.wait_recv()
+            mine = grad_down[rows_at(item, slab), :].astype(f32) + from_down[...].astype(f32)
+            down_sum[...] = mine.astype(bf16)
+            for copy in time_links:
+                copy.start()
+
+        def mixed_chip(which):
+            rows = rows_at(which, chip_rows)
+            d_mixed_ref[rows, :] = lax.dot_general(
+                proj_all[rows, :], out_w[...], turned, preferred_element_type=f32
+            ).astype(bf16)
+
+        gather(proj_all, mixed_chip, down_time)
+        grad_out_ref[...] = lax.dot_general(mixed_ref[...], proj_all[...], sunk, preferred_element_type=f32).astype(bf16)
+        gate_link.wait_recv()
+        gate_sum_ref[...] = (
+            grad_gate[rows_at(item, part_rows), :].astype(f32) + from_gate[...].astype(f32)
+        ).astype(bf16)
+        own_ref[...] = down_sum[rows_at(time, d_rows), :].astype(f32)
+        for i, copy in enumerate(time_links):
+            copy.wait_recv()
+            own_ref[...] += from_time[i].astype(f32)
+        down_grad_ref[...] = own_ref[...]
+        up_link.wait_recv()
+        up_sum_ref[...] = (grad_up[rows_at(item, part_rows), :].astype(f32) + from_up[...].astype(f32)).astype(bf16)
+        for copy in [down_link, gate_link, up_link] + time_links:
+            copy.wait_send()
+        moves.finish()
+
+    links = 7 * 3 + 7 * 3 + 3 + others
+    result = pl.pallas_call(
+        kernel,
+        out_shape=[
+            jax.ShapeDtypeStruct((TOK, D), f32),
+            jax.ShapeDtypeStruct((TOK, D), f32),
+            jax.ShapeDtypeStruct((ROWS, deep), bf16),
+            jax.ShapeDtypeStruct((deep, D), bf16),
+            jax.ShapeDtypeStruct((part_rows, width), bf16),
+            jax.ShapeDtypeStruct((part_rows, width), bf16),
+            jax.ShapeDtypeStruct((d_rows, D), f32),
+            jax.ShapeDtypeStruct((16, D), f32),
+        ]
+        + moves.out_shapes(),
+        in_specs=[VMEM] * 8 + [ANY] * n_in,
+        out_specs=[VMEM] * 8 + [ANY] * n_out,
+        scratch_shapes=[
+            pltpu.VMEM((D, width), bf16),
+            pltpu.VMEM((D, width), bf16),
+            pltpu.VMEM((ROWS, D), bf16),
+            pltpu.VMEM((ROWS, D), bf16),
+            pltpu.VMEM((ROWS, D), bf16),
+            pltpu.VMEM((ROWS, width), f32),
+            pltpu.VMEM((ROWS, width), f32),
+            pltpu.VMEM((ROWS, width), bf16),
+            pltpu.VMEM((ROWS, width), bf16),
+            pltpu.VMEM((ROWS, width), bf16),
+            pltpu.VMEM((D, width), bf16),
+            pltpu.VMEM((D, width), bf16),
+            pltpu.VMEM((width, D), bf16),
+            pltpu.VMEM((part_rows, width), bf16),
+            pltpu.VMEM((part_rows, width), bf16),
+            pltpu.VMEM((slab, D), bf16),
+            pltpu.VMEM((slab, D), bf16),
+            pltpu.VMEM((max(others, 1), d_rows, D), bf16),
+            pltpu.VMEM((4, TOK, D), bf16),
+            pltpu.VMEM((4, TOK, D), bf16),
+            pltpu.VMEM((3, TOK, D), bf16),
+            pltpu.VMEM((3, TOK, D), bf16),
+            pltpu.VMEM((TOK, D), f32),
+            pltpu.VMEM((TOK, D), f32),
+            pltpu.VMEM((TOK, D), f32),
+            pltpu.VMEM((d_rows, D), f32),
+            pltpu.SemaphoreType.DMA((links,)),
+            pltpu.SemaphoreType.DMA((links,)),
+            pltpu.SemaphoreType.DMA((1,)),
+        ]
+        + moves.scratch(),
+        name="feed_forward",
+        compiler_params=pltpu.CompilerParams(
+            collective_id=plan.identity(), has_side_effects=True, vmem_limit_bytes=60 * 2**20
+        ),
+    )(mixed, out_full, latents, cotangent, modulation, gains, first_rows, down_full, *moves.operands())
+    return result[:8]
+
+
 def normed(value, gain_row):
     return value * lax.rsqrt(jnp.mean(value * value, axis=-1, keepdims=True) + epsilon) * gain_row
 
 
 def attn_head(input_rows, scale_rows, gain_row):
     return normed(input_rows, gain_row) * (1.0 + scale_rows)
-
-
-def attn_tail(input_rows, proj_rows, gate_rows, gain_row):
-    return input_rows + jnp.tanh(gate_rows) * normed(proj_rows, gain_row)
 
 
 def dot(a, b, dims=(1, 0)):
@@ -927,9 +1263,8 @@
     frame_q = lax.dynamic_slice_in_dim(frame_k, time * ROWS, ROWS)
     position_q = lax.dynamic_slice_in_dim(position_all.reshape(-1), time * ROWS, ROWS).astype(f32)
     frame_own = lax.dynamic_index_in_dim(frame_all, group_place, 0, keepdims=False)
-    mod_rows = jnp.where(frame_own[:, None] == 0, modulation[0][None], modulation[1][None])
-    scale_attn, gate_attn = mod_rows[:, :D], mod_rows[:, D : 2 * D]
-    scale_ffn, gate_ffn = mod_rows[:, 2 * D : 3 * D], mod_rows[:, 3 * D :]
+    mod_rows = jnp.where(frame_own[:, None] == 0, modulation[0, :D][None], modulation[1, :D][None])
+    scale_attn = mod_rows
     onehot = (frame_own[:, None] == jnp.arange(FRAMES, dtype=jnp.int32)[None, :]).astype(f32)
     text_line = jnp.arange(FRAMES * TEXT, dtype=jnp.int32)
     text_frame = text_line // TEXT
@@ -1027,67 +1362,30 @@
         text_packed,
         text_features,
         gates_v,
-        [plan.gather_time(gate_shard), plan.swap_item(down_time)],
+        [plan.stack_time(gate_shard.reshape(M * k_rows, sets * d_rows)), plan.swap_item(down_time)],
     )
     down_full = down_full.reshape(sets * d_rows, D)
-    attn_proj, (up_time, gate_full) = product_scatter(
-        plan, "out_proj", [(mixed, out_full)], False, [plan.gather_time(up_shard), plan.swap_item(gate_time)]
-    )
-    gate_full = gate_full.reshape(D, sets * d_rows)
-
-    state_rows, attn_tail_back = jax.vjp(attn_tail, inputs, attn_proj, gate_attn, gains[1])
-    ffn_in_float, ffn_head_back = jax.vjp(attn_head, state_rows, scale_ffn, gains[2])
-    ffn_in_all, up_full = exchange(
-        plan, "gather_ffn_in", [plan.gather_ring(ffn_in_float.astype(bf16)), plan.swap_item(up_time)]
-    )
-    ffn_in_all = ffn_in_all.reshape(ROWS, D)
-    up_full = up_full.reshape(D, sets * d_rows)
-    gate, up = dot(ffn_in_all, gate_full), dot(ffn_in_all, up_full)
-
-    def swiglu(gate_rows, up_rows):
-        return jax.nn.silu(gate_rows) * up_rows
-
-    activated, swiglu_back = jax.vjp(swiglu, gate, up)
-    activated = activated.astype(bf16)
-    down_out, _ = product_scatter(plan, "down", [(activated, down_full)], False)
-    result_rows, ffn_tail_back = jax.vjp(attn_tail, state_rows, down_out, gate_ffn, gains[3])
-
-    d_state_tail, d_down, d_gate_ffn, d_gain_four = ffn_tail_back(cotangent[0])
-    (d_down_all,) = exchange(plan, "gather_d_down", [plan.gather_ring(d_down.astype(bf16))])
-    d_down_all = d_down_all.reshape(ROWS, D)
-    grad_down = dot(activated, d_down_all, (0, 0)).astype(bf16)
-    d_activated = dot(d_down_all, down_full, (1, 1))
-    d_gate, d_up = swiglu_back(d_activated)
-    d_gate, d_up = d_gate.astype(bf16), d_up.astype(bf16)
-    span_block = (GROUPS, times, M * k_rows, sets * d_rows)
+    first_rows = (frame_own == 0).astype(f32)[:, None]
+    (result_rows, d_state, d_mixed, grad_out, gate_sum, up_sum, down_grad, ffn_sums) = feed_forward(
+        plan,
+        mixed,
+        out_full,
+        inputs,
+        cotangent[0],
+        modulation,
+        gains,
+        first_rows,
+        gate_time,
+        up_shard.reshape(M * k_rows, sets * d_rows),
+        down_full,
+        d_rows,
+    )
+    grad_out = grad_out[HEAD:]
 
     def add(parts):
         return jnp.sum(parts.astype(f32), axis=0)
 
-    d_ffn_in, (down_parts,) = product_scatter(
-        plan,
-        "d_ffn_in",
-        [(d_gate, gate_full), (d_up, up_full)],
-        True,
-        [plan.scatter_item(grad_down.reshape(GROUPS, times, d_rows, D))],
-    )
-    down_sum = add(down_parts).astype(bf16)
-    grad_gate = dot(ffn_in_all, d_gate, (0, 0)).astype(bf16).reshape(span_block)
-    grad_up = dot(ffn_in_all, d_up, (0, 0)).astype(bf16).reshape(span_block)
-    d_state_head, d_scale_ffn, d_gain_three = ffn_head_back(d_ffn_in)
-    d_state = d_state_tail + d_state_head
-    d_inputs_tail, d_proj, d_gate_attn, d_gain_two = attn_tail_back(d_state)
-    d_proj_all, gate_parts, down_parts = exchange(
-        plan,
-        "gather_d_proj",
-        [plan.gather_ring(d_proj.astype(bf16)), plan.scatter_item(grad_gate), plan.scatter_time(down_sum)],
-    )
-    d_proj_all = d_proj_all.reshape(ROWS, D)
-    down_grad = add(down_parts)
-    gate_sum = add(gate_parts).astype(bf16)
-    grad_out = dot(mixed, d_proj_all, (0, 0))[HEAD:].astype(bf16)
-    d_mixed = dot(d_proj_all, out_full, (1, 1)).astype(bf16)
-    (dq, dk, dv, tdk, tdv, gate_sums), (gate_parts, up_parts, out_parts) = flash_backward(
+    (dq, dk, dv, tdk, tdv, gate_sums), (gate_parts, out_parts) = flash_backward(
         plan,
         query,
         kv_all,
@@ -1100,13 +1398,11 @@
         gates_q,
         gates_v,
         [
-            plan.scatter_time(gate_sum),
-            plan.scatter_item(grad_up),
+            plan.split_time(gate_sum),
             plan.scatter_item(grad_out.reshape(GROUPS, times, o_rows, D)),
         ],
     )
     gate_sum = add(gate_parts).astype(bf16).reshape(M, k_rows, sets * d_rows)
-    up_sum = add(up_parts).astype(bf16)
     out_sum = add(out_parts).astype(bf16)
     gate_sums = jnp.sum(gate_sums[0, HEAD:].reshape(heads, HEAD), axis=1)
     dq, dk, dv, tdk, tdv = dq[:, :LOCAL], dk[:, :LOCAL], dv[:, HEAD:], tdk[:, :LOCAL], tdv[:, HEAD:]
@@ -1141,7 +1437,7 @@
             plan.scatter_item(grad_qkv[:, :, 0]),
             plan.scatter_time(grad_qkv[:, :, 1].transpose(1, 0, 2, 3)),
             plan.scatter_item(grad_text),
-            plan.scatter_time(up_sum),
+            plan.split_time(up_sum),
         ],
     )
     qkv_sum_a = add(qkv_parts_a).astype(bf16)
@@ -1149,10 +1445,11 @@
     text_sum = add(text_parts).astype(bf16).reshape(M, t_rows, 2 * LOCAL)
     up_sum = add(up_parts).astype(bf16).reshape(M, k_rows, sets * d_rows)
     d_inputs_head, d_scale_attn, d_gain_one = attn_head_back(d_attn_in)
-    grad_latent = d_inputs_tail + d_inputs_head
-
-    d_mod_rows = jnp.concatenate([d_scale_attn, d_gate_attn, d_scale_ffn, d_gate_ffn], axis=1)
-    d_mod = jnp.einsum("tf,td->fd", onehot, d_mod_rows, precision=highest)
+    grad_latent = d_state + d_inputs_head
+
+    d_mod = jnp.concatenate(
+        [jnp.einsum("tf,td->fd", onehot, d_scale_attn, precision=highest), ffn_sums[3:5], ffn_sums[5:7], ffn_sums[7:9]], axis=1
+    )
     d_mod = d_mod.reshape(FRAMES, rows_axis, part_n).transpose(1, 0, 2).reshape(times, M, FRAMES, part_n)
 
     def spread(vector):
@@ -1165,9 +1462,9 @@
     d_gains = jnp.stack(
         [
             d_gain_one,
-            d_gain_two,
-            d_gain_three,
-            d_gain_four,
+            ffn_sums[0],
+            ffn_sums[1],
+            ffn_sums[2],
             spread(unhalve(d_gain_q)),
             spread(unhalve(d_gain_k)),
             spread(d_gain_t * first),

time: 727 us -> 704 us (0.968)
  other arithmetic: 75.9 us -> 51 us
  matrix products: 42.2 us -> 22.9 us
  Pallas kernels: 509 us -> 524 us
  local copies, waits for them, and re-layouts: 81.4 us -> 89.2 us
    pallas_call x0 -> x1, Pallas kernels: none -> 171 us  [feed_forward(): pl.pallas_call(kernel, out_shape=[jax.ShapeDtypeStruct((TOK, D), f32), ja...]
    pallas_call x4 -> x1, Pallas kernels: 130 us -> 46.6 us  [product_scatter(): pl.pallas_call(kernel, out_shape=[jax.ShapeDtypeStruct((TOK, D), f32)] +...]
    pallas_call x11 -> x8, Pallas kernels: 245 us -> 172 us  [exchange(): pl.pallas_call(kernel, out_shape=moves.out_shapes(), in_specs=[ANY] * n_i...]
    dot_general x16 -> x8, matrix products: 37 us -> 18.4 us  [dot(): lax.dot_general(a, b, (((dims[0],), (dims[1],)), ((), ())), preferred_ele...]
    reduce_sum x4 -> x1, other arithmetic: 11.2 us -> 1.11 us  [normed(): value * lax.rsqrt(jnp.mean(value * value, axis=-1, keepdims=True) + epsilon)]
    another operation x15 -> x14, local copies, waits for them, and re-layouts: 4.74 us -> 13.8 us  [the longest x13 13.8 us: shards(): jnp.stack([d_gain_one, ffn_sums[0], ffn_sums[1], ffn_sums[2], spread(unha...]
    reduce_sum x13 -> x9, other arithmetic: 15.3 us -> 10 us  [add(): return jnp.sum(parts.astype(f32), axis=0)]
    unnamed x252 -> x187, local copies, waits for them, and re-layouts: 30.5 us -> 30.3 us
  transfers between devices with their start and end apart: 2 -> 2, of which waited for: 0 -> 0; matrix products, arithmetic and copies ran while one was open for 8% -> 7% of each run, Pallas kernels for 7% -> 7%
where the time goes in v2:
time: 704 us; the launch traced here: 695 us
  Pallas kernels  524 us (74%)
  local copies, waits for them, and re-layouts  89.2 us (13%)
  other arithmetic  51 us (7%)
  matrix products  22.9 us (3%)
    pallas_call x8, Pallas kernels, exchange(): pl.pallas_call(kernel, out_shape=moves.out_shapes(), in_specs=[ANY] * n_i...  172 us
    pallas_call x1, Pallas kernels, feed_forward(): pl.pallas_call(kernel, out_shape=[jax.ShapeDtypeStruct((TOK, D), f32), ja...  171 us
    pallas_call x1, Pallas kernels, flash_backward(): pl.pallas_call(kernel, out_shape=[jax.ShapeDtypeStruct((ROWS, WIDE), f32)...  76.2 us
    pallas_call x1, Pallas kernels, flash_forward(): pl.pallas_call(kernel, out_shape=[jax.ShapeDtypeStruct((ROWS, WIDE), bf16...  58.1 us
    pallas_call x1, Pallas kernels, product_scatter(): pl.pallas_call(kernel, out_shape=[jax.ShapeDtypeStruct((TOK, D), f32)] +...  46.6 us
    unnamed x187, local copies, waits for them, and re-layouts  30.3 us
    dot_general x8, matrix products, dot(): lax.dot_general(a, b, (((dims[0],), (dims[1],)), ((), ())), preferred_ele...  18.4 us
  transfers between devices with their start and end apart: 2, of which 0 were waited for; matrix products, arithmetic and copies ran while one was open for 7% of the time, Pallas kernels for 7%

profile of v2, /device:TPU:0, one launch (start us, length us, event | category | flops | bytes accessed | tf_op | source)
XLA Modules:
  0.0 694.8 jit_solution(267738762666795365)
XLA Ops:
  7.1 34.8 %gather_small.1 = (f32[4,8,8,128]{3,2,1,0:T(8,128)S(1)}, bf16[2,2,1024]{2,1,0:T(2,128)(2,1)S(1)}, bf16[8,48,576]{2,1,0:T(8,128)(2,1)S(1)}, bf16[8,128,384]{2,1,0:T(8,128)(2,1)S(1)}, bf16[2,128,1536]{2,1,0:T(8,128)(2,1)S(1)}) custom-call(f32[8,128]{1,0:T(8,128)S(1)} %fusion.61.refs_0_, bf16[2,1024]{1,0:T(2,128)(2,1)S(1)} %fusion.58.refs_1_, ...), custom_call_target="tpu_custom_call" | custom-call | tf_op jit(solution)/shard_map/gather_small/pallas_call | solution.py:362
  61.6 2.9 constant_dynamic-slice_fusion.3
  64.5 25.3 %scatter_modulation.1 = (f32[4,8,2,384]{3,2,1,0:T(2,128)S(1)}, bf16[2,4,48,576]{3,2,1,0:T(8,128)(2,1)S(1)}, bf16[2,4,128,384]{3,2,1,0:T(8,128)(2,1)S(1)}, bf16[8...) custom-call(f32[4,8,2,384]{3,2,1,0:T(2,128)S(1)} %bitcast.185, bf16[8,48,576]{2,1,0:T(8,128)(2,1)S(1)} %get-tuple-element.71.refs_1_, ...), custom_call_target="tpu_custom_call" | custom-call | tf_op jit(solution)/shard_map/scatter_modulation/pallas_call | solution.py:362
  91.5 17.1 %gather_modulation.1 = (f32[2,8,2,384]{3,2,1,0:T(2,128)S(1)}, bf16[2,4,48,576]{3,2,1,0:T(8,128)(2,1)S(1)}, bf16[2,4,128,384]{3,2,1,0:T(8,128)(2,1)S(1)}, bf16[8,48,512]{2,1,0:T(8,128)(2,1)S(1)}) custom-call(f32[2,384]{1,0:T(2,128)S(1)} %reduce_sum.299.refs_0_, bf16[8,48,576]{2,1,0:T(8,128)(2,1)S(1)} %get-tuple-element.71.refs_1_, ...), custom_call_target="tpu_custom_call" | custom-call | tf_op jit(solution)/shard_map/gather_modulation/pallas_call | solution.py:362
  112.2 30.8 %gather_attn_in.1 = (bf16[8,128,1536]{2,1,0:T(8,128)(2,1)S(1)}, bf16[2,2,4,48,576]{4,3,2,1,0:T(8,128)(2,1)S(1)}, bf16[2,2,4,48,576]{4,3,2,1,0:T(8,128)(2,1)S(1)}...) custom-call(bf16[128,1536]{1,0:T(8,128)(2,1)S(1)} %multiply_convert_fusion.2.refs_0_, ...), custom_call_target="tpu_custom_call" | custom-call | tf_op jit(solution)/shard_map/gather_attn_in/pallas_call | solution.py:362
  153.7 5.0 gather_squares.1
  166.7 2.5 fusion.42
  172.7 58.1 %flash_forward.1 = (bf16[1024,256]{1,0:T(8,128)(2,1)}, f32[1024,256]{1,0:T(8,128)}, f32[1024,256]{1,0:T(8,128)}, bf16[2,1024,384]{2,1,0:T(8,128)(2,1)}, bf16[768...) custom-call(bf16[1024,256]{1,0:T(8,128)(2,1)} %pad_maximum_fusion.6.refs_0_, ...), custom_call_target="tpu_custom_call" | custom-call | tf_op jit(solution)/shard_map/flash_forward/pallas_call | solution.py:924
  230.9 170.6 %feed_forward.1 = (f32[128,1536]{1,0:T(8,128)}, f32[128,1536]{1,0:T(8,128)}, bf16[1024,256]{1,0:T(8,128)(2,1)}, bf16[256,1536]{1,0:T(8,128)(2,1)}, bf16[768,512]...) custom-call(bf16[1024,256]{1,0:T(8,128)(2,1)} %get-tuple-element.86., ...), custom_call_target="tpu_custom_call" | custom-call | tf_op jit(solution)/shard_map/feed_forward/pallas_call | solution.py:724
  403.4 76.2 %flash_backward.1 = (f32[1024,256]{1,0:T(8,128)}, f32[1024,256]{1,0:T(8,128)}, f32[1024,256]{1,0:T(8,128)}, f32[512,256]{1,0:T(8,128)}, f32[512,256]{1,0:T(8,128...) custom-call(bf16[1024,256]{1,0:T(8,128)(2,1)} %pad_maximum_fusion.6.refs_0_, ...), custom_call_target="tpu_custom_call" | custom-call | tf_op jit(solution)/shard_map/flash_backward/pallas_call | solution.py:1109
  479.6 2.7 multiply_reduce_fusion.9
  482.5 4.2 fusion.33
  488.9 10.5 %gather_sums.1 = (f32[8,20,128]{2,1,0:T(8,128)S(1)}, bf16[2,48,1536]{2,1,0:T(8,128)(2,1)S(1)}) custom-call(f32[20,128]{1,0:T(8,128)S(1)} %maximum_bitcast_fusion.1.refs_0_, bf16[2,48,1536]{2,1,0:T(8,128)(2,1)S(1)} %reduce_sum.308.refs_1_), custom_call_target="tpu_custom_call" | custom-call | tf_op jit(solution)/shard_map/gather_sums/pallas_call | solution.py:362
  504.0 2.9 convolution_convert_fusion.3
  512.7 6.0 convolution_convert_fusion.2
  518.6 2.7 copy.144
  523.0 46.6 %d_attn_in.1 = (f32[128,1536]{1,0:T(8,128)S(1)}, bf16[2,2,192,576]{3,2,1,0:T(8,128)(2,1)S(1)}, bf16[2,2,192,576]{3,2,1,0:T(8,128)(2,1)S(1)}, bf16[2,2,512,384]{3,2,1,0:T(8,128)(2,1)}, bf16[2,384,512]{2,1,0:T(8,128)(2,1)S(1)}) custom-call(bf16[1024,576]{1,0:T(8,128)(2,1)} %pad_maximum_fusion.2.refs_0_, bf16[1536,576]{1,0:T(8,128)(2,1)} %copy-done.37, ...), custom_call_target="tpu_custom_call" | custom-call | tf_op jit(solution)/shard_map/d_attn_in/pallas_call | solution.py:451
  594.4 2.3 fusion.9
  605.9 32.0 %scatter_grads.1 = (f32[2,8,2,384]{3,2,1,0:T(2,128)S(1)}, f32[4,8,8,48]{3,2,1,0:T(8,128)S(1)}, f32[4,8,1,128]{3,2,1,0:T(1,128)S(1)}, bf16[2,192,576]{2,1,0:T(8,1...) custom-call(f32[2,8,2,384]{3,2,1,0:T(2,128)S(1)} %bitcast.187, ...), custom_call_target="tpu_custom_call" | custom-call | tf_op jit(solution)/shard_map/scatter_grads/pallas_call | solution.py:362
  648.9 3.9 collective-permute-start.1
  654.5 16.8 %gather_d_mod.1 = (f32[4,8,2,384]{3,2,1,0:T(2,128)S(1)}, bf16[8,48,576]{2,1,0:T(8,128)(2,1)S(1)}) custom-call(f32[2,384]{1,0:T(2,128)S(1)} %reduce_sum.321.refs_0_, bf16[8,48,576]{2,1,0:T(8,128)(2,1)S(1)} %bitcast.177), custom_call_target="tpu_custom_call" | custom-call | tf_op jit(solution)/shard_map/gather_d_mod/pallas_call | solution.py:362
  671.4 2.3 fusion.8
  679.9 2.6 reshape.453
  684.0 3.1 copy.158
  (370 shorter events, 130.7 us)
Async XLA Ops:
  0.6 46.7 %copy-start = (bf16[32,6144]{1,0:T(8,128)(2,1)S(1)}, bf16[32,6144]{1,0:T(8,128)(2,1)}, u32[]{:S(2)}) copy-start(bf16[32,6144]{1,0:T(8,128)(2,1)} %param.32) | copy-start | bytes 1179652
  0.7 63.8 %collective-permute-start = (bf16[48,1536]{1,0:T(8,128)(2,1)}, bf16[48,1536]{1,0:T(8,128)(2,1)S(1)}, u32[]{:S(2)}, u32[]{:S(2)}) collective-permute-start(bf16[48,1536]{1,0:T(8,128)(2,1)} %param.29), channel_id=1, source_target_pairs={{0,0},{1,8},{2,16},{3,24},{4,1},{5,9},{6,17},{7,25},{8,2},{9,10},{... | collective-permute-start | bytes 442376 | tf_op jit(solution)/shard_map/ppermute | solution.py:1210
  45.1 64.4 %copy-start.68 = (pred[128]{0:T(512)(128)(4,1)}, pred[128]{0:T(512)(128)(4,1)S(1)}, u32[]{:S(2)}) copy-start(pred[128]{0:T(512)(128)(4,1)S(1)} %broadcast_compare_fusion.2) | copy-start | bytes 388
  52.4 57.1 %copy-start.66 = (f32[128]{0:T(128)}, f32[128]{0:T(128)S(1)}, u32[]{:S(2)}) copy-start(f32[128]{0:T(128)S(1)} %fusion.83) | copy-start | bytes 1540
  64.5 44.9 %copy-start.58 = (f32[6144]{0:T(1024)S(1)}, f32[6144]{0:T(1024)}, u32[]{:S(2)}) copy-start(f32[6144]{0:T(1024)} %add.198) | copy-start | bytes 73732
  91.4 19.5 %copy-start.45 = (bf16[512,512]{1,0:T(8,128)(2,1)S(1)}, bf16[512,512]{1,0:T(8,128)(2,1)}, u32[]{:S(2)}) copy-start(bf16[512,512]{1,0:T(8,128)(2,1)} %get-tuple-element.178) | copy-start | bytes 1572868
  91.5 19.4 %copy-start.25 = (bf16[2,4,128,384]{3,2,1,0:T(8,128)(2,1)S(1)}, bf16[2,4,128,384]{3,2,1,0:T(8,128)(2,1)}, u32[]{:S(2)}) copy-start(bf16[2,4,128,384]{3,2,1,0:T(8,128)(2,1)} %copy-done.24) | copy-start | bytes 2359300
  91.5 19.4 %copy-start.46 = (bf16[512,512]{1,0:T(8,128)(2,1)S(1)}, bf16[512,512]{1,0:T(8,128)(2,1)}, u32[]{:S(2)}) copy-start(bf16[512,512]{1,0:T(8,128)(2,1)} %get-tuple-element.179) | copy-start | bytes 1572868
  91.5 19.4 %copy-start.47 = (bf16[512,512]{1,0:T(8,128)(2,1)S(1)}, bf16[512,512]{1,0:T(8,128)(2,1)}, u32[]{:S(2)}) copy-start(bf16[512,512]{1,0:T(8,128)(2,1)} %get-tuple-element.180) | copy-start | bytes 1572868
  91.5 19.4 %copy-start.48 = (bf16[512,512]{1,0:T(8,128)(2,1)S(1)}, bf16[512,512]{1,0:T(8,128)(2,1)}, u32[]{:S(2)}) copy-start(bf16[512,512]{1,0:T(8,128)(2,1)} %get-tuple-element.181) | copy-start | bytes 1572868
  403.4 76.2 %copy-start.29 = (f32[512,384]{1,0:T(8,128)S(1)}, f32[512,384]{1,0:T(8,128)}, u32[]{:S(2)}) copy-start(f32[512,384]{1,0:T(8,128)} %copy-done.28) | copy-start | bytes 2359300
  523.0 46.7 %copy-start.26 = (f32[1,128,1536]{2,1,0:T(8,128)S(1)}, f32[1,128,1536]{2,1,0:T(8,128)}, u32[]{:S(2)}) copy-start(f32[1,128,1536]{2,1,0:T(8,128)} %param.22) | copy-start | bytes 2359300
  523.0 46.7 %copy-start.53 = (f32[1536]{0:T(1024)S(1)}, f32[1536]{0:T(1024)}, u32[]{:S(2)}) copy-start(f32[1536]{0:T(1024)} %copy-done.52) | copy-start | bytes 18436
  523.0 46.7 %copy-start.56 = (f32[1536]{0:T(1024)S(1)}, f32[1536]{0:T(1024)}, u32[]{:S(2)}) copy-start(f32[1536]{0:T(1024)} %copy-done.55) | copy-start | bytes 18436
  523.0 46.7 %copy-start.67 = (f32[128]{0:T(128)S(1)}, f32[128]{0:T(128)}, u32[]{:S(2)}) copy-start(f32[128]{0:T(128)} %copy-done.66) | copy-start | bytes 1540
  523.0 46.7 %copy-start.69 = (pred[128]{0:T(512)(128)(4,1)S(1)}, pred[128]{0:T(512)(128)(4,1)}, u32[]{:S(2)}) copy-start(pred[128]{0:T(512)(128)(4,1)} %copy-done.68) | copy-start | bytes 388
  569.6 27.0 %copy-start.2 = (bf16[2,2,192,576]{3,2,1,0:T(8,128)(2,1)}, bf16[2,2,192,576]{3,2,1,0:T(8,128)(2,1)S(1)}, u32[]{:S(2)}) copy-start(bf16[2,2,192,576]{3,2,1,0:T(8,128)(2,1)S(1)} %get-tuple-element.110) | copy-start | bytes 2654212
  569.7 28.9 %copy-start.4 = (bf16[2,384,512]{2,1,0:T(8,128)(2,1)}, bf16[2,384,512]{2,1,0:T(8,128)(2,1)S(1)}, u32[]{:S(2)}) copy-start(bf16[2,384,512]{2,1,0:T(8,128)(2,1)S(1)} %get-tuple-element.114) | copy-start | bytes 2359300
  648.9 22.4 %copy-start.27 = (f32[1,128,1536]{2,1,0:T(8,128)S(1)}, f32[1,128,1536]{2,1,0:T(8,128)}, u32[]{:S(2)}) copy-start(f32[1,128,1536]{2,1,0:T(8,128)} %param.22) | copy-start | bytes 2359300
  648.9 22.5 %copy-start.54 = (f32[1536]{0:T(1024)S(1)}, f32[1536]{0:T(1024)}, u32[]{:S(2)}) copy-start(f32[1536]{0:T(1024)} %copy-done.52) | copy-start | bytes 18436
  648.9 22.5 %copy-start.57 = (f32[1536]{0:T(1024)S(1)}, f32[1536]{0:T(1024)}, u32[]{:S(2)}) copy-start(f32[1536]{0:T(1024)} %copy-done.55) | copy-start | bytes 18436
  648.9 22.5 %copy-start.70 = (pred[128]{0:T(512)(128)(4,1)S(1)}, pred[128]{0:T(512)(128)(4,1)}, u32[]{:S(2)}) copy-start(pred[128]{0:T(512)(128)(4,1)} %copy-done.68) | copy-start | bytes 388
  648.9 42.2 %collective-permute-start.1 = (f32[48,1536]{1,0:T(8,128)}, f32[48,1536]{1,0:T(8,128)}, u32[]{:S(2)}, u32[]{:S(2)}) collective-permute-start(f32[48,1536]{1,0:T(8,128)} %convert_reduce_fusion.1), channel_id=1, source_target_pairs={{0,0},{8,1},{16,2},{24,3},{1,4},{9,5},{17,6},{25,7},{2,8},{10,9},{... | collective-permute-start | bytes 884744 | tf_op jit(solution)/shard_map/ppermute | solution.py:1420
  654.5 19.2 %copy-start.30 = (f32[48,2,4,8,128]{4,2,0,3,1:T(4,128)S(1)}, f32[48,2,4,8,128]{4,2,0,3,1:T(4,128)}, u32[]{:S(2)}) copy-start(f32[48,2,4,8,128]{4,2,0,3,1:T(4,128)} %convert_bitcast_fusion) | copy-start | bytes 4718596
  (63 other events, 200.2 us)

commit v3 on v1

v3 whole, which is shorter than its diff:
```python
import jax
import jax.numpy as jnp
import numpy as np
from jax import lax
from jax.experimental import pallas as pl
from jax.experimental.pallas import tpu as pltpu
from jax.sharding import Mesh
from jax.sharding import PartitionSpec as P

D = 1536
HEADS = 24
HEAD = 64
FF = 4096
TEXT_DIM = 4096
COND = 1024
TEXT = 256
FRAMES = 2
TOK = 128
GROUPS = 2
M = 8
LOCAL = HEADS // M * HEAD
ROWS = M * TOK
WIDE = 256
SPARE = 96
APART = 8192.0

epsilon = 1e-05
theta_base = 10000.0
highest = lax.Precision.HIGHEST
MESH = pl.DeviceIdType.MESH
f32 = jnp.float32
bf16 = jnp.bfloat16
ANY = pl.BlockSpec(memory_space=pl.ANY)
VMEM = pl.BlockSpec(memory_space=pltpu.VMEM)


def flip(where, mask):
    return tuple(a if b == 0 else a ^ b for a, b in zip(where, mask))


class Job:
    def __init__(self, x, shape, masks, src, dst, pass_on=(), by=None, source=None, piece=None):
        self.x, self.shape, self.masks, self.src, self.dst = x, shape, masks, src, dst
        self.piece = piece
        self.pass_on, self.by, self.source = tuple(pass_on), by, source
        if source is not None:
            self.x = None
        self.dtype = x.dtype

    def count(self):
        return len(self.masks) + len(self.pass_on)

    def block(self):
        return self.piece or self.shape[len(self.dst((0, 0, 0))) :]

    def peers(self):
        return set(self.masks) | ({self.by} if self.pass_on else set())


class Transfers:
    def __init__(self, jobs):
        self.jobs = jobs
        self.sent = [j for j in jobs if j.source is None]
        self.total = sum(j.count() for j in jobs)

    def operands(self):
        return [j.x for j in self.sent]

    def out_shapes(self):
        return [jax.ShapeDtypeStruct(j.shape, j.dtype) for j in self.jobs]

    def scratch(self):
        if not self.jobs:
            return []
        return [
            pltpu.SemaphoreType.DMA((self.total,)),
            pltpu.SemaphoreType.DMA((self.total,)),
            pltpu.SemaphoreType.DMA((2, len(self.jobs))),
        ] + [pltpu.VMEM(j.block(), j.dtype) for j in self.jobs]

    def peers(self):
        found = set()
        for j in self.jobs:
            found |= j.peers()
        return found

    def bind(self, me, ins, outs, sems):
        self.me, self.outs, self.sems = me, outs, sems
        left = list(ins)
        self.ins = []
        for j in self.jobs:
            self.ins.append(left.pop(0) if j.source is None else outs[self.jobs.index(j.source)])
        self.base, at = [], 0
        for j in self.jobs:
            self.base.append(at)
            at += j.count()
        self.arrived, self.kept, self.settled, self.chained, self.forwarded = set(), set(), set(), set(), set()

    def remote(self, src, dst, slot, dest):
        return pltpu.make_async_remote_copy(
            src_ref=src,
            dst_ref=dst,
            send_sem=self.sems[0].at[slot],
            recv_sem=self.sems[1].at[slot],
            device_id=dest,
            device_id_type=MESH,
        )

    def send(self, k, i):
        j = self.jobs[k]
        if i < len(j.masks):
            dest = flip(self.me, j.masks[i])
            at = j.src(dest)
            src = self.ins[k] if at is None else self.ins[k].at[at]
            return self.remote(src, self.outs[k].at[j.dst(self.me)], self.base[k] + i, dest)
        mask = j.pass_on[i - len(j.masks)]
        block = self.outs[k].at[j.dst(flip(self.me, mask))]
        return self.remote(block, block, self.base[k] + i, flip(self.me, j.by))

    def own(self, k, leg):
        j = self.jobs[k]
        room = self.sems[3 + k]
        if leg == 0:
            at = j.src(self.me)
            src = self.ins[k] if at is None else self.ins[k].at[at]
            return pltpu.make_async_copy(src, room, self.sems[2].at[0, k])
        return pltpu.make_async_copy(room, self.outs[k].at[j.dst(self.me)], self.sems[2].at[1, k])

    def start_job(self, k):
        j = self.jobs[k]
        for i in range(len(j.masks)):
            self.send(k, i).start()
        self.own(k, 0).start()

    def start(self, late=()):
        for k, j in enumerate(self.jobs):
            if j.source is None and k not in late:
                self.start_job(k)

    def receive(self, k, i):
        if (k, i) not in self.arrived:
            self.arrived.add((k, i))
            self.send(k, i).wait_recv()

    def take(self, k):
        self.keep(k)
        for i in range(self.jobs[k].count()):
            self.receive(k, i)
        if k not in self.settled:
            self.settled.add(k)
            self.own(k, 1).wait()

    def keep(self, k):
        if k not in self.kept:
            self.kept.add(k)
            self.own(k, 0).wait()
            self.own(k, 1).start()

    def chain(self, late=()):
        for k, j in enumerate(self.jobs):
            if j.source is not None and k not in self.chained and k not in late:
                self.chained.add(k)
                self.take(self.jobs.index(j.source))
                self.start_job(k)

    def forward(self):
        self.chain()
        for k in range(len(self.jobs)):
            self.keep(k)
        for k, j in enumerate(self.jobs):
            if k not in self.forwarded:
                self.forwarded.add(k)
                for n, mask in enumerate(j.pass_on):
                    self.receive(k, j.masks.index(mask))
                    self.send(k, len(j.masks) + n).start()

    def finish(self):
        self.forward()
        for k, j in enumerate(self.jobs):
            self.take(k)
            for i in range(j.count()):
                self.send(k, i).wait_send()


class Plan:
    def __init__(self, times):
        self.times = times
        self.sets = GROUPS * times
        self.rows = times * M
        self.next_id = 0
        ones = [(i, t, m) for i in range(GROUPS) for t in range(times) for m in range(M)]
        self.all = ones[1:]
        self.ring = [(0, 0, m) for m in range(1, M)]
        self.chips = [(0, 0, m) for m in range(2, M, 2)]
        self.mate = (0, 0, 1)
        self.time = [(0, t, 0) for t in range(1, times)]
        self.item = (1, 0, 0)
        self.span = [(i, t, 0) for i in range(GROUPS) for t in range(times)][1:]
        self.group = [(0, t, m) for t in range(times) for m in range(M)][1:]

    def identity(self):
        self.next_id += 1
        return self.next_id

    def set_of(self, where):
        return where[0] * self.times + where[1]

    def gather_ring(self, x):
        return Job(
            x,
            (M,) + x.shape,
            [self.mate] + self.chips,
            lambda dest: None,
            lambda sender: (sender[2],),
            self.chips,
            self.mate,
        )

    def direct_ring(self, x):
        return Job(x, (M,) + x.shape, self.ring, lambda dest: None, lambda sender: (sender[2],))

    def scatter_ring(self, x):
        return Job(x, x.shape, self.ring, lambda dest: (dest[2],), lambda sender: (sender[2],))

    def gather_span(self, x, shape=None, source=None):
        return Job(
            x,
            (self.sets,) + (x.shape if shape is None else shape),
            [self.item] + self.time,
            lambda dest: None,
            lambda sender: (self.set_of(sender),),
            self.time,
            self.item,
            source,
        )

    def scatter_span(self, x):
        return Job(x, x.shape, self.span, lambda dest: (self.set_of(dest),), lambda sender: (self.set_of(sender),))

    def gather_time(self, x):
        return Job(x, (self.times,) + x.shape, self.time, lambda dest: None, lambda sender: (sender[1],))

    def stack_time(self, x):
        n = x.shape[0]
        return Job(
            x,
            (self.times * n,) + x.shape[1:],
            self.time,
            lambda dest: None,
            lambda sender: (pl.ds(pl.multiple_of(sender[1] * n, n), n),),
            piece=x.shape,
        )

    def stack_item(self, x, source=None):
        shape = x.shape if source is None else source.shape
        n = shape[0]
        return Job(
            x,
            (GROUPS * n,) + shape[1:],
            [self.item],
            lambda dest: None,
            lambda sender: (pl.ds(pl.multiple_of(sender[0] * n, n), n),),
            source=source,
            piece=shape,
        )

    def split_time(self, x):
        n = x.shape[0] // self.times
        return Job(
            x,
            (self.times, n) + x.shape[1:],
            self.time,
            lambda dest: (pl.ds(pl.multiple_of(dest[1] * n, n), n),),
            lambda sender: (sender[1],),
        )

    def scatter_group_ring(self, x):
        return Job(
            x,
            (self.times,) + x.shape,
            self.group,
            lambda dest: (dest[2],),
            lambda sender: (sender[1], sender[2]),
        )

    def swap_source(self, source):
        return Job(
            source.x if source.x is not None else source,
            (GROUPS,) + source.shape,
            [self.item],
            lambda dest: None,
            lambda sender: (sender[0],),
            source=source,
        )

    def gather_time_source(self, source):
        return Job(
            source,
            (self.times,) + source.shape,
            self.time,
            lambda dest: None,
            lambda sender: (sender[1],),
            source=source,
        )

    def ring_of_times(self, x, source=None):
        shape = x.shape if source is None else source.shape
        return Job(
            x if source is None else source,
            (M, shape[0]) + tuple(shape[2:]),
            self.ring,
            lambda dest: (slice(None), dest[2]),
            lambda sender: (sender[2],),
            source=source,
        )

    def times_of_ring(self, source):
        shape = source.shape
        return Job(
            source,
            (shape[1], shape[0]) + tuple(shape[2:]),
            self.time,
            lambda dest: (slice(None), dest[1]),
            lambda sender: (sender[1],),
            source=source,
        )

    def scatter_time(self, x):
        return Job(x, x.shape, self.time, lambda dest: (dest[1],), lambda sender: (sender[1],))

    def scatter_item(self, x):
        return Job(x, x.shape, [self.item], lambda dest: (dest[0],), lambda sender: (sender[0],))

    def gather_all(self, x):
        return Job(
            x,
            (self.sets, M) + x.shape,
            self.all,
            lambda dest: None,
            lambda sender: (self.set_of(sender), sender[2]),
        )

    def scatter_all(self, x):
        return Job(
            x,
            x.shape,
            self.all,
            lambda dest: (self.set_of(dest), dest[2]),
            lambda sender: (self.set_of(sender), sender[2]),
        )

    def swap_item(self, x):
        return Job(x, (GROUPS,) + x.shape, [self.item], lambda dest: None, lambda sender: (sender[0],))

    def gather_group(self, x):
        return Job(
            x,
            (self.times, M) + x.shape,
            self.group,
            lambda dest: None,
            lambda sender: (sender[1], sender[2]),
        )

    def scatter_group(self, x):
        return Job(
            x,
            x.shape,
            self.group,
            lambda dest: (dest[1], dest[2]),
            lambda sender: (sender[1], sender[2]),
        )


def here():
    return (lax.axis_index("items"), lax.axis_index("times"), lax.axis_index("ring"))


def greet(me, peers):
    barrier = pltpu.get_barrier_semaphore()
    for mask in sorted(peers):
        pl.semaphore_signal(barrier, inc=1, device_id=flip(me, mask), device_id_type=MESH)
    pl.semaphore_wait(barrier, len(peers))


def exchange(plan, name, jobs):
    moves = Transfers(jobs)
    n_in, n_out = len(moves.sent), len(jobs)

    def kernel(*refs):
        me = here()
        greet(me, moves.peers())
        moves.bind(me, refs[:n_in], refs[n_in : n_in + n_out], refs[n_in + n_out :])
        moves.start()
        moves.finish()

    return pl.pallas_call(
        kernel,
        out_shape=moves.out_shapes(),
        in_specs=[ANY] * n_in,
        out_specs=[ANY] * n_out,
        scratch_shapes=moves.scratch(),
        name=name,
        compiler_params=pltpu.CompilerParams(
            collective_id=plan.identity(), has_side_effects=True, vmem_limit_bytes=32 * 2**20
        ),
    )(*moves.operands())


def lane_masks():
    lane = np.arange(WIDE)
    query, value = np.zeros((8, WIDE), np.float32), np.zeros((8, WIDE), np.float32)
    back = np.zeros((8, WIDE), np.float32)
    inner = lane % 128
    for h in range(LOCAL // HEAD):
        query[h] = ((inner < SPARE) & (inner // (HEAD // 2) == h)) | (lane == 128 + SPARE) | (lane == 129 + SPARE)
        query[h] += (lane >= 130 + SPARE + 3 * h) & (lane < 133 + SPARE + 3 * h)
        value[h] = ((lane >= HEAD) & (lane // HEAD - 1 == h)) | (lane // 16 == h)
        back[h] = ((lane >= HEAD) & (lane // HEAD - 1 == h)) | (lane == 2 * h) | (lane == 2 * h + 1)
    return query, value, back


def wide_order():
    col = np.arange(LOCAL)
    head, pair, odd = col // HEAD, col % HEAD // 2, col % 2
    return odd * 128 + head * (HEAD // 2) + pair, HEAD + col


def placing(places, width):
    return (jnp.asarray(places, jnp.int32)[:, None] == jnp.arange(width, dtype=jnp.int32)[None, :]).astype(bf16)


def widen(packed_ref, feature, key_ref, value_ref, rows):
    lane = lax.broadcasted_iota(jnp.int32, (rows, 128), 1)
    first, second = packed_ref[:, :128].astype(f32), packed_ref[:, 128:256].astype(f32)
    key_ref[:rows, :128] = jnp.where(lane < SPARE, first, 0.0).astype(bf16)
    key_ref[:rows, 128:] = jnp.where(lane < SPARE, second, feature.astype(f32)).astype(bf16)
    moved = jnp.where(lane < SPARE, pltpu.roll(first, 96, 1), second)
    value_ref[:rows, :128] = jnp.where(lane < HEAD, 1.0, moved).astype(bf16)
    value_ref[:rows, 128:] = packed_ref[:, 256:]


def pack(key_first, key_second, value_first, value_second, packed_ref, rows):
    lane = lax.broadcasted_iota(jnp.int32, (rows, 128), 1)
    packed_ref[:, :128] = jnp.where(lane < SPARE, key_first, pltpu.roll(value_first, 32, 1)).astype(bf16)
    packed_ref[:, 128:256] = jnp.where(lane < SPARE, key_second, value_first).astype(bf16)
    packed_ref[:, 256:] = value_second.astype(bf16)


def unpack(packed, rows):
    lane = lax.broadcasted_iota(jnp.int32, (rows, 128), 1)
    first, second = packed[:, :128].astype(f32), packed[:, 128:256].astype(f32)
    moved = jnp.where(lane < SPARE, pltpu.roll(first, 96, 1), second)
    return (
        jnp.where(lane < SPARE, first, 0.0),
        jnp.where(lane < SPARE, second, 0.0),
        jnp.where(lane < HEAD, 0.0, moved),
        packed[:, 256:].astype(f32),
    )


def fold_rows(values):
    ones = jnp.ones((8, WIDE), f32)
    sums = lax.dot_general(ones, values, (((1,), (1,)), ((), ())), precision=highest, preferred_element_type=f32)
    return jnp.concatenate([sums[0:1, 128 * i : 128 * (i + 1)] for i in range(values.shape[0] // 128)], axis=0)


def spread_rows(folded, out_ref):
    n = folded.shape[0]
    row = lax.broadcasted_iota(jnp.int32, (n, 128), 0)
    ones = jnp.ones((n, 128), f32)
    for i in range(n):
        out_ref[128 * i : 128 * (i + 1), :] = lax.dot_general(
            jnp.where(row == i, folded, 0.0),
            ones,
            (((0,), (0,)), ((), ())),
            precision=highest,
            preferred_element_type=f32,
        )


class Links:
    def __init__(self, me, send_sem, recv_sem):
        self.me, self.send_sem, self.recv_sem, self.used = me, send_sem, recv_sem, 0

    def __call__(self, src, dst, mask):
        slot = self.used
        self.used += 1
        return pltpu.make_async_remote_copy(
            src_ref=src,
            dst_ref=dst,
            send_sem=self.send_sem.at[slot],
            recv_sem=self.recv_sem.at[slot],
            device_id=flip(self.me, mask),
            device_id_type=MESH,
        )


def rows_at(index, count):
    return pl.ds(pl.multiple_of(index * count, count), count)


def ring_sum(plan, link, me, buffers, product, meanwhile=lambda: None):
    to_mate, from_mate, to_chip, from_chip, part = buffers
    core, chip = me[2] % 2, me[2] // 2
    mates = [link(to_mate.at[d], from_mate.at[d], plan.mate) for d in range(4)]
    chips = [link(to_chip.at[d - 1], from_chip.at[d - 1], (0, 0, 2 * d)) for d in (1, 2, 3)]
    for d in (3, 2, 1, 0):
        to_mate[d] = product((chip ^ d) * 2 + 1 - core).astype(bf16)
        mates[d].start()
    for d in (3, 2, 1):
        part[...] = product((chip ^ d) * 2 + core)
        mates[d].wait_recv()
        to_chip[d - 1] = (part[...] + from_mate[d].astype(f32)).astype(bf16)
        chips[d - 1].start()
    part[...] = product(chip * 2 + core)
    mates[0].wait_recv()
    part[...] = part[...] + from_mate[0].astype(f32)
    meanwhile()
    for copy in chips:
        copy.wait_recv()
    part[...] = part[...] + (from_chip[0].astype(f32) + from_chip[1].astype(f32) + from_chip[2].astype(f32))
    for copy in mates + chips:
        copy.wait_send()


def ring_gather(plan, link, me, all_ref, each, meanwhile=lambda: None):
    ring = me[2]
    chip = ring // 2
    own = all_ref.at[rows_at(ring, TOK)]
    first = [link(own, own, plan.mate)] + [link(own, own, (0, 0, 2 * d)) for d in (1, 2, 3)]
    for copy in first[1:] + first[:1]:
        copy.start()
    meanwhile()
    first[0].wait_recv()
    each(chip)
    later = []
    for d in (1, 2, 3):
        first[d].wait_recv()
        block = all_ref.at[rows_at(ring ^ (2 * d), TOK)]
        copy = link(block, block, plan.mate)
        copy.start()
        later.append(copy)
    for d in (1, 2, 3):
        later[d - 1].wait_recv()
        each(chip ^ d)
    for copy in first + later:
        copy.wait_send()


def ring_share(plan, link, all_ref):
    copies = [link(all_ref.at[0], all_ref.at[i + 1], mask) for i, mask in enumerate(plan.ring)]
    for copy in copies:
        copy.start()
    return copies


def scale_of(values):
    return lax.rsqrt(jnp.mean(values * values, axis=1, keepdims=True) + epsilon)


def norm_back(d_hat, hat, inverse):
    return inverse * (d_hat - hat * jnp.mean(d_hat * hat, axis=1, keepdims=True))


RING_BUFFERS = [
    pltpu.VMEM((4, TOK, D), bf16),
    pltpu.VMEM((4, TOK, D), bf16),
    pltpu.VMEM((3, TOK, D), bf16),
    pltpu.VMEM((3, TOK, D), bf16),
    pltpu.VMEM((TOK, D), f32),
]


def params(plan, megabytes):
    return pltpu.CompilerParams(
        collective_id=plan.identity(), has_side_effects=True, vmem_limit_bytes=megabytes * 2**20
    )


def prologue(plan, tiles, package, cond, ada_weight, jobs):
    moves = Transfers([plan.gather_all(package)] + list(jobs))
    n_in, n_out = len(moves.sent), len(moves.jobs)
    total_tiles = 4 * D // 128
    peers, group = plan.all, plan.group

    def kernel(*refs):
        cond_ref, ada_ref = refs[:2]
        ins = refs[2 : 2 + n_in]
        mod_ref, cond_out = refs[2 + n_in : 4 + n_in]
        outs = refs[4 + n_in : 4 + n_in + n_out]
        refs = refs[4 + n_in + n_out :]
        cond_in, part_ref, send_ref, recv_ref, sum_ref, mod_in, send_sem, recv_sem = refs[:8]
        me = here()
        greet(me, moves.peers() | set(peers))
        link = Links(me, send_sem, recv_sem)
        swap = link(cond_ref.at[1], cond_in, plan.item)
        swap.start()
        moves.bind(me, ins, outs, refs[8:])
        moves.start()
        deep = ada_ref.shape[0]
        part_ref[0] = jnp.dot(cond_ref[0][:, :deep].astype(bf16), ada_ref[...], preferred_element_type=f32)
        swap.wait_recv()
        cond_out[...] = cond_in[...]
        part_ref[1] = jnp.dot(cond_in[:, :deep].astype(bf16), ada_ref[...], preferred_element_type=f32)
        for g in range(GROUPS):
            for r in range(plan.rows):
                for f in range(FRAMES):
                    for j in range(tiles):
                        tile = r * tiles + j
                        at = f * tiles + j
                        if tile < total_tiles:
                            send_ref[g, r, at : at + 1, :] = part_ref[g, f : f + 1, 128 * tile : 128 * (tile + 1)]
        copies = []
        for i, mask in enumerate(peers):
            dest = flip(me, mask)
            copies.append(link(send_ref.at[mask[0], dest[1] * M + dest[2]], recv_ref.at[i], mask))
            copies[-1].start()
        place = me[1] * M + me[2]
        total = send_ref[0, place]
        for i, copy in enumerate(copies):
            copy.wait_recv()
            total = total + recv_ref[i]
        sum_ref[...] = total
        mod_in[place] = total
        shares = [link(sum_ref, mod_in.at[place], mask) for mask in group]
        for copy in shares:
            copy.start()
        moves.forward()
        for copy in shares:
            copy.wait_recv()
        mod_ref[...] = mod_in[...]
        for copy in [swap] + copies + shares:
            copy.wait_send()
        moves.finish()

    links = 1 + len(peers) + len(group)
    result = pl.pallas_call(
        kernel,
        out_shape=[jax.ShapeDtypeStruct((plan.rows, 8, 128), f32), jax.ShapeDtypeStruct((8, 128), f32)]
        + moves.out_shapes(),
        in_specs=[VMEM] * 2 + [ANY] * n_in,
        out_specs=[VMEM] * 2 + [ANY] * n_out,
        scratch_shapes=[
            pltpu.VMEM((8, 128), f32),
            pltpu.VMEM((GROUPS, 8, 4 * D), f32),
            pltpu.VMEM((GROUPS, plan.rows, 8, 128), f32),
            pltpu.VMEM((len(peers), 8, 128), f32),
            pltpu.VMEM((8, 128), f32),
            pltpu.VMEM((plan.rows, 8, 128), f32),
            pltpu.SemaphoreType.DMA((links,)),
            pltpu.SemaphoreType.DMA((links,)),
        ]
        + moves.scratch(),
        name="prologue",
        compiler_params=params(plan, 40),
    )(cond, ada_weight, *moves.operands())
    return result[0], result[1], result[2:]


def attention_forward(
    plan,
    latents,
    modulation,
    gains,
    first_rows,
    captions,
    text_weight,
    mix,
    text_mix,
    gain_wide,
    cos,
    sin,
    query_features,
    features,
    text_features,
    gates,
    qkv_time,
    out_shard,
    gate_send,
    up_send,
):
    heads = LOCAL // HEAD
    text_rows = captions.shape[0]
    text_deep = text_weight.shape[0]
    others = len(plan.time)
    out_job = plan.gather_time(out_shard)
    gate_job = plan.scatter_ring(gate_send)
    jobs = [
        plan.stack_item(qkv_time),
        out_job,
        plan.swap_source(out_job),
        gate_job,
        plan.scatter_ring(up_send),
        plan.gather_time_source(gate_job),
    ]
    moves = Transfers(jobs)
    n_in, n_out = len(moves.sent), len(moves.jobs)
    block = 256
    chip_rows = 2 * TOK
    span = text_deep // GROUPS
    folded = 2 * ROWS // 128 + text_rows // 128
    folded_rows = -(-folded // 8) * 8

    def kernel(*refs):
        (latent_ref, mod_ref, gain_ref, first_ref, caption_ref, text_w, mix_ref, text_mix_ref) = refs[:8]
        (wide_ref, cos_ref, sin_ref, qfeature_ref, feature_ref, text_feature_ref, gate_ref, qmask_ref, vmask_ref) = refs[8:17]
        ins = refs[17 : 17 + n_in]
        refs = refs[17 + n_in :]
        (mixed_ref, self_ref, cross_ref, attn_all, query_ref, packed_out, text_packed) = refs[:7]
        (qn_ref, kn_ref, qinv_ref, kinv_ref, tn_ref, tinv_ref) = refs[7:13]
        outs = refs[13 : 13 + n_out]
        refs = refs[13 + n_out :]
        (key_ref, value_ref, packed_ref, far_ref, max_ref, raw_w, weight_ref, raw_ref, own_caps, text_part, text_far) = refs[:11]
        (text_raw, sums_ref, send_sem, recv_sem, local_sem) = refs[11:16]
        me = here()
        item, time, ring = me
        greet(me, moves.peers() | {plan.mate} | set(plan.chips) | set(plan.ring) | set(plan.time))
        link = Links(me, send_sem, recv_sem)
        moves.bind(me, ins, outs, refs[16:])
        loads = []
        for i in range(GROUPS):
            where = pl.ds(pl.multiple_of((i * plan.times + time) * span, span), span)
            loads.append(
                pltpu.make_async_copy(caption_ref.at[:, where], own_caps.at[:, i * span : (i + 1) * span], local_sem.at[i])
            )
            loads[-1].start()

        is_first = first_ref[...] > 0.5
        scale = jnp.where(is_first, mod_ref[0:1, :D], mod_ref[1:2, :D])
        rows = latent_ref[...]
        attn_in = rows * scale_of(rows) * gain_ref[0:1, :] * (1.0 + scale)
        attn_all[rows_at(ring, TOK), :] = attn_in.astype(bf16)

        text_copies = [link(text_part, text_far.at[i], mask) for i, mask in enumerate(plan.time)]

        def text_projection():
            moves.start(late=(3, 4))
            for copy in loads:
                copy.wait()
            text_wide = jnp.dot(text_w[...], text_mix_ref[...], preferred_element_type=f32).astype(bf16)
            text_part[...] = jnp.dot(own_caps[...], text_wide, preferred_element_type=f32).astype(bf16)
            for copy in text_copies:
                copy.start()
            moves.take(0)
            copy = pltpu.make_async_copy(outs[0], raw_w, local_sem.at[0])
            copy.start()
            copy.wait()
            weight_ref[...] = jnp.dot(raw_w[...], mix_ref[...], preferred_element_type=f32).astype(bf16)

        def project(which):
            where = rows_at(which, chip_rows)
            raw_ref[where, :] = jnp.dot(attn_all[where, :], weight_ref[...], preferred_element_type=f32)

        ring_gather(plan, link, me, attn_all, project, text_projection)
        moves.start_job(3)
        moves.start_job(4)
        moves.chain(late=(5,))

        total = text_part[...].astype(f32)
        for i, copy in enumerate(text_copies):
            copy.wait_recv()
            total = total + text_far[i].astype(f32)
        text_raw[...] = total
        q_raw, k_raw, t_raw = raw_ref[:, :WIDE], raw_ref[:, WIDE : 2 * WIDE], total[:, :WIDE]
        squares = [fold_rows(q_raw * q_raw), fold_rows(k_raw * k_raw), fold_rows(t_raw * t_raw)]
        if folded_rows > folded:
            squares.append(jnp.zeros((folded_rows - folded, 128), f32))
        sums_ref[0] = jnp.concatenate(squares, axis=0)
        shares = ring_share(plan, link, sums_ref)
        for copy in shares:
            copy.wait_recv()
        total = sums_ref[0]
        for i in range(1, M):
            total = total + sums_ref[i]
        inverse = lax.rsqrt(total / D + epsilon)
        n = ROWS // 128
        spread_rows(inverse[:n], qinv_ref)
        spread_rows(inverse[n : 2 * n], kinv_ref)
        spread_rows(inverse[2 * n : folded], tinv_ref)

        def turn(where, at, inv_ref, n_ref, gain_row):
            first = raw_ref[where, at : at + 128] * inv_ref[where, :]
            second = raw_ref[where, at + 128 : at + 256] * inv_ref[where, :]
            n_ref[where, :128], n_ref[where, 128:] = first, second
            first = first * wide_ref[gain_row : gain_row + 1, :128]
            second = second * wide_ref[gain_row : gain_row + 1, 128:]
            cosine, sine = cos_ref[where, :], sin_ref[where, :]
            return first * cosine - second * sine, second * cosine + first * sine

        def shape(at, carry):
            where = rows_at(at, block)
            first, second = turn(where, 0, qinv_ref, qn_ref, 0)
            query_ref[where, :128] = (first.astype(bf16).astype(f32) * 0.125).astype(bf16)
            lane = lax.broadcasted_iota(jnp.int32, (block, 128), 1)
            second = jnp.where(lane < SPARE, second.astype(bf16).astype(f32) * 0.125, qfeature_ref[where, :].astype(f32))
            query_ref[where, 128:] = second.astype(bf16)
            first, second = turn(where, WIDE, kinv_ref, kn_ref, 1)
            values = raw_ref[where, 2 * WIDE :]
            pack(first, second, values[:, :128], values[:, 128:], packed_ref.at[where, :], block)
            return carry

        lax.fori_loop(0, ROWS // block, shape, 0)
        key_copies = [link(packed_ref, far_ref.at[i], mask) for i, mask in enumerate(plan.time)]
        for copy in key_copies:
            copy.start()
        first = text_raw[:, :128] * tinv_ref[...]
        second = text_raw[:, 128:256] * tinv_ref[...]
        tn_ref[:, :128], tn_ref[:, 128:] = first, second
        pack(
            first * wide_ref[2:3, :128],
            second * wide_ref[2:3, 128:],
            text_raw[:, 256:384],
            text_raw[:, 384:],
            text_packed,
            text_rows,
        )

        def segment(rows, first, out_ref):
            def body(at, carry):
                where = rows_at(at, block)
                query_rows = query_ref[where, :]
                total = jnp.zeros((block, WIDE), f32)
                tops = jnp.zeros((block, WIDE), f32)
                for h in range(heads):
                    own_query = query_rows * qmask_ref[h : h + 1, :]
                    scores = lax.dot_general(
                        own_query, key_ref[:rows, :], (((1,), (1,)), ((), ())), preferred_element_type=f32
                    )
                    top = jnp.max(scores, axis=1, keepdims=True)
                    weights = jnp.exp(scores - top).astype(bf16)
                    product = jnp.dot(weights, value_ref[:rows, :], preferred_element_type=f32)
                    total += product * vmask_ref[h : h + 1, :]
                    tops += top * vmask_ref[h : h + 1, :]
                if first:
                    out_ref[where, :] = total
                    max_ref[where, :] = tops
                else:
                    before = max_ref[where, :]
                    after = jnp.maximum(before, tops)
                    out_ref[where, :] = out_ref[where, :] * jnp.exp(before - after) + total * jnp.exp(tops - after)
                    max_ref[where, :] = after
                return carry

            lax.fori_loop(0, ROWS // block, body, 0)

        def close(out_ref):
            def body(at, carry):
                where = rows_at(at, block)
                lane = lax.broadcasted_iota(jnp.int32, (block, WIDE), 1)
                values = out_ref[where, :]
                share = jnp.ones((block, WIDE), f32)
                for h in range(heads):
                    share = jnp.where(
                        (lane >= HEAD * (h + 1)) & (lane < HEAD * (h + 2)), values[:, 16 * h : 16 * h + 1], share
                    )
                logs = max_ref[where, :] + jnp.log(jnp.maximum(values, 1e-30))
                out_ref[where, :] = jnp.where(
                    lane < HEAD, jnp.where(lane < 16 * heads, logs, 0.0), values / share
                )
                return carry

            lax.fori_loop(0, ROWS // block, body, 0)

        widen(text_packed, text_feature_ref[...], key_ref, value_ref, text_rows)
        segment(text_rows, True, cross_ref)
        close(cross_ref)
        widen(packed_ref, feature_ref[rows_at(time, ROWS), :], key_ref, value_ref, ROWS)
        packed_out[time] = packed_ref[...]
        segment(ROWS, True, self_ref)
        for i, mask in enumerate(plan.time):
            key_copies[i].wait_recv()
            if i == others - 1:
                moves.chain()
            far = time ^ mask[1]
            packed_out[far] = far_ref[i]
            widen(far_ref.at[i], feature_ref[rows_at(far, ROWS), :], key_ref, value_ref, ROWS)
            segment(ROWS, False, self_ref)
        close(self_ref)
        lane = lax.broadcasted_iota(jnp.int32, (ROWS, WIDE), 1)
        both = self_ref[...] + gate_ref[...] * cross_ref[...]
        mixed_ref[...] = jnp.where(lane < HEAD, 0.0, both).astype(bf16)
        for copy in text_copies + shares + key_copies:
            copy.wait_send()
        moves.finish()

    qmask, vmask, _ = lane_masks()
    links = 7 + (M - 1) + 2 * others
    result = pl.pallas_call(
        kernel,
        out_shape=[
            jax.ShapeDtypeStruct((ROWS, WIDE), bf16),
            jax.ShapeDtypeStruct((ROWS, WIDE), f32),
            jax.ShapeDtypeStruct((ROWS, WIDE), f32),
            jax.ShapeDtypeStruct((ROWS, D), bf16),
            jax.ShapeDtypeStruct((ROWS, WIDE), bf16),
            jax.ShapeDtypeStruct((plan.times, ROWS, 2 * LOCAL), bf16),
            jax.ShapeDtypeStruct((text_rows, 2 * LOCAL), bf16),
            jax.ShapeDtypeStruct((ROWS, WIDE), f32),
            jax.ShapeDtypeStruct((ROWS, WIDE), f32),
            jax.ShapeDtypeStruct((ROWS, 128), f32),
            jax.ShapeDtypeStruct((ROWS, 128), f32),
            jax.ShapeDtypeStruct((text_rows, WIDE), f32),
            jax.ShapeDtypeStruct((text_rows, 128), f32),
        ]
        + moves.out_shapes(),
        in_specs=[VMEM] * 4 + [ANY] + [VMEM] * 12 + [ANY] * n_in,
        out_specs=[VMEM] * 13 + [ANY] * n_out,
        scratch_shapes=[
            pltpu.VMEM((ROWS, WIDE), bf16),
            pltpu.VMEM((ROWS, WIDE), bf16),
            pltpu.VMEM((ROWS, 2 * LOCAL), bf16),
            pltpu.VMEM((max(others, 1), ROWS, 2 * LOCAL), bf16),
            pltpu.VMEM((ROWS, WIDE), f32),
            pltpu.VMEM((D, 3 * LOCAL), bf16),
            pltpu.VMEM((D, 3 * WIDE), bf16),
            pltpu.VMEM((ROWS, 3 * WIDE), f32),
            pltpu.VMEM((text_rows, text_deep), bf16),
            pltpu.VMEM((text_rows, 2 * WIDE), bf16),
            pltpu.VMEM((max(others, 1), text_rows, 2 * WIDE), bf16),
            pltpu.VMEM((text_rows, 2 * WIDE), f32),
            pltpu.VMEM((M, folded_rows, 128), f32),
            pltpu.SemaphoreType.DMA((links,)),
            pltpu.SemaphoreType.DMA((links,)),
            pltpu.SemaphoreType.DMA((GROUPS,)),
        ]
        + moves.scratch(),
        name="attention_forward",
        compiler_params=params(plan, 60),
    )(
        latents,
        modulation,
        gains,
        first_rows,
        captions,
        text_weight,
        mix,
        text_mix,
        gain_wide,
        cos,
        sin,
        query_features,
        features,
        text_features,
        gates,
        jnp.asarray(qmask, bf16),
        jnp.asarray(vmask, f32),
        *moves.operands(),
    )
    return result[:13], result[13:]


def attention_backward(
    plan,
    query,
    packed_all,
    features,
    text_packed,
    text_features,
    self_out,
    cross_out,
    d_mixed,
    gates_q,
    gates_v,
    hats,
    inverses,
    text_hat,
    text_inverse,
    cos,
    sin,
    gain_wide,
    captions,
    attn_all,
    qkv_full,
    mix,
    text_mix,
    latents,
    d_state,
    modulation,
    gains,
    first_rows,
    gate_sum,
    up_sum,
    grad_out,
):
    heads = LOCAL // HEAD
    text_rows = text_packed.shape[0]
    gate_job = plan.scatter_time(gate_sum)
    up_job = plan.ring_of_times(up_sum)
    jobs = [gate_job, plan.ring_of_times(None, gate_job), up_job, plan.times_of_ring(up_job), plan.scatter_span(grad_out)]
    moves = Transfers(jobs)
    n_in, n_out = len(moves.sent), len(moves.jobs)
    block = 256
    others = len(plan.time)
    room = max(others, 1)
    turned = (((1,), (1,)), ((), ()))
    sunk = (((0,), (0,)), ((), ()))
    local3 = qkv_full.shape[1]
    text_deep = captions.shape[1] // plan.times
    span = text_deep // GROUPS
    set_rows = D // plan.sets
    half = set_rows // 2
    folded = 2 * ROWS // 128
    text_folded = max(8, text_rows // 128)

    def kernel(*refs):
        (query_ref, packed_in, feature_ref, text_ref, text_feature_ref, self_ref, cross_ref, d_ref) = refs[:8]
        (gateq_ref, gatev_ref, qmask_ref, bmask_ref, qn_ref, kn_ref, qinv_ref, kinv_ref, tn_ref, tinv_ref) = refs[8:18]
        (cos_ref, sin_ref, wide_ref, caption_ref, attn_ref, qkv_w, mix_ref, text_mix_ref) = refs[18:26]
        (latent_ref, d_state_ref, mod_ref, gain_ref, first_ref) = refs[26:31]
        ins = refs[31 : 31 + n_in]
        refs = refs[31 + n_in :]
        latent_grad, sums_out, wide_out, qkv_out, text_out = refs[:5]
        outs = refs[5 : 5 + n_out]
        refs = refs[5 + n_out :]
        (key_ref, value_ref, near_ref, qs_ref, ds_ref, dq_ref, dk_ref, dv_ref, tdk_ref, tdv_ref) = refs[:10]
        (to_ref, from_ref, tto_ref, tfrom_ref, du_ref, d_text, own_caps, grad_qkv, grad_text) = refs[10:19]
        (a_item, a_sum, a_time, b_time, b_sum, b_item, text_item, share_ref, tshare_ref, mean_ref) = refs[19:29]
        buffers = refs[29:34]
        send_sem, recv_sem, local_sem = refs[34:37]
        me = here()
        item, time, ring = me
        greet(me, moves.peers() | set(plan.time) | set(plan.ring) | {plan.item})
        link = Links(me, send_sem, recv_sem)
        moves.bind(me, ins, outs, refs[37:])
        moves.start()
        loads = []
        for i in range(GROUPS):
            where = pl.ds(pl.multiple_of((i * plan.times + time) * span, span), span)
            loads.append(
                pltpu.make_async_copy(
                    caption_ref.at[:, where], own_caps.at[:, i * span : (i + 1) * span], local_sem.at[1 + i]
                )
            )
            loads[-1].start()

        def prepare(out_ref):
            def body(at, carry):
                where = rows_at(at, block)
                lane = lax.broadcasted_iota(jnp.int32, (block, 128), 1)
                tail = query_ref[where, 128:].astype(f32)
                out_rows = out_ref[where, :]
                d_rows = d_ref[where, :].astype(f32)
                product = d_rows * out_rows
                head_tile = jnp.where(lane < HEAD, 0.0, d_rows[:, :128])
                for h in range(heads):
                    log = -out_rows[:, 16 * h : 16 * h + 1]
                    for j in range(3):
                        piece = log.astype(bf16).astype(f32)
                        log = log - piece
                        tail = jnp.where(lane == SPARE + 2 + 3 * h + j, piece, tail)
                    delta = -jnp.sum(product * bmask_ref[h : h + 1, :].astype(f32), axis=1, keepdims=True)
                    for j in range(2):
                        piece = delta.astype(bf16).astype(f32)
                        delta = delta - piece
                        head_tile = jnp.where(lane == 2 * h + j, piece, head_tile)
                qs_ref[where, :128] = query_ref[where, :128]
                qs_ref[where, 128:] = tail.astype(bf16)
                ds_ref[where, :128] = head_tile.astype(bf16)
                ds_ref[where, 128:] = d_ref[where, 128:]
                return carry

            lax.fori_loop(0, ROWS // block, body, 0)

        def segment(rows, first, k_ref, v_ref, scale):
            k_ref[...] = jnp.zeros_like(k_ref)
            v_ref[...] = jnp.zeros_like(v_ref)

            def body(at, carry):
                where = rows_at(at, block)
                query_rows, d_rows = qs_ref[where, :], ds_ref[where, :]
                total = jnp.zeros((block, WIDE), f32)
                for h in range(heads):
                    own_query = query_rows * qmask_ref[h : h + 1, :]
                    own_d = d_rows * bmask_ref[h : h + 1, :]
                    keys = key_ref[:rows, :]
                    weights = jnp.exp(lax.dot_general(keys, own_query, turned, preferred_element_type=f32))
                    d_weights = lax.dot_general(value_ref[:rows, :], own_d, turned, preferred_element_type=f32)
                    d_scores = (weights * d_weights).astype(bf16)
                    v_ref[...] += jnp.dot(weights.astype(bf16), own_d, preferred_element_type=f32)
                    k_ref[...] += jnp.dot(d_scores, own_query, preferred_element_type=f32)
                    d_query = lax.dot_general(d_scores, keys, sunk, preferred_element_type=f32)
                    total += d_query * qmask_ref[h : h + 1, :].astype(f32)
                total = total * scale
                if first:
                    dq_ref[where, :] = total
                else:
                    dq_ref[where, :] += total
                return carry

            lax.fori_loop(0, ROWS // block, body, 0)

        def bring(which):
            copy = pltpu.make_async_copy(packed_in.at[which], near_ref, local_sem.at[0])
            copy.start()
            copy.wait()
            widen(near_ref, feature_ref[rows_at(which, ROWS), :], key_ref, value_ref, ROWS)

        far_copies = [link(to_ref.at[i], from_ref.at[i], mask) for i, mask in enumerate(plan.time)]
        text_copies = [link(tto_ref, tfrom_ref.at[i], mask) for i, mask in enumerate(plan.time)]

        prepare(self_ref)
        for i, mask in enumerate(plan.time):
            bring(time ^ mask[1])
            segment(ROWS, i == 0, dk_ref, dv_ref, 0.125)
            pack(dk_ref[:, :128], dk_ref[:, 128:], dv_ref[:, :128], dv_ref[:, 128:], to_ref.at[i], ROWS)
            far_copies[i].start()
        moves.chain(late=(3,))
        bring(time)
        segment(ROWS, others == 0, dk_ref, dv_ref, 0.125)
        prepare(cross_ref)
        widen(text_ref, text_feature_ref[...], key_ref, value_ref, text_rows)
        segment(text_rows, False, tdk_ref, tdv_ref, 0.125 * gateq_ref[...])
        tdk_ref[...] = tdk_ref[...] * gateq_ref[...]
        tdv_ref[...] = tdv_ref[...] * gatev_ref[...]
        pack(tdk_ref[:, :128], tdk_ref[:, 128:], tdv_ref[:, :128], tdv_ref[:, 128:], tto_ref, text_rows)
        for copy in text_copies:
            copy.start()
        wide_out[...] = jnp.zeros_like(wide_out)
        wide_out[3:4, :] = jnp.sum(d_ref[...].astype(f32) * cross_ref[...], axis=0, keepdims=True)
        for i in range(others):
            far_copies[i].wait_recv()
            k_first, k_second, v_first, v_second = unpack(from_ref.at[i], ROWS)
            dk_ref[:, :128] += k_first
            dk_ref[:, 128:] += k_second
            dv_ref[:, :128] += v_first
            dv_ref[:, 128:] += v_second

        def unturn(d_all, hat_ref, gain_row):
            pieces = []
            for at in range(ROWS // block):
                where = slice(at * block, (at + 1) * block)
                first, second = d_all[where, :128], d_all[where, 128:]
                cosine, sine = cos_ref[where, :], sin_ref[where, :]
                lane = lax.broadcasted_iota(jnp.int32, (block, 128), 1)
                first, second = jnp.where(lane < SPARE, first, 0.0), jnp.where(lane < SPARE, second, 0.0)
                both = jnp.concatenate([first * cosine + second * sine, second * cosine - first * sine], axis=1)
                hat = hat_ref[where, :]
                wide_out[gain_row : gain_row + 1, :] += jnp.sum(both * hat, axis=0, keepdims=True)
                both = both * wide_ref[gain_row : gain_row + 1, :]
                d_all[where, :] = both
                pieces.append(fold_rows(both * hat))
            return pieces

        pieces = unturn(dq_ref, qn_ref, 0) + unturn(dk_ref, kn_ref, 1)
        share_ref[0] = jnp.concatenate(pieces, axis=0)
        shares = ring_share(plan, link, share_ref)
        for copy in shares:
            copy.wait_recv()
        total = share_ref[0]
        for i in range(1, M):
            total = total + share_ref[i]
        total = total / D
        n = ROWS // 128

        def settle(d_all, hat_ref, inv_ref, means):
            spread_rows(means, mean_ref)
            for c in (0, 128):
                lanes = slice(c, c + 128)
                d_all[:, lanes] = (d_all[:, lanes] - hat_ref[:, lanes] * mean_ref[...]) * inv_ref[...]

        settle(dq_ref, qn_ref, qinv_ref, total[:n])
        settle(dk_ref, kn_ref, kinv_ref, total[n:])
        for at in range(ROWS // block):
            where = slice(at * block, (at + 1) * block)
            lane = lax.broadcasted_iota(jnp.int32, (block, 128), 1)
            values = jnp.concatenate([jnp.where(lane < HEAD, 0.0, dv_ref[where, :128]), dv_ref[where, 128:]], axis=1)
            wide = jnp.concatenate([dq_ref[where, :], dk_ref[where, :], values], axis=1).astype(bf16)
            du_ref[where, :] = lax.dot_general(wide, mix_ref[...], turned, preferred_element_type=f32).astype(bf16)

        grad_qkv[...] = lax.dot_general(attn_ref[...], du_ref[...], sunk, preferred_element_type=f32).astype(bf16)
        away = 1 - item

        def part(i, t, which):
            return pl.ds(pl.multiple_of((i * plan.times + t) * set_rows + which * half, half), half)

        a_items = [link(grad_qkv.at[part(away, t, 0)], a_item.at[t], plan.item) for t in range(plan.times)]
        b_times = [
            link(grad_qkv.at[part(i, time ^ mask[1], 1)], b_time.at[k, i], mask)
            for k, mask in enumerate(plan.time)
            for i in range(GROUPS)
        ]
        a_times = [link(a_sum.at[time ^ mask[1]], a_time.at[k], mask) for k, mask in enumerate(plan.time)]
        b_items = [link(b_sum.at[away], b_item, plan.item)]
        text_items = [link(grad_text.at[rows_at(away, span)], text_item, plan.item)]
        for copy in a_items + b_times:
            copy.start()
        moves.chain()

        def meanwhile():
            for i, copy in enumerate(text_copies):
                copy.wait_recv()
                k_first, k_second, v_first, v_second = unpack(tfrom_ref.at[i], text_rows)
                tdk_ref[:, :128] += k_first
                tdk_ref[:, 128:] += k_second
                tdv_ref[:, :128] += v_first
                tdv_ref[:, 128:] += v_second
            lane = lax.broadcasted_iota(jnp.int32, (text_rows, WIDE), 1) % 128
            d_keys = jnp.where(lane < SPARE, tdk_ref[...], 0.0)
            hat = tn_ref[...]
            wide_out[2:3, :] = jnp.sum(d_keys * hat, axis=0, keepdims=True)
            d_keys = d_keys * wide_ref[2:3, :]
            tdk_ref[...] = d_keys
            sums = fold_rows(d_keys * hat)
            if text_folded > text_rows // 128:
                sums = jnp.concatenate([sums, jnp.zeros((text_folded - text_rows // 128, 128), f32)], axis=0)
            tshare_ref[0] = sums
            text_shares = ring_share(plan, link, tshare_ref)
            for t, copy in enumerate(a_items):
                copy.wait_recv()
                a_sum[t] = (grad_qkv[part(item, t, 0), :].astype(f32) + a_item[t].astype(f32)).astype(bf16)
            for copy in a_times:
                copy.start()
            for copy in text_shares:
                copy.wait_recv()
            total = tshare_ref[0]
            for i in range(1, M):
                total = total + tshare_ref[i]
            total = total / D
            spread_rows(total[: text_rows // 128], mean_ref.at[:text_rows])
            for c in (0, 128):
                lanes = slice(c, c + 128)
                tdk_ref[:, lanes] = (tdk_ref[:, lanes] - tn_ref[:, lanes] * mean_ref[:text_rows, :]) * tinv_ref[...]
            lane = lax.broadcasted_iota(jnp.int32, (text_rows, WIDE), 1)
            values = jnp.where(lane < HEAD, 0.0, tdv_ref[...])
            wide = jnp.concatenate([tdk_ref[...], values], axis=1).astype(bf16)
            d_text[...] = lax.dot_general(wide, text_mix_ref[...], turned, preferred_element_type=f32).astype(bf16)
            for copy in loads:
                copy.wait()
            grad_text[...] = lax.dot_general(own_caps[...], d_text[...], sunk, preferred_element_type=f32).astype(bf16)
            text_items[0].start()
            for copy in text_shares:
                copy.wait_send()
            for copy in b_times:
                copy.wait_recv()
            for i in range(GROUPS):
                total = grad_qkv[part(i, time, 1), :].astype(f32)
                for k in range(others):
                    total = total + b_time[k, i].astype(f32)
                b_sum[i] = total.astype(bf16)
            b_items[0].start()

        def back_product(which):
            return lax.dot_general(du_ref[rows_at(which, TOK), :], qkv_w[...], turned, preferred_element_type=f32)

        ring_sum(plan, link, me, buffers, back_product, meanwhile)

        d_in = buffers[4][...]
        rows = latent_ref[...]
        inverse = scale_of(rows)
        hat = rows * inverse
        gain = gain_ref[0:1, :]
        is_first = first_ref[...] > 0.5
        scale = jnp.where(is_first, mod_ref[0:1, :D], mod_ref[1:2, :D])
        sums_out[...] = jnp.zeros_like(sums_out)
        values = d_in * (hat * gain)
        total = jnp.sum(values, axis=0, keepdims=True)
        start = jnp.sum(jnp.where(is_first, values, 0.0), axis=0, keepdims=True)
        sums_out[1:2, :] = start
        sums_out[2:3, :] = total - start
        d_norm = d_in * (1.0 + scale)
        sums_out[0:1, :] = jnp.sum(d_norm * hat, axis=0, keepdims=True)
        latent_grad[...] = d_state_ref[...] + norm_back(d_norm * gain, hat, inverse)

        total = a_sum[time].astype(f32)
        for k, copy in enumerate(a_times):
            copy.wait_recv()
            total = total + a_time[k].astype(f32)
        qkv_out[:half, :] = total.astype(bf16)
        b_items[0].wait_recv()
        qkv_out[half:, :] = (b_sum[item].astype(f32) + b_item[...].astype(f32)).astype(bf16)
        text_items[0].wait_recv()
        text_out[...] = (grad_text[rows_at(item, span), :].astype(f32) + text_item[...].astype(f32)).astype(bf16)
        for copy in far_copies + text_copies + shares + a_items + b_times + a_times + b_items + text_items:
            copy.wait_send()
        moves.finish()

    qmask, _, bmask = lane_masks()
    links = 2 * others + 2 * (M - 1) + plan.times + GROUPS * others + others + 2 + 7
    result = pl.pallas_call(
        kernel,
        out_shape=[
            jax.ShapeDtypeStruct((TOK, D), f32),
            jax.ShapeDtypeStruct((8, D), f32),
            jax.ShapeDtypeStruct((8, WIDE), f32),
            jax.ShapeDtypeStruct((set_rows, local3), bf16),
            jax.ShapeDtypeStruct((span, 2 * LOCAL), bf16),
        ]
        + moves.out_shapes(),
        in_specs=[VMEM, ANY] + [VMEM] * 19 + [ANY] + [VMEM] * 9 + [ANY] * n_in,
        out_specs=[VMEM] * 5 + [ANY] * n_out,
        scratch_shapes=[
            pltpu.VMEM((ROWS, WIDE), bf16),
            pltpu.VMEM((ROWS, WIDE), bf16),
            pltpu.VMEM((ROWS, 2 * LOCAL), bf16),
            pltpu.VMEM((ROWS, WIDE), bf16),
            pltpu.VMEM((ROWS, WIDE), bf16),
            pltpu.VMEM((ROWS, WIDE), f32),
            pltpu.VMEM((ROWS, WIDE), f32),
            pltpu.VMEM((ROWS, WIDE), f32),
            pltpu.VMEM((text_rows, WIDE), f32),
            pltpu.VMEM((text_rows, WIDE), f32),
            pltpu.VMEM((room, ROWS, 2 * LOCAL), bf16),
            pltpu.VMEM((room, ROWS, 2 * LOCAL), bf16),
            pltpu.VMEM((text_rows, 2 * LOCAL), bf16),
            pltpu.VMEM((room, text_rows, 2 * LOCAL), bf16),
            pltpu.VMEM((ROWS, local3), bf16),
            pltpu.VMEM((text_rows, 2 * LOCAL), bf16),
            pltpu.VMEM((text_rows, text_deep), bf16),
            pltpu.VMEM((D, local3), bf16),
            pltpu.VMEM((text_deep, 2 * LOCAL), bf16),
            pltpu.VMEM((plan.times, half, local3), bf16),
            pltpu.VMEM((plan.times, half, local3), bf16),
            pltpu.VMEM((room, half, local3), bf16),
            pltpu.VMEM((room, GROUPS, half, local3), bf16),
            pltpu.VMEM((GROUPS, half, local3), bf16),
            pltpu.VMEM((half, local3), bf16),
            pltpu.VMEM((span, 2 * LOCAL), bf16),
            pltpu.VMEM((M, folded, 128), f32),
            pltpu.VMEM((M, text_folded, 128), f32),
            pltpu.VMEM((ROWS, 128), f32),
        ]
        + RING_BUFFERS
        + [
            pltpu.SemaphoreType.DMA((links,)),
            pltpu.SemaphoreType.DMA((links,)),
            pltpu.SemaphoreType.DMA((1 + GROUPS,)),
        ]
        + moves.scratch(),
        name="attention_backward",
        compiler_params=params(plan, 63),
    )(
        query,
        packed_all,
        features,
        text_packed,
        text_features,
        self_out,
        cross_out,
        d_mixed,
        gates_q,
        gates_v,
        jnp.asarray(qmask, bf16),
        jnp.asarray(bmask, bf16),
        *hats,
        *inverses,
        text_hat,
        text_inverse,
        cos,
        sin,
        gain_wide,
        captions,
        attn_all,
        qkv_full,
        mix,
        text_mix,
        latents,
        d_state,
        modulation,
        gains,
        first_rows,
        *moves.operands(),
    )
    return result[:5], result[5:]


def finish(plan, small, jobs):
    moves = Transfers(list(jobs))
    n_in, n_out = len(moves.sent), len(moves.jobs)
    peers = plan.all

    def kernel(*refs):
        small_ref = refs[0]
        ins = refs[1 : 1 + n_in]
        all_ref = refs[1 + n_in]
        outs = refs[2 + n_in : 2 + n_in + n_out]
        recv_ref, sum_ref, all_in, send_sem, recv_sem = refs[2 + n_in + n_out : 7 + n_in + n_out]
        me = here()
        greet(me, moves.peers() | set(peers))
        link = Links(me, send_sem, recv_sem)
        moves.bind(me, ins, outs, refs[7 + n_in + n_out :])
        copies = []
        for i, mask in enumerate(peers):
            dest = flip(me, mask)
            copies.append(link(small_ref.at[plan.set_of(dest), dest[2]], recv_ref.at[i], mask))
            copies[-1].start()
        moves.start()
        own = small_ref[plan.set_of(me), me[2]]
        group, everyone = own[:8], own[8:]
        for i, mask in enumerate(peers):
            copies[i].wait_recv()
            if mask[0] == 0:
                group = group + recv_ref[i, :8, :]
            everyone = everyone + recv_ref[i, 8:, :]
        sum_ref[:8, :] = group
        sum_ref[8:, :] = everyone
        place = plan.set_of(me) * M + me[2]
        shares = [link(sum_ref, all_in.at[place], mask) for mask in peers]
        for copy in shares:
            copy.start()
        all_in[place] = sum_ref[...]
        for copy in shares:
            copy.wait_recv()
        all_ref[...] = all_in[...]
        for copy in copies + shares:
            copy.wait_send()
        moves.finish()

    devices = plan.sets * M
    result = pl.pallas_call(
        kernel,
        out_shape=[jax.ShapeDtypeStruct((devices, 16, 128), f32)] + moves.out_shapes(),
        in_specs=[VMEM] + [ANY] * n_in,
        out_specs=[VMEM] + [ANY] * n_out,
        scratch_shapes=[
            pltpu.VMEM((len(peers), 16, 128), f32),
            pltpu.VMEM((16, 128), f32),
            pltpu.VMEM((devices, 16, 128), f32),
            pltpu.SemaphoreType.DMA((2 * len(peers),)),
            pltpu.SemaphoreType.DMA((2 * len(peers),)),
        ]
        + moves.scratch(),
        name="finish",
        compiler_params=params(plan, 40),
    )(small, *moves.operands())
    return result[0], result[1:]


def feed_forward(
    plan, mixed, out_full, latents, cotangent, modulation, gains, first_rows, gate_time, up_shard, down_weight
):
    d_rows = down_weight.shape[0]
    width = plan.sets * d_rows
    deep = out_full.shape[0]
    up_job = plan.stack_time(up_shard)
    down_job = plan.stack_time(down_weight)
    moves = Transfers(
        [plan.stack_item(gate_time), up_job, plan.stack_item(up_shard, up_job), down_job, plan.stack_item(down_weight, down_job)]
    )
    n_in, n_out = len(moves.sent), len(moves.jobs)
    turned = (((1,), (1,)), ((), ()))
    sunk = (((0,), (0,)), ((), ()))
    plain = (((1,), (0,)), ((), ()))
    chip_rows = 2 * TOK
    part_rows = D // GROUPS
    others = len(plan.time)
    slab = plan.times * d_rows

    def kernel(*refs):
        (mixed_ref, out_w, latent_ref, cot_ref, mod_ref, gain_ref, first_ref) = refs[:7]
        ins = refs[7 : 7 + n_in]
        refs = refs[7 + n_in :]
        (result_ref, d_state_ref, d_mixed_ref, grad_out_ref, gate_sum_ref, up_sum_ref, down_grad_ref, sums_ref) = refs[:8]
        outs = refs[8 : 8 + n_out]
        refs = refs[8 + n_out :]
        (gate_w, up_w, down_w, ffn_all, down_all, proj_all, gate_ref, up_ref, act_ref, d_gate_ref, d_up_ref) = refs[:11]
        (grad_gate, grad_up, grad_down, from_gate, from_up, from_down, down_sum, from_time) = refs[11:19]
        (to_mate, from_mate, to_chip, from_chip, part, proj_ref, state_ref, own_ref, send_sem, recv_sem, local_sem) = refs[
            19:30
        ]
        me = here()
        item, time, ring = me
        core, chip = ring % 2, ring // 2
        greet(me, moves.peers() | {plan.mate, plan.item} | set(plan.chips) | set(plan.time))
        moves.bind(me, ins, outs, refs[30:])
        moves.start()
        used = [0]

        def link(src, dst, mask):
            slot = used[0]
            used[0] += 1
            return pltpu.make_async_remote_copy(
                src_ref=src,
                dst_ref=dst,
                send_sem=send_sem.at[slot],
                recv_sem=recv_sem.at[slot],
                device_id=flip(me, mask),
                device_id_type=MESH,
            )

        def rows_at(index, count):
            return pl.ds(pl.multiple_of(index * count, count), count)

        def scatter(product, meanwhile=lambda: None):
            mates = [link(to_mate.at[d], from_mate.at[d], plan.mate) for d in range(4)]
            chips = [link(to_chip.at[d - 1], from_chip.at[d - 1], (0, 0, 2 * d)) for d in (1, 2, 3)]
            for d in (3, 2, 1, 0):
                to_mate[d] = product((chip ^ d) * 2 + 1 - core).astype(bf16)
                mates[d].start()
            for d in (3, 2, 1):
                part[...] = product((chip ^ d) * 2 + core)
                mates[d].wait_recv()
                to_chip[d - 1] = (part[...] + from_mate[d].astype(f32)).astype(bf16)
                chips[d - 1].start()
            part[...] = product(chip * 2 + core)
            mates[0].wait_recv()
            part[...] = part[...] + from_mate[0].astype(f32)
            meanwhile()
            for copy in chips:
                copy.wait_recv()
            part[...] = part[...] + (
                from_chip[0].astype(f32) + from_chip[1].astype(f32) + from_chip[2].astype(f32)
            )
            for copy in mates + chips:
                copy.wait_send()

        def gather(all_ref, each, meanwhile=lambda: None):
            own = all_ref.at[rows_at(ring, TOK)]
            first = [link(own, own, plan.mate)] + [link(own, own, (0, 0, 2 * d)) for d in (1, 2, 3)]
            for copy in first[1:] + first[:1]:
                copy.start()
            meanwhile()
            first[0].wait_recv()
            each(chip)
            later = []
            for d in (1, 2, 3):
                first[d].wait_recv()
                block = all_ref.at[rows_at(ring ^ (2 * d), TOK)]
                copy = link(block, block, plan.mate)
                copy.start()
                later.append(copy)
            for d in (1, 2, 3):
                later[d - 1].wait_recv()
                each(chip ^ d)
            for copy in first + later:
                copy.wait_send()

        is_first = first_ref[...] > 0.5

        def modulated(index):
            cols = pl.ds(index * D, D)
            return jnp.where(is_first, mod_ref[0:1, cols], mod_ref[1:2, cols])

        def column_sums(at, values):
            total = jnp.sum(values, axis=0, keepdims=True)
            start = jnp.sum(jnp.where(is_first, values, 0.0), axis=0, keepdims=True)
            sums_ref[at : at + 1, :] = start
            sums_ref[at + 1 : at + 2, :] = total - start

        def scale_of(values):
            return lax.rsqrt(jnp.mean(values * values, axis=1, keepdims=True) + epsilon)

        def norm_back(d_hat, hat, inverse):
            return inverse * (d_hat - hat * jnp.mean(d_hat * hat, axis=1, keepdims=True))

        def load(job, target):
            moves.take(job)
            copy = pltpu.make_async_copy(outs[job], target, local_sem.at[0])
            copy.start()
            copy.wait()

        def out_product(block):
            return jnp.dot(mixed_ref[rows_at(block, TOK), :], out_w[...], preferred_element_type=f32)

        scatter(out_product)
        moves.chain(late=(4,))
        proj_ref[...] = part[...]
        proj = proj_ref[...]
        gate_attn = jnp.tanh(modulated(1))
        state_ref[...] = latent_ref[...] + gate_attn * (proj * scale_of(proj) * gain_ref[1:2, :])
        state = state_ref[...]
        ffn_in = state * scale_of(state) * gain_ref[2:3, :] * (1.0 + modulated(2))
        ffn_all[rows_at(ring, TOK), :] = ffn_in.astype(bf16)

        def forward_chip(which):
            rows = rows_at(which, chip_rows)
            block = ffn_all[rows, :]
            gate = jnp.dot(block, gate_w[...], preferred_element_type=f32)
            up = jnp.dot(block, up_w[...], preferred_element_type=f32)
            gate_ref[rows, :] = gate
            up_ref[rows, :] = up
            act_ref[rows, :] = (gate * (1.0 / (1.0 + jnp.exp(-gate))) * up).astype(bf16)

        def weights_here():
            load(0, gate_w)
            load(2, up_w)
            moves.chain()

        gather(ffn_all, forward_chip, weights_here)

        load(4, down_w)

        def down_product(block):
            return jnp.dot(act_ref[rows_at(block, TOK), :], down_w[...], preferred_element_type=f32)

        scatter(down_product)

        down = part[...]
        inverse = scale_of(down)
        hat = down * inverse
        gate_ffn = jnp.tanh(modulated(3))
        gain = gain_ref[3:4, :]
        cot = cot_ref[...]
        result_ref[...] = state_ref[...] + gate_ffn * (hat * gain)
        column_sums(7, cot * (hat * gain) * (1.0 - gate_ffn * gate_ffn))
        d_norm = cot * gate_ffn
        sums_ref[2:3, :] = jnp.sum(d_norm * hat, axis=0, keepdims=True)
        down_all[rows_at(ring, TOK), :] = norm_back(d_norm * gain, hat, inverse).astype(bf16)

        def backward_chip(which):
            rows = rows_at(which, chip_rows)
            d_act = lax.dot_general(down_all[rows, :], down_w[...], turned, preferred_element_type=f32)
            gate, up = gate_ref[rows, :], up_ref[rows, :]
            sigmoid = 1.0 / (1.0 + jnp.exp(-gate))
            d_up_ref[rows, :] = (d_act * (gate * sigmoid)).astype(bf16)
            d_gate_ref[rows, :] = (d_act * up * (sigmoid * (1.0 + gate * (1.0 - sigmoid)))).astype(bf16)

        gather(down_all, backward_chip)

        away = 1 - item
        down_link = link(grad_down.at[rows_at(away, slab)], from_down, plan.item)
        gate_link = link(grad_gate.at[rows_at(away, part_rows)], from_gate, plan.item)
        up_link = link(grad_up.at[rows_at(away, part_rows)], from_up, plan.item)
        time_links = [link(down_sum.at[rows_at(time ^ mask[1], d_rows)], from_time.at[i], mask) for i, mask in enumerate(plan.time)]

        def down_gradient():
            grad_down[...] = lax.dot_general(act_ref[...], down_all[...], sunk, preferred_element_type=f32).astype(bf16)
            down_link.start()

        def gate_gradients():
            down_gradient()
            grad_gate[...] = lax.dot_general(ffn_all[...], d_gate_ref[...], sunk, preferred_element_type=f32).astype(bf16)
            gate_link.start()
            grad_up[...] = lax.dot_general(ffn_all[...], d_up_ref[...], sunk, preferred_element_type=f32).astype(bf16)
            up_link.start()

        def back_product(block):
            rows = rows_at(block, TOK)
            return lax.dot_general(d_gate_ref[rows, :], gate_w[...], turned, preferred_element_type=f32) + lax.dot_general(
                d_up_ref[rows, :], up_w[...], turned, preferred_element_type=f32
            )

        scatter(back_product, gate_gradients)

        d_ffn = part[...]
        state = state_ref[...]
        inverse = scale_of(state)
        hat = state * inverse
        gain = gain_ref[2:3, :]
        column_sums(5, d_ffn * (hat * gain))
        d_norm = d_ffn * (1.0 + modulated(2))
        sums_ref[1:2, :] = jnp.sum(d_norm * hat, axis=0, keepdims=True)
        d_state_ref[...] = cot_ref[...] + norm_back(d_norm * gain, hat, inverse)
        d_state = d_state_ref[...]
        proj = proj_ref[...]
        inverse = scale_of(proj)
        hat = proj * inverse
        gate_attn = jnp.tanh(modulated(1))
        gain = gain_ref[1:2, :]
        column_sums(3, d_state * (hat * gain) * (1.0 - gate_attn * gate_attn))
        d_norm = d_state * gate_attn
        sums_ref[0:1, :] = jnp.sum(d_norm * hat, axis=0, keepdims=True)
        proj_all[rows_at(ring, TOK), :] = norm_back(d_norm * gain, hat, inverse).astype(bf16)

        def down_time():
            down_link.wait_recv()
            mine = grad_down[rows_at(item, slab), :].astype(f32) + from_down[...].astype(f32)
            down_sum[...] = mine.astype(bf16)
            for copy in time_links:
                copy.start()

        def mixed_chip(which):
            rows = rows_at(which, chip_rows)
            d_mixed_ref[rows, :] = lax.dot_general(
                proj_all[rows, :], out_w[...], turned, preferred_element_type=f32
            ).astype(bf16)

        gather(proj_all, mixed_chip, down_time)
        grad_out_ref[...] = lax.dot_general(mixed_ref[...], proj_all[...], sunk, preferred_element_type=f32).astype(bf16)
        gate_link.wait_recv()
        gate_sum_ref[...] = (
            grad_gate[rows_at(item, part_rows), :].astype(f32) + from_gate[...].astype(f32)
        ).astype(bf16)
        own_ref[...] = down_sum[rows_at(time, d_rows), :].astype(f32)
        for i, copy in enumerate(time_links):
            copy.wait_recv()
            own_ref[...] += from_time[i].astype(f32)
        down_grad_ref[...] = own_ref[...]
        up_link.wait_recv()
        up_sum_ref[...] = (grad_up[rows_at(item, part_rows), :].astype(f32) + from_up[...].astype(f32)).astype(bf16)
        for copy in [down_link, gate_link, up_link] + time_links:
            copy.wait_send()
        moves.finish()

    links = 7 * 3 + 7 * 3 + 3 + others
    result = pl.pallas_call(
        kernel,
        out_shape=[
            jax.ShapeDtypeStruct((TOK, D), f32),
            jax.ShapeDtypeStruct((TOK, D), f32),
            jax.ShapeDtypeStruct((ROWS, deep), bf16),
            jax.ShapeDtypeStruct((deep, D), bf16),
            jax.ShapeDtypeStruct((part_rows, width), bf16),
            jax.ShapeDtypeStruct((part_rows, width), bf16),
            jax.ShapeDtypeStruct((d_rows, D), f32),
            jax.ShapeDtypeStruct((16, D), f32),
        ]
        + moves.out_shapes(),
        in_specs=[VMEM] * 7 + [ANY] * n_in,
        out_specs=[VMEM] * 8 + [ANY] * n_out,
        scratch_shapes=[
            pltpu.VMEM((D, width), bf16),
            pltpu.VMEM((D, width), bf16),
            pltpu.VMEM((width, D), bf16),
            pltpu.VMEM((ROWS, D), bf16),
            pltpu.VMEM((ROWS, D), bf16),
            pltpu.VMEM((ROWS, D), bf16),
            pltpu.VMEM((ROWS, width), f32),
            pltpu.VMEM((ROWS, width), f32),
            pltpu.VMEM((ROWS, width), bf16),
            pltpu.VMEM((ROWS, width), bf16),
            pltpu.VMEM((ROWS, width), bf16),
            pltpu.VMEM((D, width), bf16),
            pltpu.VMEM((D, width), bf16),
            pltpu.VMEM((width, D), bf16),
            pltpu.VMEM((part_rows, width), bf16),
            pltpu.VMEM((part_rows, width), bf16),
            pltpu.VMEM((slab, D), bf16),
            pltpu.VMEM((slab, D), bf16),
            pltpu.VMEM((max(others, 1), d_rows, D), bf16),
            pltpu.VMEM((4, TOK, D), bf16),
            pltpu.VMEM((4, TOK, D), bf16),
            pltpu.VMEM((3, TOK, D), bf16),
            pltpu.VMEM((3, TOK, D), bf16),
            pltpu.VMEM((TOK, D), f32),
            pltpu.VMEM((TOK, D), f32),
            pltpu.VMEM((TOK, D), f32),
            pltpu.VMEM((d_rows, D), f32),
            pltpu.SemaphoreType.DMA((links,)),
            pltpu.SemaphoreType.DMA((links,)),
            pltpu.SemaphoreType.DMA((1,)),
        ]
        + moves.scratch(),
        name="feed_forward",
        compiler_params=params(plan, 60),
    )(mixed, out_full, latents, cotangent, modulation, gains, first_rows, *moves.operands())
    return result[:8]


def shards(
    latents,
    conditions,
    captions,
    row_counts,
    text_lengths,
    qkv_weight,
    text_weight,
    out_weight,
    gate_up_weight,
    down_weight,
    ada_weight,
    ada_bias,
    norm_gains,
    head_gates,
    cotangent,
):
    times = lax.axis_size("times")
    plan = Plan(times)
    sets, rows_axis = plan.sets, plan.rows
    devices = sets * M
    item, time, ring = here()
    place = (item * times + time) * M + ring
    group_place = time * M + ring
    heads = LOCAL // HEAD

    k_rows = qkv_weight.shape[0]
    t_rows = text_weight.shape[0]
    o_rows = out_weight.shape[0]
    d_rows = down_weight.shape[0]
    a_rows = ada_weight.shape[0]
    bias_n = ada_bias.shape[0]
    gain_n = norm_gains.shape[1]
    tiles = -(-(4 * D // 128) // rows_axis)

    package = jnp.concatenate(
        [norm_gains.astype(f32).reshape(-1), ada_bias.astype(f32), row_counts[0, 0].astype(f32)]
    )
    package_n = package.shape[0]
    lines = -(-package_n // 1024) * 8
    package = jnp.pad(package, (0, lines * 128 - package_n)).reshape(lines, 128)

    silu = jax.nn.silu(conditions[0].astype(f32)).astype(bf16).astype(f32)
    other_place = ((1 - item) * times + time) * M + ring
    cond = jnp.stack(
        [lax.dynamic_slice_in_dim(silu, p * a_rows, a_rows, 1) for p in (place, other_place)]
    )
    cond = jnp.pad(cond, ((0, 0), (0, 8 - FRAMES), (0, 128 - a_rows)))

    key_places, value_places = wide_order()
    mix = placing(np.concatenate([key_places, WIDE + key_places, 2 * WIDE + value_places]), 3 * WIDE)
    text_mix = placing(np.concatenate([key_places, WIDE + value_places]), 2 * WIDE)
    qkv_send = qkv_weight.reshape(k_rows, 3, M, LOCAL).transpose(2, 0, 1, 3).reshape(M, k_rows, 3 * LOCAL)
    text_send = text_weight.reshape(t_rows, 2, M, LOCAL).transpose(2, 0, 1, 3).reshape(M, t_rows, 2 * LOCAL)
    gate_up_send = gate_up_weight.reshape(k_rows, 2, sets, M, d_rows).transpose(1, 3, 0, 2, 4)
    gate_up_send = gate_up_send.reshape(2, M, k_rows, sets * d_rows)
    out_forth = [(o, (o % sets) * M + o // sets) for o in range(devices)]
    out_back = [(b, a) for a, b in out_forth]
    axes = ("items", "times", "ring")
    out_shard = lax.ppermute(out_weight, axes, out_forth)

    text_job = plan.scatter_ring(text_send)
    mod_tiles, cond_other, (packages, qkv_time, _, text_full) = prologue(
        plan,
        tiles,
        package,
        cond,
        ada_weight,
        [plan.scatter_group_ring(qkv_send), text_job, plan.swap_source(text_job)],
    )
    packages = packages.reshape(devices, lines * 128)
    gains = packages[:, : 7 * gain_n].reshape(devices, 7, gain_n).transpose(1, 0, 2).reshape(7, D)
    gains = jnp.pad(gains, ((0, 1), (0, 0)))
    bias = packages[:, 7 * gain_n : 7 * gain_n + bias_n].reshape(4 * D)
    counts_all = packages[:, 7 * gain_n + bias_n : package_n].astype(jnp.int32).reshape(GROUPS, rows_axis, FRAMES)
    counts = lax.dynamic_index_in_dim(counts_all, item, 0, keepdims=False)

    def from_tiles(array):
        lead = array.shape[:-3]
        array = array[..., : FRAMES * tiles, :].reshape(lead + (rows_axis, FRAMES, tiles, 128))
        array = jnp.moveaxis(array, -3, -4).reshape(lead + (FRAMES, rows_axis * tiles * 128))
        return array[..., : 4 * D]

    modulation = from_tiles(mod_tiles) + bias

    line = jnp.arange(TOK, dtype=jnp.int32)[None, :]
    clip = counts[:, :1]
    before = jnp.cumsum(counts, axis=0) - counts
    frame_all = (line >= clip).astype(jnp.int32)
    position_all = jnp.where(frame_all == 0, before[:, :1] + line, before[:, 1:] + line - clip)
    frame_k = frame_all.reshape(-1)
    frame_q = lax.dynamic_slice_in_dim(frame_k, time * ROWS, ROWS)
    position_q = lax.dynamic_slice_in_dim(position_all.reshape(-1), time * ROWS, ROWS).astype(f32)
    frame_own = lax.dynamic_index_in_dim(frame_all, group_place, 0, keepdims=False)
    first_rows = (frame_own == 0).astype(f32)[:, None]
    text_line = jnp.arange(FRAMES * TEXT, dtype=jnp.int32)
    text_frame = text_line // TEXT
    text_live = text_line % TEXT < jnp.repeat(text_lengths[0], TEXT)

    feature = jnp.arange(128, dtype=jnp.int32)[None, :]

    def key_features(apart_first, apart_second):
        ones = (feature >= SPARE + 2) & (feature < SPARE + 2 + 3 * heads)
        pick = jnp.where(feature == SPARE, apart_first[:, None], (feature == SPARE + 1) & apart_second[:, None])
        return jnp.where(pick | ones, 1.0, 0.0).astype(bf16)

    features = key_features(frame_k == 1, frame_k == 0)
    text_features = key_features(~((text_frame == 0) & text_live), ~((text_frame == 1) & text_live))
    query_features = jnp.where(feature == SPARE + frame_q[:, None], -APART, 0.0).astype(bf16)
    pair = jnp.arange(128, dtype=jnp.int32)
    frequency = theta_base ** (-2.0 * (pair % (HEAD // 2)).astype(f32) / HEAD)
    angle = position_q[:, None] * frequency[None, :]
    live_lane = (pair < SPARE)[None, :]
    cos, sin = jnp.where(live_lane, jnp.cos(angle), 0.0), jnp.where(live_lane, jnp.sin(angle), 0.0)
    own_gates = jnp.tanh(lax.dynamic_slice_in_dim(head_gates.astype(f32), ring * heads, heads))
    gates_v = jnp.concatenate([jnp.zeros((HEAD,), f32), jnp.repeat(own_gates, HEAD)]).reshape(1, WIDE)
    half_gates = jnp.pad(jnp.repeat(own_gates, HEAD // 2), (0, 128 - SPARE))
    gates_q = jnp.concatenate([half_gates, half_gates]).reshape(1, WIDE)
    gain_wide = lax.dynamic_slice(gains, (4, ring * LOCAL), (3, LOCAL))
    gain_wide = gain_wide.reshape(3, heads, HEAD // 2, 2).transpose(0, 3, 1, 2).reshape(3, 2, SPARE)
    gain_wide = jnp.pad(gain_wide, ((0, 5), (0, 0), (0, 128 - SPARE))).reshape(8, WIDE)

    inputs = latents[0]
    caption_rows = captions[0].reshape(FRAMES * TEXT, TEXT_DIM)
    forward, (qkv_full, _, out_full, _, up_shard, gate_time) = attention_forward(
        plan,
        inputs,
        modulation,
        gains,
        first_rows,
        caption_rows,
        text_full.reshape(GROUPS * M * t_rows, 2 * LOCAL),
        mix,
        text_mix,
        gain_wide,
        cos,
        sin,
        query_features,
        features,
        text_features,
        gates_v,
        qkv_time.reshape(times * M * k_rows, 3 * LOCAL),
        out_shard,
        gate_up_send[0],
        gate_up_send[1],
    )
    (mixed, self_out, cross_out, attn_all, query, packed_all, text_packed, qn, kn, q_inv, k_inv, tn, t_inv) = forward
    out_full = jnp.pad(out_full.reshape(LOCAL, D), ((HEAD, 0), (0, 0)))

    (result_rows, d_state, d_mixed, grad_out, gate_sum, up_sum, down_grad, ffn_sums) = feed_forward(
        plan,
        mixed,
        out_full,
        inputs,
        cotangent[0],
        modulation,
        gains,
        first_rows,
        gate_time.reshape(times * M * k_rows, sets * d_rows),
        up_shard.reshape(M * k_rows, sets * d_rows),
        down_weight,
    )
    ring_shape = (times, M, k_rows, sets * d_rows)
    (grad_latent, attn_sums, wide_sums, qkv_sum, text_sum), (_, gate_parts, _, up_parts, out_parts) = attention_backward(
        plan,
        query,
        packed_all,
        features,
        text_packed,
        text_features,
        self_out,
        cross_out,
        d_mixed,
        gates_q,
        gates_v,
        (qn, kn),
        (q_inv, k_inv),
        tn,
        t_inv,
        cos,
        sin,
        gain_wide,
        caption_rows,
        attn_all,
        qkv_full,
        mix,
        text_mix,
        inputs,
        d_state,
        modulation,
        gains,
        first_rows,
        gate_sum.reshape(ring_shape),
        up_sum.reshape(ring_shape),
        grad_out[HEAD:].reshape(sets, o_rows, D),
    )

    def add(parts, axis=0):
        return jnp.sum(parts.astype(f32), axis=axis)

    d_mod = jnp.concatenate([attn_sums[1:3], ffn_sums[3:5], ffn_sums[5:7], ffn_sums[7:9]], axis=1)
    d_mod = jnp.pad(d_mod, ((0, 0), (0, rows_axis * tiles * 128 - 4 * D)))
    d_mod = d_mod.reshape(FRAMES, rows_axis, tiles, 128).transpose(1, 0, 2, 3).reshape(rows_axis, FRAMES * tiles, 128)
    d_mod = jnp.pad(d_mod, ((0, 0), (0, 8 - FRAMES * tiles), (0, 0)))
    d_mod = jnp.tile(d_mod, (GROUPS, 1, 1))
    wide_gains = wide_sums[:3].reshape(3, 2, 128)[:, :, :SPARE].reshape(3, 2, heads, HEAD // 2)
    wide_gains = wide_gains.transpose(0, 2, 3, 1).reshape(3, LOCAL)
    wide_gains = wide_gains * jnp.stack([jnp.ones(()), jnp.ones(()), (time == 0).astype(f32)])[:, None]
    wide_gains = lax.dynamic_update_slice(jnp.zeros((3, D), f32), wide_gains, (0, ring * LOCAL))
    gate_sums = jnp.sum(wide_sums[3, HEAD:].reshape(heads, HEAD), axis=1) * (1.0 - own_gates * own_gates)
    gate_row = lax.dynamic_update_slice_in_dim(jnp.zeros((1, D), f32), gate_sums[None], ring * heads, 1)
    d_gains = jnp.concatenate([attn_sums[:1], ffn_sums[:3], wide_gains, gate_row], axis=0)
    gain_tiles = D // 128
    d_gains = d_gains.reshape(8, gain_tiles, 128).transpose(1, 0, 2)
    d_gains = jnp.pad(d_gains, ((0, devices - gain_tiles), (0, 0), (0, 0)))
    small = jnp.concatenate([d_mod, d_gains], axis=1).reshape(sets, M, 16, 128)
    small_all, (qkv_pieces, text_pieces) = finish(
        plan,
        small,
        [
            plan.scatter_ring(qkv_sum.reshape(M, k_rows, 3 * LOCAL)),
            plan.scatter_ring(text_sum.reshape(M, t_rows, 2 * LOCAL)),
        ],
    )
    gains_all = small_all[:gain_tiles, 8:].transpose(1, 0, 2).reshape(8, D)
    gains_grad = lax.dynamic_slice_in_dim(gains_all[:7], place * gain_n, gain_n, 1)
    gates_grad = gains_all[7, :HEADS]
    d_mod_all = from_tiles(small_all[:, :8].reshape(GROUPS, rows_axis, 8, 128)).reshape(GROUPS * FRAMES, 4 * D)
    cond_own, cond_other = cond[0, :FRAMES], cond_other[:FRAMES]
    silu_both = jnp.where(
        item == 0, jnp.concatenate([cond_own, cond_other]), jnp.concatenate([cond_other, cond_own])
    )
    ada_grad = jnp.einsum("fc,fd->cd", silu_both[:, :a_rows], d_mod_all, precision=highest)
    bias_grad = lax.dynamic_slice_in_dim(jnp.sum(d_mod_all, axis=0), place * bias_n, bias_n)
    out_grad = lax.ppermute(add(out_parts), axes, out_back)
    qkv_grad = qkv_pieces.reshape(M, k_rows, 3, LOCAL).transpose(1, 2, 0, 3).reshape(k_rows, 3 * D).astype(f32)
    text_grad = text_pieces.reshape(M, t_rows, 2, LOCAL).transpose(1, 2, 0, 3).reshape(t_rows, 2 * D).astype(f32)
    gate_up_grad = jnp.stack([add(gate_parts, 1), add(up_parts, 0)]).reshape(2, M, k_rows, sets, d_rows)
    gate_up_grad = gate_up_grad.transpose(2, 0, 3, 1, 4).reshape(k_rows, 2 * FF)
    return (
        result_rows[None],
        grad_latent[None],
        qkv_grad,
        text_grad,
        out_grad,
        gate_up_grad,
        down_grad,
        ada_grad,
        bias_grad,
        gains_grad,
        gates_grad,
    )


def solution(mesh):
    items, rows = mesh.shape["items"], mesh.shape["rows"]
    fine = Mesh(mesh.devices.reshape(items, rows // M, M), ("items", "times", "ring"))
    whole = ("items", "times", "ring")
    rows_of = ("times", "ring")
    return jax.shard_map(
        shards,
        mesh=fine,
        in_specs=(
            P("items", rows_of, None),
            P("items", None, None),
            P("items", None, None, None),
            P("items", rows_of, None),
            P("items", None),
            P(whole, None),
            P(whole, None),
            P(whole, None),
            P(whole, None),
            P(whole, None),
            P(whole, None),
            P(whole),
            P(None, whole),
            P(),
            P("items", rows_of, None),
        ),
        out_specs=(
            P("items", rows_of, None),
            P("items", rows_of, None),
            P(whole, None),
            P(whole, None),
            P(whole, None),
            P(whole, None),
            P(whole, None),
            P(whole, None),
            P(whole),
            P(None, whole),
            P(),
        ),
        check_vma=False,
    )
```

time: 727 us -> 644 us (0.89)
  Pallas kernels: 509 us -> 568 us
  other arithmetic: 75.9 us -> 18.8 us
  matrix products: 42.2 us -> 1.73 us
  local copies, waits for them, and re-layouts: 81.4 us -> 41.9 us
    pallas_call x17 -> x5, Pallas kernels: 509 us -> 568 us  [the longest x1 195 us: feed_forward(): pl.pallas_call(kernel, out_shape=[jax.ShapeDtypeStruct((TOK, D), f32), ja...]
    dot_general x18 -> x1, matrix products: 42.2 us -> 1.73 us  [shards(): jnp.einsum('fc,fd->cd', silu_both[:, :a_rows], d_mod_all, precision=highest)]
    reduce_sum x33 -> x4, other arithmetic: 32.6 us -> 4.75 us  [the longest x3 4.63 us: add(): return jnp.sum(parts.astype(f32), axis=axis)]
    unnamed x252 -> x57, local copies, waits for them, and re-layouts: 30.5 us -> 13.8 us
  transfers between devices with their start and end apart: 2 -> 2, of which waited for: 0 -> 0; matrix products, arithmetic and copies ran while one was open for 8% -> 6% of each run, Pallas kernels for 7% -> 10%
where the time goes in v3:
time: 644 us; the launch traced here: 637 us
  Pallas kernels  568 us (88%)
  local copies, waits for them, and re-layouts  41.9 us (7%)
  other arithmetic  18.8 us (3%)
    pallas_call x1, Pallas kernels, feed_forward(): pl.pallas_call(kernel, out_shape=[jax.ShapeDtypeStruct((TOK, D), f32), ja...  195 us
    pallas_call x1, Pallas kernels, attention_backward(): pl.pallas_call(kernel, out_shape=[jax.ShapeDtypeStruct((TOK, D), f32), ja...  165 us
    pallas_call x1, Pallas kernels, attention_forward(): pl.pallas_call(kernel, out_shape=[jax.ShapeDtypeStruct((ROWS, WIDE), bf16...  113 us
    pallas_call x1, Pallas kernels, prologue(): pl.pallas_call(kernel, out_shape=[jax.ShapeDtypeStruct((plan.rows, 8, 128...  63.7 us
    pallas_call x1, Pallas kernels, finish(): pl.pallas_call(kernel, out_shape=[jax.ShapeDtypeStruct((devices, 16, 128)...  30.8 us
    unnamed x57, local copies, waits for them, and re-layouts  13.8 us
  transfers between devices with their start and end apart: 2, of which 0 were waited for; matrix products, arithmetic and copies ran while one was open for 6% of the time, Pallas kernels for 10%

profile of v3, /device:TPU:0, one launch (start us, length us, event | category | flops | bytes accessed | tf_op | source)
XLA Modules:
  0.0 637.3 jit_solution(13121108480553448357)
XLA Ops:
  0.7 1.6 collective-permute-start
  3.0 1.5 copy.94
  7.2 63.7 %prologue.1 = (f32[16,8,128]{2,1,0:T(8,128)S(1)}, f32[8,128]{1,0:T(8,128)S(1)}, f32[4,8,8,128]{3,2,1,0:T(8,128)S(1)}, bf16[2,8,48,576]{3,2,1,0:T(8,128)(2,1)S(1)...) custom-call(f32[2,8,128]{2,1,0:T(8,128)S(1)} %select_maximum_fusion.refs_0_, ...), custom_call_target="tpu_custom_call" | custom-call | tf_op jit(solution)/shard_map/prologue/pallas_call | solution.py:637
  81.3 2.3 select_convert_fusion.refs_12_.refs_2_
  84.5 3.2 fusion.3
  93.0 112.9 %attention_forward.1 = (bf16[1024,256]{1,0:T(8,128)(2,1)}, f32[1024,256]{1,0:T(8,128)}, f32[1024,256]{1,0:T(8,128)}, bf16[1024,1536]{1,0:T(8,128)(2,1)}, bf16[10...) custom-call(f32[128,1536]{1,0:T(8,128)} %bitcast.143, ...), custom_call_target="tpu_custom_call" | custom-call | tf_op jit(solution)/shard_map/attention_forward/pallas_call | solution.py:888
  205.9 2.0 pad.39.refs_1_
  207.9 195.1 %feed_forward.1 = (f32[128,1536]{1,0:T(8,128)}, f32[128,1536]{1,0:T(8,128)}, bf16[1024,256]{1,0:T(8,128)(2,1)}, bf16[256,1536]{1,0:T(8,128)(2,1)}, bf16[768,512]...) custom-call(bf16[1024,256]{1,0:T(8,128)(2,1)} %get-tuple-element.56., ...), custom_call_target="tpu_custom_call" | custom-call | tf_op jit(solution)/shard_map/feed_forward/pallas_call | solution.py:1685
  403.0 1.9 slice.95
  404.9 165.4 %attention_backward.1 = (f32[128,1536]{1,0:T(8,128)}, f32[8,1536]{1,0:T(8,128)}, f32[8,256]{1,0:T(8,128)}, bf16[384,576]{1,0:T(8,128)(2,1)}, bf16[1024,384]{1,0:...) custom-call(bf16[1024,256]{1,0:T(8,128)(2,1)} %get-tuple-element.61., ...), custom_call_target="tpu_custom_call" | custom-call | tf_op jit(solution)/shard_map/attention_backward/pallas_call | solution.py:1279
  573.5 1.4 convert_reduce_fusion.1
  575.1 1.4 convert_reduce_fusion
  579.0 30.8 %finish.1 = (f32[32,16,128]{2,1,0:T(8,128)S(1)}, bf16[8,48,576]{2,1,0:T(8,128)(2,1)S(1)}, bf16[8,128,384]{2,1,0:T(8,128)(2,1)S(1)}) custom-call(f32[4,8,16,128]{3,2,1,0:T(8,128)S(1)} %pad_maximum_fusion.refs_0_, bf16[8,48,576]{2,1,0:T(8,128)(2,1)S(1)} %bitcast.139, bf16[8,128,384]{2,1,0:T(8,128)(2,1)S(1)} %bitcast.138), custom_call_target="tpu_custom_call" | custom-call | tf_op jit(solution)/shard_map/finish/pallas_call | solution.py:1409
  610.4 1.9 convert_reduce_fusion.2
  612.3 3.9 collective-permute-start.1
  616.2 1.5 maximum_bitcast_fusion
  618.5 2.3 copy.114
  620.8 2.0 copy.135
  622.9 1.4 copy.112
  624.4 1.5 copy.113
  625.9 1.6 copy.118
  628.9 1.3 reshape.355
  630.9 1.7 fusion.19
  634.4 1.7 copy.148
  (165 shorter events, 31.7 us)
Async XLA Ops:
  0.6 76.1 %copy-start = (s32[1,2]{1,0:T(1,128)S(1)}, s32[1,2]{1,0:T(1,128)}, u32[]{:S(2)}) copy-start(s32[1,2]{1,0:T(1,128)} %param.25) | copy-start | bytes 28
  0.7 91.7 %collective-permute-start = (bf16[48,1536]{1,0:T(8,128)(2,1)}, bf16[48,1536]{1,0:T(8,128)(2,1)S(1)}, u32[]{:S(2)}, u32[]{:S(2)}) collective-permute-start(bf16[48,1536]{1,0:T(8,128)(2,1)} %param.28), channel_id=1, source_target_pairs={{0,0},{1,8},{2,16},{3,24},{4,1},{5,9},{6,17},{7,25},{8,2},{9,10},{... | collective-permute-start | bytes 442376 | tf_op jit(solution)/shard_map/ppermute | solution.py:1798
  4.5 1.0 copy-start.12
  5.9 1.0 copy-start.17
  6.0 1.0 copy-start.18
  6.0 1.0 copy-start.19
  6.0 1.2 copy-start.6
  7.2 69.5 %copy-start.20 = (bf16[24]{0:T(256)(128)(2,1)S(1)}, bf16[24]{0:T(256)(128)(2,1)}, u32[]{:S(2)}) copy-start(bf16[24]{0:T(256)(128)(2,1)} %param.34) | copy-start | bytes 148
  7.2 69.6 %copy-start.8 = (bf16[48,8192]{1,0:T(8,128)(2,1)S(1)}, bf16[48,8192]{1,0:T(8,128)(2,1)}, u32[]{:S(2)}) copy-start(bf16[48,8192]{1,0:T(8,128)(2,1)} %param.29) | copy-start | bytes 2359300
  70.9 1.1 copy-start.2
  72.0 0.9 copy-start.3
  77.0 0.7 copy-start.15
  77.4 1.5 copy-start.16
  92.4 0.7 copy-start.13
  404.9 168.5 %copy-start.14 = (f32[16,1536]{1,0:T(8,128)S(1)}, f32[16,1536]{1,0:T(8,128)}, u32[]{:S(2)}) copy-start(f32[16,1536]{1,0:T(8,128)} %get-tuple-element.81) | copy-start | bytes 294916
  576.5 2.5 copy-start.4
  576.5 2.5 copy-start.5
  579.0 37.2 %copy-start.7 = (f32[1,8,48,4,128]{4,3,2,1,0:T(4,128)S(1)}, f32[1,8,48,4,128]{4,3,2,1,0:T(4,128)}, u32[]{:S(2)}) copy-start(f32[1,8,48,4,128]{4,3,2,1,0:T(4,128)} %stack.34) | copy-start | bytes 2359300
  612.3 20.4 %collective-permute-start.1 = (f32[48,1536]{1,0:T(8,128)}, f32[48,1536]{1,0:T(8,128)}, u32[]{:S(2)}, u32[]{:S(2)}) collective-permute-start(f32[48,1536]{1,0:T(8,128)} %convert_reduce_fusion.2), channel_id=1, source_target_pairs={{0,0},{8,1},{16,2},{24,3},{1,4},{9,5},{17,6},{25,7},{2,8},{10,9},{... | collective-permute-start | bytes 884744 | tf_op jit(solution)/shard_map/ppermute | solution.py:1973
  628.9 3.7 copy-start.10
  630.3 3.3 copy-start.11
  632.7 3.5 copy-start.9
  632.7 4.4 copy-start.1

commit v4 on v3

--- a/solution.py
+++ b/solution.py
@@ -314,15 +314,14 @@
             source=source,
         )
 
-    def times_of_ring(self, source):
-        shape = source.shape
+    def times_of_ring(self, x):
+        shape = x.shape
         return Job(
-            source,
+            x,
             (shape[1], shape[0]) + tuple(shape[2:]),
             self.time,
             lambda dest: (slice(None), dest[1]),
             lambda sender: (sender[1],),
-            source=source,
         )
 
     def scatter_time(self, x):
@@ -499,51 +498,79 @@
     return pl.ds(pl.multiple_of(index * count, count), count)
 
 
+ASIDE, ABOVE = (0, 0, 2), (0, 0, 4)
+
+
 def ring_sum(plan, link, me, buffers, product, meanwhile=lambda: None):
     to_mate, from_mate, to_chip, from_chip, part = buffers
     core, chip = me[2] % 2, me[2] // 2
     mates = [link(to_mate.at[d], from_mate.at[d], plan.mate) for d in range(4)]
-    chips = [link(to_chip.at[d - 1], from_chip.at[d - 1], (0, 0, 2 * d)) for d in (1, 2, 3)]
-    for d in (3, 2, 1, 0):
+    across = link(to_chip.at[2], from_chip.at[2], ASIDE)
+    aside = link(to_chip.at[0], from_chip.at[0], ASIDE)
+    above = link(to_chip.at[1], from_chip.at[1], ABOVE)
+    for d in (3, 1, 2, 0):
         to_mate[d] = product((chip ^ d) * 2 + 1 - core).astype(bf16)
         mates[d].start()
-    for d in (3, 2, 1):
-        part[...] = product((chip ^ d) * 2 + core)
+
+    def both_cores(d):
+        total = product((chip ^ d) * 2 + core)
         mates[d].wait_recv()
-        to_chip[d - 1] = (part[...] + from_mate[d].astype(f32)).astype(bf16)
-        chips[d - 1].start()
-    part[...] = product(chip * 2 + core)
-    mates[0].wait_recv()
-    part[...] = part[...] + from_mate[0].astype(f32)
+        return total + from_mate[d].astype(f32)
+
+    to_chip[2] = both_cores(3).astype(bf16)
+    across.start()
+    to_chip[0] = both_cores(1).astype(bf16)
+    aside.start()
+    part[...] = both_cores(2)
+    across.wait_recv()
+    to_chip[1] = (part[...] + from_chip[2].astype(f32)).astype(bf16)
+    above.start()
+    part[...] = both_cores(0)
     meanwhile()
-    for copy in chips:
-        copy.wait_recv()
-    part[...] = part[...] + (from_chip[0].astype(f32) + from_chip[1].astype(f32) + from_chip[2].astype(f32))
-    for copy in mates + chips:
+    aside.wait_recv()
+    above.wait_recv()
+    part[...] = part[...] + (from_chip[0].astype(f32) + from_chip[1].astype(f32))
+    for copy in mates + [across, aside, above]:
         copy.wait_send()
 
 
-def ring_gather(plan, link, me, all_ref, each, meanwhile=lambda: None):
+def ring_gather(plan, link, me, all_ref, each, meanwhile=lambda: None, ready=lambda: None):
     ring = me[2]
     chip = ring // 2
-    own = all_ref.at[rows_at(ring, TOK)]
-    first = [link(own, own, plan.mate)] + [link(own, own, (0, 0, 2 * d)) for d in (1, 2, 3)]
-    for copy in first[1:] + first[:1]:
+
+    def block(place):
+        return all_ref.at[rows_at(place, TOK)]
+
+    mate = link(block(ring), block(ring), plan.mate)
+    aside = link(block(ring), block(ring), ASIDE)
+    above = link(block(ring), block(ring), ABOVE)
+    for copy in (above, aside, mate):
         copy.start()
     meanwhile()
-    first[0].wait_recv()
+    later = []
+
+    def hand_over(place):
+        later.append(link(block(place), block(place), plan.mate))
+        later[-1].start()
+
+    above.wait_recv()
+    onward = link(block(ring ^ 4), block(ring ^ 4), ASIDE)
+    onward.start()
+    hand_over(ring ^ 4)
+    aside.wait_recv()
+    hand_over(ring ^ 2)
+    ready()
+    mate.wait_recv()
     each(chip)
-    later = []
-    for d in (1, 2, 3):
-        first[d].wait_recv()
-        block = all_ref.at[rows_at(ring ^ (2 * d), TOK)]
-        copy = link(block, block, plan.mate)
-        copy.start()
-        later.append(copy)
-    for d in (1, 2, 3):
-        later[d - 1].wait_recv()
-        each(chip ^ d)
-    for copy in first + later:
+    later[0].wait_recv()
+    each(chip ^ 2)
+    later[1].wait_recv()
+    each(chip ^ 1)
+    onward.wait_recv()
+    hand_over(ring ^ 6)
+    later[2].wait_recv()
+    each(chip ^ 3)
+    for copy in [mate, aside, above, onward] + later:
         copy.wait_send()
 
 
@@ -615,6 +642,7 @@
             dest = flip(me, mask)
             copies.append(link(send_ref.at[mask[0], dest[1] * M + dest[2]], recv_ref.at[i], mask))
             copies[-1].start()
+        moves.chain()
         place = me[1] * M + me[2]
         total = send_ref[0, place]
         for i, copy in enumerate(copies):
@@ -685,13 +713,15 @@
     others = len(plan.time)
     out_job = plan.gather_time(out_shard)
     gate_job = plan.scatter_ring(gate_send)
+    gate_time = plan.gather_time_source(gate_job)
     jobs = [
         plan.stack_item(qkv_time),
         out_job,
         plan.swap_source(out_job),
         gate_job,
         plan.scatter_ring(up_send),
-        plan.gather_time_source(gate_job),
+        gate_time,
+        plan.swap_source(gate_time),
     ]
     moves = Transfers(jobs)
     n_in, n_out = len(moves.sent), len(moves.jobs)
@@ -734,13 +764,14 @@
         text_copies = [link(text_part, text_far.at[i], mask) for i, mask in enumerate(plan.time)]
 
         def text_projection():
-            moves.start(late=(3, 4))
+            moves.start(late=(4,))
             for copy in loads:
                 copy.wait()
-            text_wide = jnp.dot(text_w[...], text_mix_ref[...], preferred_element_type=f32).astype(bf16)
-            text_part[...] = jnp.dot(own_caps[...], text_wide, preferred_element_type=f32).astype(bf16)
+            text_part[...] = jnp.dot(own_caps[...], text_w[...], preferred_element_type=f32).astype(bf16)
             for copy in text_copies:
                 copy.start()
+
+        def weights_here():
             moves.take(0)
             copy = pltpu.make_async_copy(outs[0], raw_w, local_sem.at[0])
             copy.start()
@@ -751,17 +782,16 @@
             where = rows_at(which, chip_rows)
             raw_ref[where, :] = jnp.dot(attn_all[where, :], weight_ref[...], preferred_element_type=f32)
 
-        ring_gather(plan, link, me, attn_all, project, text_projection)
-        moves.start_job(3)
+        ring_gather(plan, link, me, attn_all, project, text_projection, weights_here)
         moves.start_job(4)
-        moves.chain(late=(5,))
+        moves.chain(late=(6,))
 
         total = text_part[...].astype(f32)
         for i, copy in enumerate(text_copies):
             copy.wait_recv()
             total = total + text_far[i].astype(f32)
-        text_raw[...] = total
-        q_raw, k_raw, t_raw = raw_ref[:, :WIDE], raw_ref[:, WIDE : 2 * WIDE], total[:, :WIDE]
+        text_raw[...] = jnp.dot(total, text_mix_ref[...].astype(f32), precision=highest, preferred_element_type=f32)
+        q_raw, k_raw, t_raw = raw_ref[:, :WIDE], raw_ref[:, WIDE : 2 * WIDE], text_raw[:, :WIDE]
         squares = [fold_rows(q_raw * q_raw), fold_rows(k_raw * k_raw), fold_rows(t_raw * t_raw)]
         if folded_rows > folded:
             squares.append(jnp.zeros((folded_rows - folded, 128), f32))
@@ -803,6 +833,7 @@
         key_copies = [link(packed_ref, far_ref.at[i], mask) for i, mask in enumerate(plan.time)]
         for copy in key_copies:
             copy.start()
+        moves.chain()
         first = text_raw[:, :128] * tinv_ref[...]
         second = text_raw[:, 128:256] * tinv_ref[...]
         tn_ref[:, :128], tn_ref[:, 128:] = first, second
@@ -869,8 +900,6 @@
         segment(ROWS, True, self_ref)
         for i, mask in enumerate(plan.time):
             key_copies[i].wait_recv()
-            if i == others - 1:
-                moves.chain()
             far = time ^ mask[1]
             packed_out[far] = far_ref[i]
             widen(far_ref.at[i], feature_ref[rows_at(far, ROWS), :], key_ref, value_ref, ROWS)
@@ -915,8 +944,8 @@
             pltpu.VMEM((D, 3 * WIDE), bf16),
             pltpu.VMEM((ROWS, 3 * WIDE), f32),
             pltpu.VMEM((text_rows, text_deep), bf16),
-            pltpu.VMEM((text_rows, 2 * WIDE), bf16),
-            pltpu.VMEM((max(others, 1), text_rows, 2 * WIDE), bf16),
+            pltpu.VMEM((text_rows, 2 * LOCAL), bf16),
+            pltpu.VMEM((max(others, 1), text_rows, 2 * LOCAL), bf16),
             pltpu.VMEM((text_rows, 2 * WIDE), f32),
             pltpu.VMEM((M, folded_rows, 128), f32),
             pltpu.SemaphoreType.DMA((links,)),
@@ -986,7 +1015,7 @@
     text_rows = text_packed.shape[0]
     gate_job = plan.scatter_time(gate_sum)
     up_job = plan.ring_of_times(up_sum)
-    jobs = [gate_job, plan.ring_of_times(None, gate_job), up_job, plan.times_of_ring(up_job), plan.scatter_span(grad_out)]
+    jobs = [gate_job, plan.ring_of_times(None, gate_job), up_job, plan.scatter_span(grad_out)]
     moves = Transfers(jobs)
     n_in, n_out = len(moves.sent), len(moves.jobs)
     block = 256
@@ -1022,7 +1051,7 @@
         greet(me, moves.peers() | set(plan.time) | set(plan.ring) | {plan.item})
         link = Links(me, send_sem, recv_sem)
         moves.bind(me, ins, outs, refs[37:])
-        moves.start()
+        moves.start(late=(3,))
         loads = []
         for i in range(GROUPS):
             where = pl.ds(pl.multiple_of((i * plan.times + time) * span, span), span)
@@ -1104,7 +1133,7 @@
             segment(ROWS, i == 0, dk_ref, dv_ref, 0.125)
             pack(dk_ref[:, :128], dk_ref[:, 128:], dv_ref[:, :128], dv_ref[:, 128:], to_ref.at[i], ROWS)
             far_copies[i].start()
-        moves.chain(late=(3,))
+        moves.chain()
         bring(time)
         segment(ROWS, others == 0, dk_ref, dv_ref, 0.125)
         prepare(cross_ref)
@@ -1125,6 +1154,8 @@
             dv_ref[:, :128] += v_first
             dv_ref[:, 128:] += v_second
 
+        moves.start_job(3)
+
         def unturn(d_all, hat_ref, gain_row):
             pieces = []
             for at in range(ROWS // block):
@@ -1167,7 +1198,6 @@
             wide = jnp.concatenate([dq_ref[where, :], dk_ref[where, :], values], axis=1).astype(bf16)
             du_ref[where, :] = lax.dot_general(wide, mix_ref[...], turned, preferred_element_type=f32).astype(bf16)
 
-        grad_qkv[...] = lax.dot_general(attn_ref[...], du_ref[...], sunk, preferred_element_type=f32).astype(bf16)
         away = 1 - item
 
         def part(i, t, which):
@@ -1182,11 +1212,11 @@
         a_times = [link(a_sum.at[time ^ mask[1]], a_time.at[k], mask) for k, mask in enumerate(plan.time)]
         b_items = [link(b_sum.at[away], b_item, plan.item)]
         text_items = [link(grad_text.at[rows_at(away, span)], text_item, plan.item)]
-        for copy in a_items + b_times:
-            copy.start()
-        moves.chain()
 
         def meanwhile():
+            grad_qkv[...] = lax.dot_general(attn_ref[...], du_ref[...], sunk, preferred_element_type=f32).astype(bf16)
+            for copy in a_items + b_times:
+                copy.start()
             for i, copy in enumerate(text_copies):
                 copy.wait_recv()
                 k_first, k_second, v_first, v_second = unpack(tfrom_ref.at[i], text_rows)
@@ -1426,7 +1456,7 @@
 
 
 def feed_forward(
-    plan, mixed, out_full, latents, cotangent, modulation, gains, first_rows, gate_time, up_shard, down_weight
+    plan, mixed, out_full, latents, cotangent, modulation, gains, first_rows, gate_full, up_shard, down_weight
 ):
     d_rows = down_weight.shape[0]
     width = plan.sets * d_rows
@@ -1434,7 +1464,7 @@
     up_job = plan.stack_time(up_shard)
     down_job = plan.stack_time(down_weight)
     moves = Transfers(
-        [plan.stack_item(gate_time), up_job, plan.stack_item(up_shard, up_job), down_job, plan.stack_item(down_weight, down_job)]
+        [up_job, plan.stack_item(up_shard, up_job), down_job, plan.stack_item(down_weight, down_job)]
     )
     n_in, n_out = len(moves.sent), len(moves.jobs)
     turned = (((1,), (1,)), ((), ()))
@@ -1446,83 +1476,31 @@
     slab = plan.times * d_rows
 
     def kernel(*refs):
-        (mixed_ref, out_w, latent_ref, cot_ref, mod_ref, gain_ref, first_ref) = refs[:7]
-        ins = refs[7 : 7 + n_in]
-        refs = refs[7 + n_in :]
+        (mixed_ref, out_w, latent_ref, cot_ref, mod_ref, gain_ref, first_ref, gate_w) = refs[:8]
+        ins = refs[8 : 8 + n_in]
+        refs = refs[8 + n_in :]
         (result_ref, d_state_ref, d_mixed_ref, grad_out_ref, gate_sum_ref, up_sum_ref, down_grad_ref, sums_ref) = refs[:8]
         outs = refs[8 : 8 + n_out]
         refs = refs[8 + n_out :]
-        (gate_w, up_w, down_w, ffn_all, down_all, proj_all, gate_ref, up_ref, act_ref, d_gate_ref, d_up_ref) = refs[:11]
-        (grad_gate, grad_up, grad_down, from_gate, from_up, from_down, down_sum, from_time) = refs[11:19]
+        (up_w, down_w, ffn_all, down_all, proj_all, gate_ref, up_ref, act_ref, d_gate_ref, d_up_ref) = refs[:10]
+        (grad_gate, grad_up, grad_down, from_gate, from_up, from_down, down_sum, from_time) = refs[10:18]
         (to_mate, from_mate, to_chip, from_chip, part, proj_ref, state_ref, own_ref, send_sem, recv_sem, local_sem) = refs[
-            19:30
+            18:29
         ]
         me = here()
         item, time, ring = me
         core, chip = ring % 2, ring // 2
         greet(me, moves.peers() | {plan.mate, plan.item} | set(plan.chips) | set(plan.time))
-        moves.bind(me, ins, outs, refs[30:])
-        moves.start()
-        used = [0]
-
-        def link(src, dst, mask):
-            slot = used[0]
-            used[0] += 1
-            return pltpu.make_async_remote_copy(
-                src_ref=src,
-                dst_ref=dst,
-                send_sem=send_sem.at[slot],
-                recv_sem=recv_sem.at[slot],
-                device_id=flip(me, mask),
-                device_id_type=MESH,
-            )
-
-        def rows_at(index, count):
-            return pl.ds(pl.multiple_of(index * count, count), count)
+        moves.bind(me, ins, outs, refs[29:])
+        moves.start(late=(2,))
+        link = Links(me, send_sem, recv_sem)
+        buffers = (to_mate, from_mate, to_chip, from_chip, part)
 
         def scatter(product, meanwhile=lambda: None):
-            mates = [link(to_mate.at[d], from_mate.at[d], plan.mate) for d in range(4)]
-            chips = [link(to_chip.at[d - 1], from_chip.at[d - 1], (0, 0, 2 * d)) for d in (1, 2, 3)]
-            for d in (3, 2, 1, 0):
-                to_mate[d] = product((chip ^ d) * 2 + 1 - core).astype(bf16)
-                mates[d].start()
-            for d in (3, 2, 1):
-                part[...] = product((chip ^ d) * 2 + core)
-                mates[d].wait_recv()
-                to_chip[d - 1] = (part[...] + from_mate[d].astype(f32)).astype(bf16)
-                chips[d - 1].start()
-            part[...] = product(chip * 2 + core)
-            mates[0].wait_recv()
-            part[...] = part[...] + from_mate[0].astype(f32)
-            meanwhile()
-            for copy in chips:
-                copy.wait_recv()
-            part[...] = part[...] + (
-                from_chip[0].astype(f32) + from_chip[1].astype(f32) + from_chip[2].astype(f32)
-            )
-            for copy in mates + chips:
-                copy.wait_send()
-
-        def gather(all_ref, each, meanwhile=lambda: None):
-            own = all_ref.at[rows_at(ring, TOK)]
-            first = [link(own, own, plan.mate)] + [link(own, own, (0, 0, 2 * d)) for d in (1, 2, 3)]
-            for copy in first[1:] + first[:1]:
-                copy.start()
-            meanwhile()
-            first[0].wait_recv()
-            each(chip)
-            later = []
-            for d in (1, 2, 3):
-                first[d].wait_recv()
-                block = all_ref.at[rows_at(ring ^ (2 * d), TOK)]
-                copy = link(block, block, plan.mate)
-                copy.start()
-                later.append(copy)
-            for d in (1, 2, 3):
-                later[d - 1].wait_recv()
-                each(chip ^ d)
-            for copy in first + later:
-                copy.wait_send()
+            ring_sum(plan, link, me, buffers, product, meanwhile)
+
+        def gather(all_ref, each, meanwhile=lambda: None, ready=lambda: None):
+            ring_gather(plan, link, me, all_ref, each, meanwhile, ready)
 
         is_first = first_ref[...] > 0.5
 
@@ -1551,8 +1529,11 @@
         def out_product(block):
             return jnp.dot(mixed_ref[rows_at(block, TOK), :], out_w[...], preferred_element_type=f32)
 
-        scatter(out_product)
-        moves.chain(late=(4,))
+        def next_weights():
+            moves.chain(late=(3,))
+            moves.start_job(2)
+
+        scatter(out_product, next_weights)
         proj_ref[...] = part[...]
         proj = proj_ref[...]
         gate_attn = jnp.tanh(modulated(1))
@@ -1571,13 +1552,11 @@
             act_ref[rows, :] = (gate * (1.0 / (1.0 + jnp.exp(-gate))) * up).astype(bf16)
 
         def weights_here():
-            load(0, gate_w)
-            load(2, up_w)
-            moves.chain()
-
-        gather(ffn_all, forward_chip, weights_here)
-
-        load(4, down_w)
+            load(1, up_w)
+
+        gather(ffn_all, forward_chip, moves.chain, weights_here)
+
+        load(3, down_w)
 
         def down_product(block):
             return jnp.dot(act_ref[rows_at(block, TOK), :], down_w[...], preferred_element_type=f32)
@@ -1616,8 +1595,9 @@
             grad_down[...] = lax.dot_general(act_ref[...], down_all[...], sunk, preferred_element_type=f32).astype(bf16)
             down_link.start()
 
+        down_gradient()
+
         def gate_gradients():
-            down_gradient()
             grad_gate[...] = lax.dot_general(ffn_all[...], d_gate_ref[...], sunk, preferred_element_type=f32).astype(bf16)
             gate_link.start()
             grad_up[...] = lax.dot_general(ffn_all[...], d_up_ref[...], sunk, preferred_element_type=f32).astype(bf16)
@@ -1664,7 +1644,7 @@
                 proj_all[rows, :], out_w[...], turned, preferred_element_type=f32
             ).astype(bf16)
 
-        gather(proj_all, mixed_chip, down_time)
+        gather(proj_all, mixed_chip, ready=down_time)
         grad_out_ref[...] = lax.dot_general(mixed_ref[...], proj_all[...], sunk, preferred_element_type=f32).astype(bf16)
         gate_link.wait_recv()
         gate_sum_ref[...] = (
@@ -1695,10 +1675,9 @@
             jax.ShapeDtypeStruct((16, D), f32),
         ]
         + moves.out_shapes(),
-        in_specs=[VMEM] * 7 + [ANY] * n_in,
+        in_specs=[VMEM] * 8 + [ANY] * n_in,
         out_specs=[VMEM] * 8 + [ANY] * n_out,
         scratch_shapes=[
-            pltpu.VMEM((D, width), bf16),
             pltpu.VMEM((D, width), bf16),
             pltpu.VMEM((width, D), bf16),
             pltpu.VMEM((ROWS, D), bf16),
@@ -1732,7 +1711,7 @@
         + moves.scratch(),
         name="feed_forward",
         compiler_params=params(plan, 60),
-    )(mixed, out_full, latents, cotangent, modulation, gains, first_rows, *moves.operands())
+    )(mixed, out_full, latents, cotangent, modulation, gains, first_rows, gate_full, *moves.operands())
     return result[:8]
 
 
@@ -1860,7 +1839,7 @@
 
     inputs = latents[0]
     caption_rows = captions[0].reshape(FRAMES * TEXT, TEXT_DIM)
-    forward, (qkv_full, _, out_full, _, up_shard, gate_time) = attention_forward(
+    forward, (qkv_full, _, out_full, _, up_shard, _, gate_full) = attention_forward(
         plan,
         inputs,
         modulation,
@@ -1894,12 +1873,12 @@
         modulation,
         gains,
         first_rows,
-        gate_time.reshape(times * M * k_rows, sets * d_rows),
+        gate_full.reshape(D, sets * d_rows),
         up_shard.reshape(M * k_rows, sets * d_rows),
         down_weight,
     )
     ring_shape = (times, M, k_rows, sets * d_rows)
-    (grad_latent, attn_sums, wide_sums, qkv_sum, text_sum), (_, gate_parts, _, up_parts, out_parts) = attention_backward(
+    (grad_latent, attn_sums, wide_sums, qkv_sum, text_sum), (_, gate_parts, up_pieces, out_parts) = attention_backward(
         plan,
         query,
         packed_all,
@@ -1952,10 +1931,11 @@
     d_gains = d_gains.reshape(8, gain_tiles, 128).transpose(1, 0, 2)
     d_gains = jnp.pad(d_gains, ((0, devices - gain_tiles), (0, 0), (0, 0)))
     small = jnp.concatenate([d_mod, d_gains], axis=1).reshape(sets, M, 16, 128)
-    small_all, (qkv_pieces, text_pieces) = finish(
+    small_all, (up_parts, qkv_pieces, text_pieces) = finish(
         plan,
         small,
         [
+            plan.times_of_ring(up_pieces),
             plan.scatter_ring(qkv_sum.reshape(M, k_rows, 3 * LOCAL)),
             plan.scatter_ring(text_sum.reshape(M, t_rows, 2 * LOCAL)),
         ],

time: 644 us -> 591 us (0.918)
  Pallas kernels: 568 us -> 519 us
    pallas_call x1, Pallas kernels: 165 us -> 137 us  [attention_backward(): pl.pallas_call(kernel, out_shape=[jax.ShapeDtypeStruct((TOK, D), f32), ja...]
    pallas_call x1, Pallas kernels: 195 us -> 170 us  [feed_forward(): pl.pallas_call(kernel, out_shape=[jax.ShapeDtypeStruct((TOK, D), f32), ja...]
    pallas_call x1, Pallas kernels: 30.8 us -> 45.3 us  [finish(): pl.pallas_call(kernel, out_shape=[jax.ShapeDtypeStruct((devices, 16, 128)...]
    unnamed x57 -> x67, local copies, waits for them, and re-layouts: 13.8 us -> 16 us
  transfers between devices with their start and end apart: 2 -> 2, of which waited for: 0 -> 0; matrix products, arithmetic and copies ran while one was open for 6% -> 7% of each run, Pallas kernels for 10% -> 10%
where the time goes in v4:
time: 591 us; the launch traced here: 585 us
  Pallas kernels  519 us (88%)
  local copies, waits for them, and re-layouts  42.1 us (7%)
  other arithmetic  15.3 us (3%)
    pallas_call x1, Pallas kernels, feed_forward(): pl.pallas_call(kernel, out_shape=[jax.ShapeDtypeStruct((TOK, D), f32), ja...  170 us
    pallas_call x1, Pallas kernels, attention_backward(): pl.pallas_call(kernel, out_shape=[jax.ShapeDtypeStruct((TOK, D), f32), ja...  137 us
    pallas_call x1, Pallas kernels, attention_forward(): pl.pallas_call(kernel, out_shape=[jax.ShapeDtypeStruct((ROWS, WIDE), bf16...  108 us
    pallas_call x1, Pallas kernels, prologue(): pl.pallas_call(kernel, out_shape=[jax.ShapeDtypeStruct((plan.rows, 8, 128...  58 us
    pallas_call x1, Pallas kernels, finish(): pl.pallas_call(kernel, out_shape=[jax.ShapeDtypeStruct((devices, 16, 128)...  45.3 us
    unnamed x67, local copies, waits for them, and re-layouts  16 us
  transfers between devices with their start and end apart: 2, of which 0 were waited for; matrix products, arithmetic and copies ran while one was open for 7% of the time, Pallas kernels for 10%

profile of v4, /device:TPU:0, one launch (start us, length us, event | category | flops | bytes accessed | tf_op | source)
XLA Modules:
  0.0 584.8 jit_solution(14937682632419269891)
XLA Ops:
  0.7 1.6 collective-permute-start
  3.0 1.5 copy.94
  7.2 58.0 %prologue.1 = (f32[16,8,128]{2,1,0:T(8,128)S(1)}, f32[8,128]{1,0:T(8,128)S(1)}, f32[4,8,8,128]{3,2,1,0:T(8,128)S(1)}, bf16[2,8,48,576]{3,2,1,0:T(8,128)(2,1)S(1)...) custom-call(f32[2,8,128]{2,1,0:T(8,128)S(1)} %select_maximum_fusion.refs_0_, ...), custom_call_target="tpu_custom_call" | custom-call | tf_op jit(solution)/shard_map/prologue/pallas_call | solution.py:665
  65.3 1.1 copy-done.2
  66.4 0.9 copy-done.3
  72.1 1.1 fusion.refs_6_.refs_24_
  75.7 2.3 select_convert_fusion.refs_12_.refs_2_
  78.8 3.2 fusion.3
  87.3 107.5 %attention_forward.1 = (bf16[1024,256]{1,0:T(8,128)(2,1)}, f32[1024,256]{1,0:T(8,128)}, f32[1024,256]{1,0:T(8,128)}, bf16[1024,1536]{1,0:T(8,128)(2,1)}, bf16[10...) custom-call(f32[128,1536]{1,0:T(8,128)} %bitcast.143, ...), custom_call_target="tpu_custom_call" | custom-call | tf_op jit(solution)/shard_map/attention_forward/pallas_call | solution.py:917
  194.9 2.0 pad.39.refs_1_
  196.9 170.2 %feed_forward.1 = (f32[128,1536]{1,0:T(8,128)}, f32[128,1536]{1,0:T(8,128)}, bf16[1024,256]{1,0:T(8,128)(2,1)}, bf16[256,1536]{1,0:T(8,128)(2,1)}, bf16[768,512]...) custom-call(bf16[1024,256]{1,0:T(8,128)(2,1)} %get-tuple-element.57., ...), custom_call_target="tpu_custom_call" | custom-call | tf_op jit(solution)/shard_map/feed_forward/pallas_call | solution.py:1665
  367.1 1.9 slice.95
  369.0 137.5 %attention_backward.1 = (f32[128,1536]{1,0:T(8,128)}, f32[8,1536]{1,0:T(8,128)}, f32[8,256]{1,0:T(8,128)}, bf16[384,576]{1,0:T(8,128)(2,1)}, bf16[1024,384]{1,0:...) custom-call(bf16[1024,256]{1,0:T(8,128)(2,1)} %get-tuple-element.62., ...), custom_call_target="tpu_custom_call" | custom-call | tf_op jit(solution)/shard_map/attention_backward/pallas_call | solution.py:1309
  511.2 45.3 %finish.1 = (f32[32,16,128]{2,1,0:T(8,128)S(1)}, bf16[2,8,48,512]{3,2,1,0:T(8,128)(2,1)S(1)}, bf16[8,48,576]{2,1,0:T(8,128)(2,1)S(1)}, bf16[8,128,384]{2,1,0:T(8,128)(2,1)S(1)}) custom-call(f32[4,8,16,128]{3,2,1,0:T(8,128)S(1)} %pad_maximum_fusion.refs_0_, bf16[8,2,48,512]{3,2,1,0:T(8,128)(2,1)S(1)} %copy-done.5, bf16[8,48,576]{2,1,0:T(8,128)(2,1)S(1)} %bitcast.139, ...), custom_call_target="tpu_custom_call" | custom-call | tf_op jit(solution)/shard_map/finish/pallas_call | solution.py:1439
  557.3 1.1 stack.34
  558.6 1.1 stack.33
  561.1 3.9 collective-permute-start.1
  565.0 1.5 maximum_bitcast_fusion
  568.3 2.0 copy.135
  570.7 1.3 copy.113
  572.0 3.0 copy.118
  576.5 1.3 reshape.355
  578.4 1.7 fusion.19
  582.0 1.7 copy.148
  (175 shorter events, 30.1 us)
Async XLA Ops:
  0.6 70.4 %copy-start = (s32[1,2]{1,0:T(1,128)S(1)}, s32[1,2]{1,0:T(1,128)}, u32[]{:S(2)}) copy-start(s32[1,2]{1,0:T(1,128)} %param.25) | copy-start | bytes 28
  0.7 86.0 %collective-permute-start = (bf16[48,1536]{1,0:T(8,128)(2,1)}, bf16[48,1536]{1,0:T(8,128)(2,1)S(1)}, u32[]{:S(2)}, u32[]{:S(2)}) collective-permute-start(bf16[48,1536]{1,0:T(8,128)(2,1)} %param.28), channel_id=1, source_target_pairs={{0,0},{1,8},{2,16},{3,24},{4,1},{5,9},{6,17},{7,25},{8,2},{9,10},{... | collective-permute-start | bytes 442376 | tf_op jit(solution)/shard_map/ppermute | solution.py:1777
  4.5 1.0 copy-start.17
  5.9 1.0 copy-start.22
  6.0 1.0 copy-start.23
  6.0 1.0 copy-start.24
  6.0 1.2 copy-start.7
  7.2 63.9 %copy-start.25 = (bf16[24]{0:T(256)(128)(2,1)S(1)}, bf16[24]{0:T(256)(128)(2,1)}, u32[]{:S(2)}) copy-start(bf16[24]{0:T(256)(128)(2,1)} %param.34) | copy-start | bytes 148
  7.2 64.0 %copy-start.11 = (bf16[48,8192]{1,0:T(8,128)(2,1)S(1)}, bf16[48,8192]{1,0:T(8,128)(2,1)}, u32[]{:S(2)}) copy-start(bf16[48,8192]{1,0:T(8,128)(2,1)} %param.29) | copy-start | bytes 2359300
  65.2 1.1 copy-start.2
  71.8 1.5 copy-start.21
  369.0 140.8 %copy-start.19 = (f32[16,1536]{1,0:T(8,128)S(1)}, f32[16,1536]{1,0:T(8,128)}, u32[]{:S(2)}) copy-start(f32[16,1536]{1,0:T(8,128)} %get-tuple-element.82) | copy-start | bytes 294916
  506.5 4.7 copy-start.4
  506.5 4.7 copy-start.5
  506.5 4.7 copy-start.6
  557.2 1.3 copy-start.15
  558.5 1.3 copy-start.9
  558.6 1.7 copy-start.16
  559.7 5.3 copy-start.10
  561.1 19.1 %collective-permute-start.1 = (f32[48,1536]{1,0:T(8,128)}, f32[48,1536]{1,0:T(8,128)}, u32[]{:S(2)}, u32[]{:S(2)}) collective-permute-start(f32[48,1536]{1,0:T(8,128)} %convert_reduce_fusion.2), channel_id=1, source_target_pairs={{0,0},{8,1},{16,2},{24,3},{1,4},{9,5},{17,6},{25,7},{2,8},{10,9},{... | collective-permute-start | bytes 884744 | tf_op jit(solution)/shard_map/ppermute | solution.py:1953
  576.4 3.7 copy-start.13
  577.8 3.3 copy-start.14
  580.2 3.5 copy-start.12
  580.2 4.4 copy-start.1
  (4 other events, 3.0 us)

commit v5 on v4

--- a/solution.py
+++ b/solution.py
@@ -442,7 +442,8 @@
     lane = lax.broadcasted_iota(jnp.int32, (rows, 128), 1)
     packed_ref[:, :128] = jnp.where(lane < SPARE, key_first, pltpu.roll(value_first, 32, 1)).astype(bf16)
     packed_ref[:, 128:256] = jnp.where(lane < SPARE, key_second, value_first).astype(bf16)
-    packed_ref[:, 256:] = value_second.astype(bf16)
+    if value_second is not None:
+        packed_ref[:, 256:] = value_second.astype(bf16)
 
 
 def unpack(packed, rows):
@@ -623,7 +624,7 @@
         swap = link(cond_ref.at[1], cond_in, plan.item)
         swap.start()
         moves.bind(me, ins, outs, refs[8:])
-        moves.start()
+        moves.start(late=range(1, n_out))
         deep = ada_ref.shape[0]
         part_ref[0] = jnp.dot(cond_ref[0][:, :deep].astype(bf16), ada_ref[...], preferred_element_type=f32)
         swap.wait_recv()
@@ -642,7 +643,9 @@
             dest = flip(me, mask)
             copies.append(link(send_ref.at[mask[0], dest[1] * M + dest[2]], recv_ref.at[i], mask))
             copies[-1].start()
-        moves.chain()
+        for k, job in enumerate(moves.jobs):
+            if k and job.source is None:
+                moves.start_job(k)
         place = me[1] * M + me[2]
         total = send_ref[0, place]
         for i, copy in enumerate(copies):
@@ -653,7 +656,7 @@
         shares = [link(sum_ref, mod_in.at[place], mask) for mask in group]
         for copy in shares:
             copy.start()
-        moves.forward()
+        moves.chain()
         for copy in shares:
             copy.wait_recv()
         mod_ref[...] = mod_in[...]
@@ -786,6 +789,13 @@
         moves.start_job(4)
         moves.chain(late=(6,))
 
+        packed_ref[:, 256:] = raw_ref[:, 2 * WIDE + 128 :].astype(bf16)
+        value_copies = [
+            link(packed_ref.at[:, 256:], far_ref.at[i, :, 256:], mask) for i, mask in enumerate(plan.time)
+        ]
+        for copy in value_copies:
+            copy.start()
+
         total = text_part[...].astype(f32)
         for i, copy in enumerate(text_copies):
             copy.wait_recv()
@@ -826,11 +836,13 @@
             query_ref[where, 128:] = second.astype(bf16)
             first, second = turn(where, WIDE, kinv_ref, kn_ref, 1)
             values = raw_ref[where, 2 * WIDE :]
-            pack(first, second, values[:, :128], values[:, 128:], packed_ref.at[where, :], block)
+            pack(first, second, values[:, :128], None, packed_ref.at[where, :], block)
             return carry
 
         lax.fori_loop(0, ROWS // block, shape, 0)
-        key_copies = [link(packed_ref, far_ref.at[i], mask) for i, mask in enumerate(plan.time)]
+        key_copies = [
+            link(packed_ref.at[:, :256], far_ref.at[i, :, :256], mask) for i, mask in enumerate(plan.time)
+        ]
         for copy in key_copies:
             copy.start()
         moves.chain()
@@ -900,6 +912,7 @@
         segment(ROWS, True, self_ref)
         for i, mask in enumerate(plan.time):
             key_copies[i].wait_recv()
+            value_copies[i].wait_recv()
             far = time ^ mask[1]
             packed_out[far] = far_ref[i]
             widen(far_ref.at[i], feature_ref[rows_at(far, ROWS), :], key_ref, value_ref, ROWS)
@@ -908,12 +921,12 @@
         lane = lax.broadcasted_iota(jnp.int32, (ROWS, WIDE), 1)
         both = self_ref[...] + gate_ref[...] * cross_ref[...]
         mixed_ref[...] = jnp.where(lane < HEAD, 0.0, both).astype(bf16)
-        for copy in text_copies + shares + key_copies:
+        for copy in text_copies + shares + key_copies + value_copies:
             copy.wait_send()
         moves.finish()
 
     qmask, vmask, _ = lane_masks()
-    links = 7 + (M - 1) + 2 * others
+    links = 7 + (M - 1) + 3 * others
     result = pl.pallas_call(
         kernel,
         out_shape=[
@@ -1455,6 +1468,46 @@
     return result[0], result[1:]
 
 
+def deliver(gate_parts, up_parts, qkv_pieces, text_pieces, whole, sets):
+    times = gate_parts.shape[1]
+    k_rows, wide = gate_parts.shape[2:]
+    unit = wide // sets
+    t_rows = text_pieces.shape[1]
+    n = len(whole)
+
+    def kernel(gate_ref, up_ref, qkv_ref, text_ref, *refs):
+        ins, (gate_up_out, qkv_out, text_out), outs = refs[:n], refs[n : n + 3], refs[n + 3 :]
+        for m in range(M):
+            gate = sum(gate_ref[m, t].astype(f32) for t in range(times))
+            up = sum(up_ref[t, m].astype(f32) for t in range(times))
+            for j in range(sets):
+                at = (j * M + m) * unit
+                gate_up_out[:, at : at + unit] = gate[:, j * unit : (j + 1) * unit]
+                gate_up_out[:, FF + at : FF + at + unit] = up[:, j * unit : (j + 1) * unit]
+            piece = qkv_ref[m].astype(f32)
+            for j in range(3):
+                qkv_out[:, j * D + m * LOCAL : j * D + (m + 1) * LOCAL] = piece[:, j * LOCAL : (j + 1) * LOCAL]
+            piece = text_ref[m].astype(f32)
+            for j in range(2):
+                text_out[:, j * D + m * LOCAL : j * D + (m + 1) * LOCAL] = piece[:, j * LOCAL : (j + 1) * LOCAL]
+        for source, target in zip(ins, outs):
+            target[...] = source[...]
+
+    return pl.pallas_call(
+        kernel,
+        out_shape=[
+            jax.ShapeDtypeStruct((k_rows, 2 * FF), f32),
+            jax.ShapeDtypeStruct((k_rows, 3 * D), f32),
+            jax.ShapeDtypeStruct((t_rows, 2 * D), f32),
+        ]
+        + [jax.ShapeDtypeStruct(x.shape, x.dtype) for x in whole],
+        in_specs=[VMEM] * (4 + n),
+        out_specs=[VMEM] * (3 + n),
+        name="deliver",
+        compiler_params=pltpu.CompilerParams(vmem_limit_bytes=48 * 2**20),
+    )(gate_parts, up_parts, qkv_pieces, text_pieces, *whole)
+
+
 def feed_forward(
     plan, mixed, out_full, latents, cotangent, modulation, gains, first_rows, gate_full, up_shard, down_weight
 ):
@@ -1777,13 +1830,13 @@
     out_shard = lax.ppermute(out_weight, axes, out_forth)
 
     text_job = plan.scatter_ring(text_send)
-    mod_tiles, cond_other, (packages, qkv_time, _, text_full) = prologue(
+    mod_tiles, cond_other, (packages, _, text_full, qkv_time) = prologue(
         plan,
         tiles,
         package,
         cond,
         ada_weight,
-        [plan.scatter_group_ring(qkv_send), text_job, plan.swap_source(text_job)],
+        [text_job, plan.swap_source(text_job), plan.scatter_group_ring(qkv_send)],
     )
     packages = packages.reshape(devices, lines * 128)
     gains = packages[:, : 7 * gain_n].reshape(devices, 7, gain_n).transpose(1, 0, 2).reshape(7, D)
@@ -1951,10 +2004,9 @@
     ada_grad = jnp.einsum("fc,fd->cd", silu_both[:, :a_rows], d_mod_all, precision=highest)
     bias_grad = lax.dynamic_slice_in_dim(jnp.sum(d_mod_all, axis=0), place * bias_n, bias_n)
     out_grad = lax.ppermute(add(out_parts), axes, out_back)
-    qkv_grad = qkv_pieces.reshape(M, k_rows, 3, LOCAL).transpose(1, 2, 0, 3).reshape(k_rows, 3 * D).astype(f32)
-    text_grad = text_pieces.reshape(M, t_rows, 2, LOCAL).transpose(1, 2, 0, 3).reshape(t_rows, 2 * D).astype(f32)
-    gate_up_grad = jnp.stack([add(gate_parts, 1), add(up_parts, 0)]).reshape(2, M, k_rows, sets, d_rows)
-    gate_up_grad = gate_up_grad.transpose(2, 0, 3, 1, 4).reshape(k_rows, 2 * FF)
+    gate_up_grad, qkv_grad, text_grad, result_rows, grad_latent, down_grad = deliver(
+        gate_parts, up_parts, qkv_pieces, text_pieces, [result_rows, grad_latent, down_grad], sets
+    )
     return (
         result_rows[None],
         grad_latent[None],

time: 591 us -> 578 us (0.978)
  local copies, waits for them, and re-layouts: 42.1 us -> 33.1 us
  Pallas kernels: 519 us -> 512 us
    pallas_call x1, Pallas kernels: 58 us -> 50 us  [prologue(): pl.pallas_call(kernel, out_shape=[jax.ShapeDtypeStruct((plan.rows, 8, 128...]
    unnamed x67 -> x68, local copies, waits for them, and re-layouts: 16 us -> 14.4 us
  transfers between devices with their start and end apart: 2 -> 2, of which waited for: 0 -> 0; matrix products, arithmetic and copies ran while one was open for 7% -> 5% of each run, Pallas kernels for 10% -> 9%
where the time goes in v5:
time: 578 us; the launch traced here: 567 us
  Pallas kernels  512 us (89%)
  local copies, waits for them, and re-layouts  33.1 us (6%)
  other arithmetic  13.5 us (2%)
    pallas_call x1, Pallas kernels, feed_forward(): pl.pallas_call(kernel, out_shape=[jax.ShapeDtypeStruct((TOK, D), f32), ja...  170 us
    pallas_call x1, Pallas kernels, attention_backward(): pl.pallas_call(kernel, out_shape=[jax.ShapeDtypeStruct((TOK, D), f32), ja...  138 us
    pallas_call x1, Pallas kernels, attention_forward(): pl.pallas_call(kernel, out_shape=[jax.ShapeDtypeStruct((ROWS, WIDE), bf16...  106 us
    pallas_call x1, Pallas kernels, prologue(): pl.pallas_call(kernel, out_shape=[jax.ShapeDtypeStruct((plan.rows, 8, 128...  50 us
    pallas_call x1, Pallas kernels, finish(): pl.pallas_call(kernel, out_shape=[jax.ShapeDtypeStruct((devices, 16, 128)...  45.3 us
    unnamed x68, local copies, waits for them, and re-layouts  14.4 us
  transfers between devices with their start and end apart: 2, of which 0 were waited for; matrix products, arithmetic and copies ran while one was open for 5% of the time, Pallas kernels for 9%

profile of v5, /device:TPU:0, one launch (start us, length us, event | category | flops | bytes accessed | tf_op | source)
XLA Modules:
  0.0 567.3 jit_solution(6943356273029630075)
XLA Ops:
  0.7 1.6 collective-permute-start
  3.0 1.5 copy.63
  7.2 50.0 %prologue.1 = (f32[16,8,128]{2,1,0:T(8,128)S(1)}, f32[8,128]{1,0:T(8,128)S(1)}, f32[4,8,8,128]{3,2,1,0:T(8,128)S(1)}, bf16[8,128,384]{2,1,0:T(8,128)(2,1)}, bf16...) custom-call(f32[2,8,128]{2,1,0:T(8,128)S(1)} %select_maximum_fusion.refs_0_, ...), custom_call_target="tpu_custom_call" | custom-call | tf_op jit(solution)/shard_map/prologue/pallas_call | solution.py:668
  57.3 1.1 copy-done.2
  58.4 0.9 copy-done.3
  61.6 0.9 select_convert_fusion.1.refs_11_
  64.1 1.1 fusion.refs_6_.refs_24_
  65.2 0.9 fusion.1.refs_7_.refs_25_
  67.7 2.3 select_convert_fusion.refs_12_.refs_2_
  70.8 3.2 fusion.3
  79.3 105.5 %attention_forward.1 = (bf16[1024,256]{1,0:T(8,128)(2,1)}, f32[1024,256]{1,0:T(8,128)}, f32[1024,256]{1,0:T(8,128)}, bf16[1024,1536]{1,0:T(8,128)(2,1)}, bf16[10...) custom-call(f32[128,1536]{1,0:T(8,128)} %bitcast.129, ...), custom_call_target="tpu_custom_call" | custom-call | tf_op jit(solution)/shard_map/attention_forward/pallas_call | solution.py:930
  184.8 2.0 pad.39.refs_1_
  186.8 170.2 %feed_forward.1 = (f32[128,1536]{1,0:T(8,128)}, f32[128,1536]{1,0:T(8,128)}, bf16[1024,256]{1,0:T(8,128)(2,1)}, bf16[256,1536]{1,0:T(8,128)(2,1)}, bf16[768,512]...) custom-call(bf16[1024,256]{1,0:T(8,128)(2,1)} %get-tuple-element.68., ...), custom_call_target="tpu_custom_call" | custom-call | tf_op jit(solution)/shard_map/feed_forward/pallas_call | solution.py:1718
  357.0 1.9 slice.95
  359.0 138.1 %attention_backward.1 = (f32[128,1536]{1,0:T(8,128)}, f32[8,1536]{1,0:T(8,128)}, f32[8,256]{1,0:T(8,128)}, bf16[384,576]{1,0:T(8,128)(2,1)}, bf16[1024,384]{1,0:...) custom-call(bf16[1024,256]{1,0:T(8,128)(2,1)} %get-tuple-element.63., ...), custom_call_target="tpu_custom_call" | custom-call | tf_op jit(solution)/shard_map/attention_backward/pallas_call | solution.py:1322
  501.8 1.1 copy-done.14
  502.8 45.3 %finish.1 = (f32[32,16,128]{2,1,0:T(8,128)S(1)}, bf16[2,8,48,512]{3,2,1,0:T(8,128)(2,1)S(1)}, bf16[8,48,576]{2,1,0:T(8,128)(2,1)S(1)}, bf16[8,128,384]{2,1,0:T(8,128)(2,1)S(1)}) custom-call(f32[4,8,16,128]{3,2,1,0:T(8,128)S(1)} %pad_maximum_fusion.refs_0_, bf16[8,2,48,512]{3,2,1,0:T(8,128)(2,1)S(1)} %copy-done.13, bf16[8,48,576]{2,1,0:T(8,128)(2,1)S(1)} %bitcast.125, ...), custom_call_target="tpu_custom_call" | custom-call | tf_op jit(solution)/shard_map/finish/pallas_call | solution.py:1452
  552.0 3.7 collective-permute-start.1
  557.4 1.1 copy-done.9
  558.5 1.1 copy-done.11
  559.6 1.0 copy-done.16
  560.6 3.0 deliver.1
  563.7 1.7 fusion.19
  565.4 1.7 copy.105
  (166 shorter events, 24.6 us)
Async XLA Ops:
  0.6 62.4 %copy-start = (s32[1,2]{1,0:T(1,128)S(1)}, s32[1,2]{1,0:T(1,128)}, u32[]{:S(2)}) copy-start(s32[1,2]{1,0:T(1,128)} %param.25) | copy-start | bytes 28
  0.7 78.0 %collective-permute-start = (bf16[48,1536]{1,0:T(8,128)(2,1)}, bf16[48,1536]{1,0:T(8,128)(2,1)S(1)}, u32[]{:S(2)}, u32[]{:S(2)}) collective-permute-start(bf16[48,1536]{1,0:T(8,128)(2,1)} %param.28), channel_id=1, source_target_pairs={{0,0},{1,8},{2,16},{3,24},{4,1},{5,9},{6,17},{7,25},{8,2},{9,10},{... | collective-permute-start | bytes 442376 | tf_op jit(solution)/shard_map/ppermute | solution.py:1830
  4.5 1.0 copy-start.20
  5.9 1.0 copy-start.26
  6.0 1.0 copy-start.27
  6.0 1.2 copy-start.17
  7.2 55.9 %copy-start.28 = (bf16[24]{0:T(256)(128)(2,1)S(1)}, bf16[24]{0:T(256)(128)(2,1)}, u32[]{:S(2)}) copy-start(bf16[24]{0:T(256)(128)(2,1)} %param.34) | copy-start | bytes 148
  7.2 56.0 %copy-start.18 = (bf16[48,8192]{1,0:T(8,128)(2,1)S(1)}, bf16[48,8192]{1,0:T(8,128)(2,1)}, u32[]{:S(2)}) copy-start(bf16[48,8192]{1,0:T(8,128)(2,1)} %param.29) | copy-start | bytes 2359300
  57.2 1.1 copy-start.2
  63.8 1.5 copy-start.24
  359.0 141.4 %copy-start.22 = (f32[16,1536]{1,0:T(8,128)S(1)}, f32[16,1536]{1,0:T(8,128)}, u32[]{:S(2)}) copy-start(f32[16,1536]{1,0:T(8,128)} %get-tuple-element.87) | copy-start | bytes 294916
  497.1 4.7 copy-start.12
  497.1 4.7 copy-start.13
  501.7 49.6 %copy-start.19 = (bf16[4,48,1536]{2,1,0:T(8,128)(2,1)S(1)}, bf16[4,48,1536]{2,1,0:T(8,128)(2,1)}, u32[]{:S(2)}) copy-start(bf16[4,48,1536]{2,1,0:T(8,128)(2,1)} %get-tuple-element.102) | copy-start | bytes 1769476
  501.8 1.1 copy-start.14
  502.8 54.5 %copy-start.6 = (f32[128,1536]{1,0:T(8,128)S(1)}, f32[128,1536]{1,0:T(8,128)}, u32[]{:S(2)}) copy-start(f32[128,1536]{1,0:T(8,128)} %get-tuple-element.96.refs_1_) | copy-start | bytes 2359300
  502.8 54.5 %copy-start.7 = (bf16[8,2,48,512]{3,2,1,0:T(8,128)(2,1)S(1)}, bf16[8,2,48,512]{3,2,1,0:T(8,128)(2,1)}, u32[]{:S(2)}) copy-start(bf16[8,2,48,512]{3,2,1,0:T(8,128)(2,1)} %get-tuple-element.85.gate_ref) | copy-start | bytes 2359300
  550.7 6.6 %copy-start.4 = (f32[128,1536]{1,0:T(8,128)S(1)}, f32[128,1536]{1,0:T(8,128)}, u32[]{:S(2)}) copy-start(f32[128,1536]{1,0:T(8,128)} %get-tuple-element.95.refs_0_) | copy-start | bytes 2359300
  550.7 6.6 %copy-start.5 = (f32[128,1536]{1,0:T(8,128)S(1)}, f32[128,1536]{1,0:T(8,128)}, u32[]{:S(2)}) copy-start(f32[128,1536]{1,0:T(8,128)} %get-tuple-element.97.refs_2_) | copy-start | bytes 2359300
  552.0 13.4 %collective-permute-start.1 = (f32[48,1536]{1,0:T(8,128)}, f32[48,1536]{1,0:T(8,128)}, u32[]{:S(2)}, u32[]{:S(2)}) collective-permute-start(f32[48,1536]{1,0:T(8,128)} %convert_reduce_fusion), channel_id=1, source_target_pairs={{0,0},{8,1},{16,2},{24,3},{1,4},{9,5},{17,6},{25,7},{2,8},{10,9},{... | collective-permute-start | bytes 884744 | tf_op jit(solution)/shard_map/ppermute | solution.py:2006
  557.3 1.1 copy-start.9
  558.5 1.1 copy-start.11
  559.6 1.0 copy-start.16
  560.6 6.5 %copy-start.1 = (s32[1,2]{1,0:T(1,128)S(1)}, s32[1,2]{1,0:T(1,128)}, u32[]{:S(2)}) copy-start(s32[1,2]{1,0:T(1,128)} %param.25) | copy-start | bytes 28
  (7 other events, 5.8 us)

commit v6 on v5

--- a/solution.py
+++ b/solution.py
@@ -493,6 +493,36 @@
             device_id=flip(self.me, mask),
             device_id_type=MESH,
         )
+
+
+class HandOn:
+    def __init__(self, plan, me, src, dst, to_index, send_sem, recv_sem):
+        place = plan.set_of(me) * M + me[2]
+        there = to_index(place)
+        self.src, self.dst, self.away = src, dst, there != place
+        self.copy = pltpu.make_async_remote_copy(
+            src_ref=src,
+            dst_ref=dst,
+            send_sem=send_sem,
+            recv_sem=recv_sem,
+            device_id=(there // (plan.times * M), there // M % plan.times, there % M),
+            device_id_type=MESH,
+        )
+
+    def start(self):
+        @pl.when(self.away)
+        def _():
+            self.copy.start()
+
+    def wait(self):
+        @pl.when(self.away)
+        def _():
+            self.copy.wait_recv()
+            self.copy.wait_send()
+
+        @pl.when(jnp.logical_not(self.away))
+        def _():
+            self.dst[...] = self.src[...]
 
 
 def rows_at(index, count):
@@ -1406,26 +1436,31 @@
     return result[:5], result[5:]
 
 
-def finish(plan, small, jobs):
+def finish(plan, small, out_sum, jobs):
     moves = Transfers(list(jobs))
     n_in, n_out = len(moves.sent), len(moves.jobs)
     peers = plan.all
 
     def kernel(*refs):
-        small_ref = refs[0]
-        ins = refs[1 : 1 + n_in]
-        all_ref = refs[1 + n_in]
-        outs = refs[2 + n_in : 2 + n_in + n_out]
-        recv_ref, sum_ref, all_in, send_sem, recv_sem = refs[2 + n_in + n_out : 7 + n_in + n_out]
+        small_ref, out_ref = refs[:2]
+        ins = refs[2 : 2 + n_in]
+        all_ref, out_grad = refs[2 + n_in : 4 + n_in]
+        outs = refs[4 + n_in : 4 + n_in + n_out]
+        refs = refs[4 + n_in + n_out :]
+        recv_ref, sum_ref, all_in, send_sem, recv_sem, out_in = refs[:6]
         me = here()
         greet(me, moves.peers() | set(peers))
         link = Links(me, send_sem, recv_sem)
-        moves.bind(me, ins, outs, refs[7 + n_in + n_out :])
+        moves.bind(me, ins, outs, refs[6:])
         copies = []
         for i, mask in enumerate(peers):
             dest = flip(me, mask)
             copies.append(link(small_ref.at[plan.set_of(dest), dest[2]], recv_ref.at[i], mask))
             copies[-1].start()
+        hand_on = HandOn(
+            plan, me, out_ref, out_in, lambda p: p % M * plan.sets + p // M, send_sem.at[links], recv_sem.at[links]
+        )
+        hand_on.start()
         moves.start()
         own = small_ref[plan.set_of(me), me[2]]
         group, everyone = own[:8], own[8:]
@@ -1444,28 +1479,33 @@
         for copy in shares:
             copy.wait_recv()
         all_ref[...] = all_in[...]
+        hand_on.wait()
+        out_grad[...] = out_in[...].astype(f32)
         for copy in copies + shares:
             copy.wait_send()
         moves.finish()
 
     devices = plan.sets * M
+    links = 2 * len(peers)
     result = pl.pallas_call(
         kernel,
-        out_shape=[jax.ShapeDtypeStruct((devices, 16, 128), f32)] + moves.out_shapes(),
-        in_specs=[VMEM] + [ANY] * n_in,
-        out_specs=[VMEM] + [ANY] * n_out,
+        out_shape=[jax.ShapeDtypeStruct((devices, 16, 128), f32), jax.ShapeDtypeStruct(out_sum.shape, f32)]
+        + moves.out_shapes(),
+        in_specs=[VMEM] * 2 + [ANY] * n_in,
+        out_specs=[VMEM] * 2 + [ANY] * n_out,
         scratch_shapes=[
             pltpu.VMEM((len(peers), 16, 128), f32),
             pltpu.VMEM((16, 128), f32),
             pltpu.VMEM((devices, 16, 128), f32),
-            pltpu.SemaphoreType.DMA((2 * len(peers),)),
-            pltpu.SemaphoreType.DMA((2 * len(peers),)),
+            pltpu.SemaphoreType.DMA((links + 1,)),
+            pltpu.SemaphoreType.DMA((links + 1,)),
+            pltpu.VMEM(out_sum.shape, out_sum.dtype),
         ]
         + moves.scratch(),
         name="finish",
         compiler_params=params(plan, 40),
-    )(small, *moves.operands())
-    return result[0], result[1:]
+    )(small, out_sum, *moves.operands())
+    return result[0], result[1], result[2:]
 
 
 def deliver(gate_parts, up_parts, qkv_pieces, text_pieces, whole, sets):
@@ -1475,11 +1515,12 @@
     t_rows = text_pieces.shape[1]
     n = len(whole)
 
-    def kernel(gate_ref, up_ref, qkv_ref, text_ref, *refs):
+    def kernel(gate_ref, qkv_ref, text_ref, *refs):
+        up_refs, refs = refs[:times], refs[times:]
         ins, (gate_up_out, qkv_out, text_out), outs = refs[:n], refs[n : n + 3], refs[n + 3 :]
         for m in range(M):
             gate = sum(gate_ref[m, t].astype(f32) for t in range(times))
-            up = sum(up_ref[t, m].astype(f32) for t in range(times))
+            up = sum(up_ref[m].astype(f32) for up_ref in up_refs)
             for j in range(sets):
                 at = (j * M + m) * unit
                 gate_up_out[:, at : at + unit] = gate[:, j * unit : (j + 1) * unit]
@@ -1501,11 +1542,11 @@
             jax.ShapeDtypeStruct((t_rows, 2 * D), f32),
         ]
         + [jax.ShapeDtypeStruct(x.shape, x.dtype) for x in whole],
-        in_specs=[VMEM] * (4 + n),
+        in_specs=[VMEM] * (3 + times + n),
         out_specs=[VMEM] * (3 + n),
         name="deliver",
         compiler_params=pltpu.CompilerParams(vmem_limit_bytes=48 * 2**20),
-    )(gate_parts, up_parts, qkv_pieces, text_pieces, *whole)
+    )(gate_parts, qkv_pieces, text_pieces, *up_parts, *whole)
 
 
 def feed_forward(
@@ -1984,11 +2025,18 @@
     d_gains = d_gains.reshape(8, gain_tiles, 128).transpose(1, 0, 2)
     d_gains = jnp.pad(d_gains, ((0, devices - gain_tiles), (0, 0), (0, 0)))
     small = jnp.concatenate([d_mod, d_gains], axis=1).reshape(sets, M, 16, 128)
-    small_all, (up_parts, qkv_pieces, text_pieces) = finish(
+    out_sum = add(out_parts).astype(bf16)
+    up_own = lax.dynamic_index_in_dim(up_pieces, time, 1, keepdims=False)
+    up_sends = [lax.dynamic_index_in_dim(up_pieces, time ^ t, 1, keepdims=False) for t in range(1, times)]
+    small, out_sum, up_sends = lax.optimization_barrier((small, out_sum, up_sends))
+    up_parts = [up_own] + [
+        lax.ppermute(x, "times", [(a, a ^ (t + 1)) for a in range(times)]) for t, x in enumerate(up_sends)
+    ]
+    small_all, out_grad, (qkv_pieces, text_pieces) = finish(
         plan,
         small,
+        out_sum,
         [
-            plan.times_of_ring(up_pieces),
             plan.scatter_ring(qkv_sum.reshape(M, k_rows, 3 * LOCAL)),
             plan.scatter_ring(text_sum.reshape(M, t_rows, 2 * LOCAL)),
         ],
@@ -2003,9 +2051,8 @@
     )
     ada_grad = jnp.einsum("fc,fd->cd", silu_both[:, :a_rows], d_mod_all, precision=highest)
     bias_grad = lax.dynamic_slice_in_dim(jnp.sum(d_mod_all, axis=0), place * bias_n, bias_n)
-    out_grad = lax.ppermute(add(out_parts), axes, out_back)
-    gate_up_grad, qkv_grad, text_grad, result_rows, grad_latent, down_grad = deliver(
-        gate_parts, up_parts, qkv_pieces, text_pieces, [result_rows, grad_latent, down_grad], sets
+    gate_up_grad, qkv_grad, text_grad, result_rows, grad_latent, down_grad, out_grad = deliver(
+        gate_parts, up_parts, qkv_pieces, text_pieces, [result_rows, grad_latent, down_grad, out_grad], sets
     )
     return (
         result_rows[None],

time: 578 us -> 572 us (0.990)
    unnamed x68 -> x63, local copies, waits for them, and re-layouts: 14.4 us -> 10.6 us
  transfers between devices with their start and end apart: 2 -> 2, of which waited for: 0 -> 0; matrix products, arithmetic and copies ran while one was open for 5% -> 5% of each run, Pallas kernels for 9% -> 16%
where the time goes in v6:
time: 572 us; the launch traced here: 565 us
  Pallas kernels  508 us (89%)
  local copies, waits for them, and re-layouts  31.5 us (6%)
  other arithmetic  12.8 us (2%)
  starting transfers between devices  9.59 us (2%)
    pallas_call x1, Pallas kernels, feed_forward(): pl.pallas_call(kernel, out_shape=[jax.ShapeDtypeStruct((TOK, D), f32), ja...  171 us
    pallas_call x1, Pallas kernels, attention_backward(): pl.pallas_call(kernel, out_shape=[jax.ShapeDtypeStruct((TOK, D), f32), ja...  138 us
    pallas_call x1, Pallas kernels, attention_forward(): pl.pallas_call(kernel, out_shape=[jax.ShapeDtypeStruct((ROWS, WIDE), bf16...  106 us
    pallas_call x1, Pallas kernels, prologue(): pl.pallas_call(kernel, out_shape=[jax.ShapeDtypeStruct((plan.rows, 8, 128...  50 us
    pallas_call x1, Pallas kernels, finish(): pl.pallas_call(kernel, out_shape=[jax.ShapeDtypeStruct((devices, 16, 128)...  39.6 us
  transfers between devices with their start and end apart: 2, of which 0 were waited for; matrix products, arithmetic and copies ran while one was open for 5% of the time, Pallas kernels for 16%

profile of v6, /device:TPU:0, one launch (start us, length us, event | category | flops | bytes accessed | tf_op | source)
XLA Modules:
  0.0 565.1 jit_solution(8479592470523554270)
XLA Ops:
  0.7 1.6 collective-permute-start
  3.0 1.5 copy.63
  7.2 50.0 %prologue.1 = (f32[16,8,128]{2,1,0:T(8,128)S(1)}, f32[8,128]{1,0:T(8,128)S(1)}, f32[4,8,8,128]{3,2,1,0:T(8,128)S(1)}, bf16[8,128,384]{2,1,0:T(8,128)(2,1)}, bf16...) custom-call(f32[2,8,128]{2,1,0:T(8,128)S(1)} %select_maximum_fusion.refs_0_, ...), custom_call_target="tpu_custom_call" | custom-call | tf_op jit(solution)/shard_map/prologue/pallas_call | solution.py:698
  57.3 1.1 copy-done.2
  58.4 0.9 copy-done.3
  60.1 0.9 select_convert_fusion.1.refs_11_
  64.1 1.1 fusion.refs_6_.refs_24_
  65.2 0.9 fusion.1.refs_7_.refs_25_
  67.7 2.3 select_convert_fusion.refs_12_.refs_2_
  70.8 3.2 fusion.3
  77.8 0.9 squeeze.40.refs_20_
  79.3 105.6 %attention_forward.1 = (bf16[1024,256]{1,0:T(8,128)(2,1)}, f32[1024,256]{1,0:T(8,128)}, f32[1024,256]{1,0:T(8,128)}, bf16[1024,1536]{1,0:T(8,128)(2,1)}, bf16[10...) custom-call(f32[128,1536]{1,0:T(8,128)} %bitcast.133, ...), custom_call_target="tpu_custom_call" | custom-call | tf_op jit(solution)/shard_map/attention_forward/pallas_call | solution.py:960
  184.9 2.0 pad.39.refs_1_
  186.9 170.6 %feed_forward.1 = (f32[128,1536]{1,0:T(8,128)}, f32[128,1536]{1,0:T(8,128)}, bf16[1024,256]{1,0:T(8,128)(2,1)}, bf16[256,1536]{1,0:T(8,128)(2,1)}, bf16[768,512]...) custom-call(bf16[1024,256]{1,0:T(8,128)(2,1)} %get-tuple-element.72., ...), custom_call_target="tpu_custom_call" | custom-call | tf_op jit(solution)/shard_map/feed_forward/pallas_call | solution.py:1759
  357.6 1.9 slice.95
  359.5 138.1 %attention_backward.1 = (f32[128,1536]{1,0:T(8,128)}, f32[8,1536]{1,0:T(8,128)}, f32[8,256]{1,0:T(8,128)}, bf16[384,576]{1,0:T(8,128)(2,1)}, bf16[1024,384]{1,0:...) custom-call(bf16[1024,256]{1,0:T(8,128)(2,1)} %get-tuple-element.67., ...), custom_call_target="tpu_custom_call" | custom-call | tf_op jit(solution)/shard_map/attention_backward/pallas_call | solution.py:1352
  503.2 8.0 %collective-permute-start.1 = (bf16[8,48,512]{2,1,0:T(8,128)(2,1)}, bf16[8,48,512]{2,1,0:T(8,128)(2,1)}, u32[]{:S(2)}, u32[]{:S(2)}) collective-permute-start(bf16[8,48,512]{2,1,0:T(8,128)(2,1)} %get-tuple-element.101), channel_id=1, source_target_pairs={{0,8},{8,0},{1,9},{9,1},{2,10},{10,2},{3,11},{11,3},{4,12},{12,4},... | collective-permute-start | bytes 1179656 | tf_op jit(solution)/shard_map/ppermute | solution.py:2033
  511.2 39.6 %finish.1 = (f32[32,16,128]{2,1,0:T(8,128)S(1)}, f32[48,1536]{1,0:T(8,128)S(1)}, bf16[8,48,576]{2,1,0:T(8,128)(2,1)S(1)}, bf16[8,128,384]{2,1,0:T(8,128)(2,1)S(1)}) custom-call(f32[4,8,16,128]{3,2,1,0:T(8,128)S(1)} %pad_maximum_fusion.refs_0_, bf16[48,1536]{1,0:T(8,128)(2,1)S(1)} %reduce_sum.33.refs_1_, bf16[8,48,576]{2,1,0:T(8,128)(2,1)S(1)} %bitcast.129, ...), custom_call_target="tpu_custom_call" | custom-call | tf_op jit(solution)/shard_map/finish/pallas_call | solution.py:1490
  554.4 1.4 constant_dynamic-slice_fusion
  555.8 1.7 fusion.19
  557.5 1.1 copy-done.8
  558.6 1.1 copy-done.10
  559.8 1.0 copy-done.14
  560.7 4.1 deliver.1
  (162 shorter events, 22.8 us)
Async XLA Ops:
  0.6 62.4 %copy-start = (s32[1,2]{1,0:T(1,128)S(1)}, s32[1,2]{1,0:T(1,128)}, u32[]{:S(2)}) copy-start(s32[1,2]{1,0:T(1,128)} %param.25) | copy-start | bytes 28
  0.7 78.0 %collective-permute-start = (bf16[48,1536]{1,0:T(8,128)(2,1)}, bf16[48,1536]{1,0:T(8,128)(2,1)S(1)}, u32[]{:S(2)}, u32[]{:S(2)}) collective-permute-start(bf16[48,1536]{1,0:T(8,128)(2,1)} %param.28), channel_id=1, source_target_pairs={{0,0},{1,8},{2,16},{3,24},{4,1},{5,9},{6,17},{7,25},{8,2},{9,10},{... | collective-permute-start | bytes 442376 | tf_op jit(solution)/shard_map/ppermute | solution.py:1871
  4.5 1.0 copy-start.18
  5.9 1.0 copy-start.23
  5.9 1.0 copy-start.24
  6.0 1.0 copy-start.25
  6.0 1.2 copy-start.12
  7.2 55.9 %copy-start.26 = (bf16[24]{0:T(256)(128)(2,1)S(1)}, bf16[24]{0:T(256)(128)(2,1)}, u32[]{:S(2)}) copy-start(bf16[24]{0:T(256)(128)(2,1)} %param.34) | copy-start | bytes 148
  7.2 56.0 %copy-start.15 = (bf16[48,8192]{1,0:T(8,128)(2,1)S(1)}, bf16[48,8192]{1,0:T(8,128)(2,1)}, u32[]{:S(2)}) copy-start(bf16[48,8192]{1,0:T(8,128)(2,1)} %param.29) | copy-start | bytes 2359300
  57.2 1.1 copy-start.2
  63.8 1.5 copy-start.22
  359.5 141.3 %copy-start.20 = (f32[16,1536]{1,0:T(8,128)S(1)}, f32[16,1536]{1,0:T(8,128)}, u32[]{:S(2)}) copy-start(f32[16,1536]{1,0:T(8,128)} %get-tuple-element.91) | copy-start | bytes 294916
  497.6 4.6 copy-start.17
  497.6 4.8 copy-start.16
  502.1 9.0 %copy-start.4 = (bf16[1024,384]{1,0:T(8,128)(2,1)S(1)}, bf16[1024,384]{1,0:T(8,128)(2,1)}, u32[]{:S(2)}) copy-start(bf16[1024,384]{1,0:T(8,128)(2,1)} %get-tuple-element.98) | copy-start | bytes 2359300
  502.2 9.0 %copy-start.11 = (bf16[384,576]{1,0:T(8,128)(2,1)S(1)}, bf16[384,576]{1,0:T(8,128)(2,1)}, u32[]{:S(2)}) copy-start(bf16[384,576]{1,0:T(8,128)(2,1)} %get-tuple-element.97) | copy-start | bytes 1327108
  503.2 54.3 %collective-permute-start.1 = (bf16[8,48,512]{2,1,0:T(8,128)(2,1)}, bf16[8,48,512]{2,1,0:T(8,128)(2,1)}, u32[]{:S(2)}, u32[]{:S(2)}) collective-permute-start(bf16[8,48,512]{2,1,0:T(8,128)(2,1)} %get-tuple-element.101), channel_id=1, source_target_pairs={{0,8},{8,0},{1,9},{9,1},{2,10},{10,2},{3,11},{11,3},{4,12},{12,4},... | collective-permute-start | bytes 1179656 | tf_op jit(solution)/shard_map/ppermute | solution.py:2033
  552.4 5.1 copy-start.5
  552.4 5.1 copy-start.6
  552.4 5.1 copy-start.7
  557.5 7.4 %copy-start.1 = (s32[1,2]{1,0:T(1,128)S(1)}, s32[1,2]{1,0:T(1,128)}, u32[]{:S(2)}) copy-start(s32[1,2]{1,0:T(1,128)} %param.25) | copy-start | bytes 28
  557.5 1.1 copy-start.8
  558.6 1.1 copy-start.10
  559.8 1.0 copy-start.14
  (5 other events, 3.9 us)
